TPU v7x, 128 devices: a whole 4x4x4 slice. The times are simulated.
128 devices in a mesh: section: 4 (over y_lo, core), tensor: 8 (over y_hi, z), dp: 4 (over x).
Axes of the slice: x: 4, y: 4 (y_hi: 2, y_lo: 2; y = y_hi * 2 + y_lo), z: 4, core: 2. Of those that a mesh axis runs over, the one named last changes fastest.
Arguments:
- tokens: int32 [16, 1025], P('dp'), may hold values from 0 to 50303
- groups: int32 [16], replicated, may hold values from 0 to 7
- counts: int32 [4], replicated, may hold values from 1 to 4, as said below
- domain: float32 [8], replicated, may hold values from 0.25 to 4
- w_in: float32 [4, 512, 3584], P('section', None, 'tensor'), may hold values from -0.25 to 0.25
- w_back: float32 [4, 2560, 512], P('section', 'tensor'), may hold values from -0.375 to 0.375
- tables: float32 [2, 50304, 512], P(None, ('section', 'tensor'), 'dp')
- b_in: float32 [4, 3584], P('section', 'tensor'), may hold values from -1.5 to 1.5
- vecs: float32 [4, 6, 512], P('section')
- final_norm: float32 [2, 512], replicated
- w_in_mom: float32 [4, 512, 3584], P('section', None, 'tensor'), may hold values from -0.0012207031 to 0.0012207031
- w_back_mom: float32 [4, 2560, 512], P('section', 'tensor'), may hold values from -0.0012207031 to 0.0012207031
- tables_mom: float32 [2, 50304, 512], P(None, ('section', 'tensor'), 'dp'), may hold values from -1.5258789e-05 to 1.5258789e-05
- b_in_mom: float32 [4, 3584], P('section', 'tensor'), may hold values from -0.0012207031 to 0.0012207031
- vecs_mom: float32 [4, 6, 512], P('section'), may hold values from -0.0012207031 to 0.0012207031
- final_mom: float32 [2, 512], replicated, may hold values from -0.0012207031 to 0.0012207031
- w_in_ema: float32 [4, 512, 3584], P('section', None, 'tensor'), may hold values from -0.25 to 0.25
- w_back_ema: float32 [4, 2560, 512], P('section', 'tensor'), may hold values from -0.375 to 0.375
- tables_ema: float32 [2, 50304, 512], P(None, ('section', 'tensor'), 'dp'), may hold values from -4 to 4
- b_in_ema: float32 [4, 3584], P('section', 'tensor'), may hold values from -1.5 to 1.5
- vecs_ema: float32 [4, 6, 512], P('section')
- final_ema: float32 [2, 512], replicated
- w_in_err: float32 [4, 4, 512, 3584], P('dp', 'section', None, 'tensor'), may hold values from -0.01171875 to 0.01171875
- w_back_err: float32 [4, 4, 2560, 512], P('dp', 'section', 'tensor'), may hold values from -0.01171875 to 0.01171875
- tables_err: float32 [4, 2, 50304, 512], P('dp', None, ('section', 'tensor')), may hold values from -0.00010681152 to 0.00010681152
- w_in_fac: float32 [4, 3584, 8], P('section', 'tensor'), may hold values from -6 to 6
- w_back_fac: float32 [4, 2560, 8], P('section', 'tensor'), may hold values from -6 to 6
- tables_fac: float32 [2, 50304, 8], P(None, ('section', 'tensor')), may hold values from -6 to 6
Outputs:
- loss_sum: float32 [], replicated
- weight_total: float32 [], replicated
- w_in_new: float32 [4, 512, 3584], P('section', None, 'tensor')
- w_back_new: float32 [4, 2560, 512], P('section', 'tensor')
- tables_new: float32 [2, 50304, 512], P(None, ('section', 'tensor'), 'dp')
- b_in_new: float32 [4, 3584], P('section', 'tensor')
- vecs_new: float32 [4, 6, 512], P('section')
- final_new: float32 [2, 512], replicated
- w_in_mom_new: float32 [4, 512, 3584], P('section', None, 'tensor')
- w_back_mom_new: float32 [4, 2560, 512], P('section', 'tensor')
- tables_mom_new: float32 [2, 50304, 512], P(None, ('section', 'tensor'), 'dp')
- b_in_mom_new: float32 [4, 3584], P('section', 'tensor')
- vecs_mom_new: float32 [4, 6, 512], P('section')
- final_mom_new: float32 [2, 512], replicated
- w_in_ema_new: float32 [4, 512, 3584], P('section', None, 'tensor')
- w_back_ema_new: float32 [4, 2560, 512], P('section', 'tensor')
- tables_ema_new: float32 [2, 50304, 512], P(None, ('section', 'tensor'), 'dp')
- b_in_ema_new: float32 [4, 3584], P('section', 'tensor')
- vecs_ema_new: float32 [4, 6, 512], P('section')
- final_ema_new: float32 [2, 512], replicated
- w_in_err_new: float32 [4, 4, 512, 3584], P('dp', 'section', None, 'tensor')
- w_back_err_new: float32 [4, 4, 2560, 512], P('dp', 'section', 'tensor')
- tables_err_new: float32 [4, 2, 50304, 512], P('dp', None, ('section', 'tensor'))
- w_in_fac_new: float32 [4, 3584, 8], P('section', 'tensor')
- w_back_fac_new: float32 [4, 2560, 8], P('section', 'tensor')
- embed_fac_new: float32 [50304, 8], P(('section', 'tensor'))
- head_fac_new: float32 [50304, 8], P(('section', 'tensor'))
Inputs may be any that keep to these rules, and one draw needn't show every extreme that they name: Replica r trains on its first counts[r] sequences; the last replica trains on all 4, the first on at most 2.
All inputs are finite; a program needn't handle non-finite values.
Results may differ from a plain program's by a relative error of at most 0.035.
Values may be sent and summed in bfloat16 or wider, within the bound.
A program may use at most 384 MiB of HBM per device.

v0:
```python
import math

import jax
import jax.numpy as jnp
from jax import lax
from jax.sharding import PartitionSpec as P

D = 512
HEAD = 64
ROT = 16
VOCAB = 50304
LENGTH = 1024
MB = 4
RANK = 8
STEP = 5


EPS_NORM = 1e-05
MOMENTUM = 0.9
NEG_BIG = -1e30
HIGH = lax.Precision.HIGHEST


def passed_along(block, axis, distance):
    devices = range(lax.axis_size(axis))
    route = [(i - distance, i) for i in devices if i - distance in devices]
    return lax.ppermute(block, axis, route)


def rows_for(lines, peers):
    spare = -len(lines) % peers
    return jnp.pad(lines, [(0, spare)] + [(0, 0)] * (lines.ndim - 1))


def spread_2(value, axis, root):
    lines = jnp.where(lax.axis_index(axis) == root, value, jnp.zeros_like(value)).reshape(
        -1, *value.shape[1:][-1:]
    )
    padded = rows_for(lines, lax.axis_size(axis))
    own = lax.psum_scatter(padded, axis, scatter_dimension=0, tiled=True)
    return lax.all_gather(own, axis, axis=0, tiled=True)[: len(lines)].reshape(value.shape)


def sent_to_all(value, axis):
    copies = jnp.broadcast_to(value, (lax.axis_size(axis), *value.shape))
    return lax.all_to_all(copies, axis, split_axis=0, concat_axis=0, tiled=True)


def collected_together(value, axis):
    leaves = jax.tree.leaves(value)
    sequence = sorted(range(len(leaves)), key=lambda k: -leaves[k].size)
    width = (1, *leaves[sequence[0]].shape)[-1]
    lines = [
        jnp.pad(leaves[k].reshape(-1), (0, -leaves[k].size % width)).reshape(-1, width)
        for k in sequence
    ]
    both, at, found = (sent_to_all(jnp.concatenate(lines), axis), 0, {})
    for k, line in zip(sequence, lines):
        slab = both[:, at : at + len(line)].reshape(len(both), -1)
        found[k] = slab[:, : leaves[k].size].reshape(-1, *leaves[k].shape)
        at += len(line)
    numbers = iter(range(len(leaves)))
    return jax.tree.map(lambda _: found[next(numbers)], value)


def folded_in_pairs(pieces, combine):
    while len(jax.tree.leaves(pieces)[0]) > 1:
        pieces = jax.vmap(combine)(
            *(jax.tree.map(lambda part: part[side::2], pieces) for side in (0, 1))
        )
    return jax.tree.map(lambda part: part[0], pieces)


def merged(value, axis, combine):
    pieces = collected_together(
        jax.tree.map(
            lambda part, kind: part.astype(kind), value, (jnp.bfloat16, jnp.bfloat16, jnp.bfloat16)
        ),
        axis,
    )
    return folded_in_pairs(
        jax.tree.map(lambda part, own: part.astype(own.dtype), pieces, value), combine
    )


def shortened(value):

    def short(part):
        return part.astype(jnp.bfloat16) if part.dtype == jnp.float32 else part

    return jax.tree.map(short, value)


def taken_together(value, axis):
    everything = sent_to_all(value, axis)
    return jnp.sum(everything, axis=0)


def over_copies(value, axis):
    everything = sent_to_all(value, axis)
    return jnp.sum(everything.astype(jnp.float32), axis=0)


def ema_decay():
    return min(0.999, (1.0 + STEP) / (10.0 + STEP))


def layer_norm(values, gain, shift):
    center = values - jnp.mean(values, -1, keepdims=True)
    spread = jnp.mean(center * center, -1, keepdims=True)
    return center * lax.rsqrt(spread + EPS_NORM) * gain + shift


def norm_pair(values, vector):
    return (layer_norm(values, vector[0], vector[1]), layer_norm(values, vector[2], vector[3]))


def final_norm_of(values, gains):
    return layer_norm(values, gains[0], gains[1])


def rotary_tables():
    half_rot = ROT // 2
    inverse = 10000.0 ** (-jnp.arange(half_rot, dtype=jnp.float32) * (2.0 / ROT))
    angles = jnp.arange(LENGTH, dtype=jnp.float32)[:, None] * inverse[None, :]
    return (jnp.cos(angles), jnp.sin(angles))


def rotate(heads, cosine, sine):
    half_rot = ROT // 2
    first = heads[..., :half_rot]
    second = heads[..., half_rot:ROT]
    return jnp.concatenate(
        [first * cosine - second * sine, second * cosine + first * sine, heads[..., ROT:]], -1
    )


def causal(start, block):
    row_ids = start + jnp.arange(block, dtype=jnp.int32)
    return row_ids[:, None] >= jnp.arange(LENGTH, dtype=jnp.int32)[None, :]


def store(buffer, slot, value, valid):
    old_value = lax.dynamic_index_in_dim(buffer, slot, 0, False)
    return lax.dynamic_update_index_in_dim(buffer, jnp.where(valid, value, old_value), slot, 0)


def dot_rows(left, right):
    return lax.dot_general(
        left, right, (((0,), (0,)), ((), ())), preferred_element_type=jnp.float32
    )


def dot_cols(left, right):
    return lax.dot_general(
        left, right, (((1,), (1,)), ((), ())), preferred_element_type=jnp.float32
    )


def to_heads(flat, heads_here):
    row_count = flat.shape[0]
    return jnp.transpose(flat.reshape(row_count // LENGTH, LENGTH, heads_here, HEAD), (0, 2, 1, 3))


def join_heads(heads):
    return jnp.transpose(heads, (0, 2, 1, 3)).reshape(
        heads.shape[0] * LENGTH, heads.shape[1] * HEAD
    )


def attention_forward(q_rot, k_rot, v_val):
    block = min(512, LENGTH)
    scale = HEAD ** (-0.5)

    def one_block(index):
        start = index * block
        query_block = lax.dynamic_slice_in_dim(q_rot, start, block, 2)
        scores = (
            jnp.einsum("shqd,shkd->shqk", query_block, k_rot, preferred_element_type=jnp.float32)
            * scale
        )
        scores = jnp.where(causal(start, block)[None, None], scores, NEG_BIG)
        top = jnp.max(scores, -1, keepdims=True)
        expo = jnp.exp(scores - top)
        total = jnp.sum(expo, -1, keepdims=True)
        probs = (expo / total).astype(jnp.bfloat16)
        out_block = jnp.einsum("shqk,shkd->shqd", probs, v_val, preferred_element_type=jnp.float32)
        return (out_block, (top + jnp.log(total))[..., 0])

    outputs, lse = lax.map(one_block, jnp.arange(LENGTH // block, dtype=jnp.int32))
    outputs = jnp.transpose(outputs, (1, 2, 0, 3, 4)).reshape(q_rot.shape)
    lse = jnp.transpose(lse, (1, 2, 0, 3)).reshape(q_rot.shape[:3])
    return (outputs, lse)


def attention_backward(q_rot, k_rot, v_val, lse, grad_out):
    block = min(512, LENGTH)
    scale = HEAD ** (-0.5)

    def one_block(carry, index):
        grad_key, grad_value = carry
        start = index * block
        query_block = lax.dynamic_slice_in_dim(q_rot, start, block, 2)
        lse_block = lax.dynamic_slice_in_dim(lse, start, block, 2)
        grad_block = lax.dynamic_slice_in_dim(grad_out, start, block, 2)
        scores = (
            jnp.einsum("shqd,shkd->shqk", query_block, k_rot, preferred_element_type=jnp.float32)
            * scale
        )
        probs = jnp.where(
            causal(start, block)[None, None], jnp.exp(scores - lse_block[..., None]), 0.0
        )
        grad_value = grad_value + jnp.einsum(
            "shqk,shqd->shkd",
            probs.astype(jnp.bfloat16),
            grad_block,
            preferred_element_type=jnp.float32,
        )
        grad_probs = jnp.einsum(
            "shqd,shkd->shqk", grad_block, v_val, preferred_element_type=jnp.float32
        )
        grad_scores = (
            probs * (grad_probs - jnp.sum(grad_probs * probs, -1, keepdims=True))
        ).astype(jnp.bfloat16)
        grad_query = (
            jnp.einsum("shqk,shkd->shqd", grad_scores, k_rot, preferred_element_type=jnp.float32)
            * scale
        )
        grad_key = (
            grad_key
            + jnp.einsum(
                "shqk,shqd->shkd", grad_scores, query_block, preferred_element_type=jnp.float32
            )
            * scale
        )
        return ((grad_key, grad_value), grad_query)

    empty = jnp.zeros(k_rot.shape, jnp.float32)
    (grad_key, grad_value), grad_query = lax.scan(
        one_block, (empty, empty), jnp.arange(LENGTH // block, dtype=jnp.int32)
    )
    grad_query = jnp.transpose(grad_query, (1, 2, 0, 3, 4)).reshape(q_rot.shape)
    return (grad_query, grad_key, grad_value)


def block_forward(resid, weights, cosine, sine):
    w_cols, w_rows, bias, vector = weights
    heads_here = (w_cols.shape[1] - w_rows.shape[0]) // (2 * HEAD)
    query_cols = 3 * heads_here * HEAD
    att_rows = heads_here * HEAD
    first_in, second_in = norm_pair(resid, vector)
    first_in = first_in.astype(jnp.bfloat16)
    second_in = second_in.astype(jnp.bfloat16)
    qkv = (
        jnp.dot(first_in, w_cols[:, :query_cols], preferred_element_type=jnp.float32)
        + bias[:query_cols]
    )
    up_val = (
        jnp.dot(second_in, w_cols[:, query_cols:], preferred_element_type=jnp.float32)
        + bias[query_cols:]
    )
    seq_count = resid.shape[0] // LENGTH
    parts = jnp.transpose(qkv.reshape(seq_count, LENGTH, heads_here, 3, HEAD), (3, 0, 2, 1, 4))
    q_rot = rotate(parts[0], cosine, sine).astype(jnp.bfloat16)
    k_rot = rotate(parts[1], cosine, sine).astype(jnp.bfloat16)
    v_val = parts[2].astype(jnp.bfloat16)
    attended, lse = attention_forward(q_rot, k_rot, v_val)
    attended = join_heads(attended).astype(jnp.bfloat16)
    hidden = jax.nn.gelu(up_val, approximate=False).astype(jnp.bfloat16)
    branch = jnp.dot(attended, w_rows[:att_rows], preferred_element_type=jnp.float32)
    branch = branch + jnp.dot(hidden, w_rows[att_rows:], preferred_element_type=jnp.float32)
    return (branch, (first_in, second_in, q_rot, k_rot, v_val, lse, attended, up_val, hidden))


def gelu_exact(values):
    return jax.nn.gelu(values, approximate=False)


def block_backward(grad_out, kept, resid, weights, cosine, sine):
    w_cols, w_rows, bias, vector = weights
    first_in, second_in, q_rot, k_rot, v_val, lse, attended, up_val, hidden = kept
    heads_here = q_rot.shape[1]
    query_cols = 3 * heads_here * HEAD
    att_rows = heads_here * HEAD
    grad_low = grad_out.astype(jnp.bfloat16)
    grad_rows = jnp.concatenate([dot_rows(attended, grad_low), dot_rows(hidden, grad_low)], 0)
    grad_att = dot_cols(grad_low, w_rows[:att_rows])
    grad_hidden = dot_cols(grad_low, w_rows[att_rows:])
    grad_up = jax.vjp(gelu_exact, up_val)[1](grad_hidden)[0].astype(jnp.bfloat16)
    grad_heads = to_heads(grad_att, heads_here).astype(jnp.bfloat16)
    grad_query, grad_key, grad_value = attention_backward(q_rot, k_rot, v_val, lse, grad_heads)
    grad_query = rotate(grad_query, cosine, -sine)
    grad_key = rotate(grad_key, cosine, -sine)
    stacked = jnp.stack([grad_query, grad_key, grad_value], 0)
    grad_qkv = (
        jnp.transpose(stacked, (1, 3, 2, 0, 4))
        .reshape(resid.shape[0], query_cols)
        .astype(jnp.bfloat16)
    )
    grad_cols = jnp.concatenate([dot_rows(first_in, grad_qkv), dot_rows(second_in, grad_up)], 1)
    grad_bias = jnp.concatenate(
        [jnp.sum(grad_qkv.astype(jnp.float32), 0), jnp.sum(grad_up.astype(jnp.float32), 0)]
    )
    grad_first = dot_cols(grad_qkv, w_cols[:, :query_cols])
    grad_second = dot_cols(grad_up, w_cols[:, query_cols:])
    norm_back = jax.vjp(norm_pair, resid, vector[:4])[1]
    grad_resid, grad_norms = norm_back((grad_first, grad_second))
    return (grad_resid, (grad_cols, grad_rows, grad_bias, grad_norms, jnp.sum(grad_out, 0)))


def combine_stats(first, second):
    top = jnp.maximum(first[0], second[0])
    total = first[1] * jnp.exp(first[0] - top) + second[1] * jnp.exp(second[0] - top)
    return (top, total, first[2] + second[2])


def orthonormal(matrix):
    columns = []
    for index in range(RANK):
        column = matrix[..., index]
        for done in columns:
            column = column - jnp.sum(done * column, -1, keepdims=True) * done
        columns.append(column * lax.rsqrt(jnp.sum(column * column, -1, keepdims=True) + 1e-30))
    return jnp.stack(columns, -1)


def momentum_step(weight, moment, average, grad, rate):
    decay = ema_decay()
    new_moment = MOMENTUM * moment + (1.0 - MOMENTUM) * grad
    new_weight = weight - rate * new_moment
    return (new_weight, new_moment, decay * average + (1.0 - decay) * new_weight)


def on_device(
    tokens,
    groups,
    counts,
    domain,
    w_in,
    w_back,
    tables,
    b_in,
    vecs,
    final_norm,
    w_in_mom,
    w_back_mom,
    tables_mom,
    b_in_mom,
    vecs_mom,
    final_mom,
    w_in_ema,
    w_back_ema,
    tables_ema,
    b_in_ema,
    vecs_ema,
    final_ema,
    w_in_err,
    w_back_err,
    tables_err,
    w_in_fac,
    w_back_fac,
    tables_fac,
):
    n_section = lax.axis_size("section")
    n_replica = lax.axis_size("dp")
    section = lax.axis_index("section")
    replica = lax.axis_index("dp")
    vocab_part = lax.axis_index(("section", "tensor"))
    first_tensor = (lax.axis_index("tensor") == 0).astype(jnp.float32)
    table_full = lax.all_gather(tables.astype(jnp.bfloat16), "dp", axis=2, tiled=True)
    own_cols = tables.shape[2]
    seq_rep = tokens.shape[0]
    row_micro = seq_rep // MB * LENGTH
    row_total = seq_rep * LENGTH
    vocab_shard = tables.shape[1]
    cosine, sine = rotary_tables()
    seq_index = jnp.arange(groups.shape[0], dtype=jnp.int32)
    live = seq_index % seq_rep < counts[seq_index // seq_rep]
    domain_hit = groups[:, None] == jnp.arange(domain.shape[0], dtype=jnp.int32)[None, :]
    seq_weight = jnp.where(live, jnp.sum(jnp.where(domain_hit, domain[None, :], 0.0), 1), 0.0)
    weight_total = jnp.sum(seq_weight)
    own_weight = lax.dynamic_slice_in_dim(seq_weight, replica * seq_rep, seq_rep, 0)
    token_ids = tokens[:, :LENGTH].reshape(-1)
    target_ids = tokens[:, 1:].reshape(-1)
    local_ids = token_ids - vocab_part * vocab_shard
    inside = (local_ids >= 0) & (local_ids < vocab_shard)
    safe_ids = jnp.where(inside, local_ids, 0)
    looked = jnp.take(table_full[0], safe_ids, axis=0).astype(jnp.float32)
    embedded = lax.psum(
        jnp.where(inside[:, None], looked, 0.0).astype(jnp.bfloat16), ("section", "tensor")
    ).astype(jnp.float32)
    embedded = embedded.reshape(MB, row_micro, D)
    weights = (w_in[0].astype(jnp.bfloat16), w_back[0].astype(jnp.bfloat16), b_in[0], vecs[0])
    vector = vecs[0]
    ticks = MB + n_section - 1
    received = jnp.zeros((row_micro, D), jnp.float32)
    input_buf = jnp.zeros((MB, row_micro, D), jnp.float32)
    final_buf = jnp.zeros((MB, row_micro, D), jnp.float32)
    kept_buf = None
    for tick in range(ticks):
        micro = tick - section
        valid = (micro >= 0) & (micro < MB)
        slot = jnp.clip(micro, 0, MB - 1)
        resid = jnp.where(section == 0, embedded[min(tick, MB - 1)], received)
        branch, kept = block_forward(resid, weights, cosine, sine)
        layer_out = (
            resid
            + lax.psum(branch.astype(jnp.bfloat16), "tensor").astype(jnp.float32)
            + vector[4]
            + vector[5]
        )
        if kept_buf is None:
            kept_buf = jax.tree.map(lambda item: jnp.zeros((MB,) + item.shape, item.dtype), kept)
        kept_buf = jax.tree.map(
            lambda buffer, item: store(buffer, slot, item, valid), kept_buf, kept
        )
        input_buf = store(input_buf, slot, resid, valid)
        final_buf = store(final_buf, slot, layer_out, valid & (section == n_section - 1))
        if tick + 1 < ticks:
            received = passed_along(layer_out.astype(jnp.bfloat16), "section", 1).astype(
                layer_out.dtype
            )
    final_resid = spread_2(
        final_buf.reshape(row_total, D).astype(jnp.bfloat16), "section", n_section - 1
    ).astype(jnp.float32)
    normed, final_back = jax.vjp(final_norm_of, final_resid, final_norm)
    normed = normed.astype(jnp.bfloat16)
    table_low = table_full[1]
    logits = dot_cols(normed, table_low)
    vocab_ids = vocab_part * vocab_shard + jnp.arange(vocab_shard, dtype=jnp.int32)
    target_hit = target_ids[:, None] == vocab_ids[None, :]
    top_local = jnp.max(logits, 1)
    total_local = jnp.sum(jnp.exp(logits - top_local[:, None]), 1)
    target_local = jnp.sum(jnp.where(target_hit, logits, 0.0), 1)
    top_all, total_all, target_all = merged(
        (top_local, total_local, target_local), ("section", "tensor"), combine_stats
    )
    lse_all = top_all + jnp.log(total_all)
    seq_loss = jnp.mean((lse_all - target_all).reshape(seq_rep, LENGTH), 1)
    loss_part = jnp.sum(own_weight * seq_loss)
    row_coef = jnp.repeat(own_weight / (weight_total * LENGTH), LENGTH)
    grad_logits = (
        (jnp.exp(logits - lse_all[:, None]) - target_hit.astype(jnp.float32)) * row_coef[:, None]
    ).astype(jnp.bfloat16)
    grad_table = dot_rows(grad_logits, normed)
    grad_normed = jnp.dot(grad_logits, table_low, preferred_element_type=jnp.float32)
    grad_normed = lax.psum(grad_normed.astype(jnp.bfloat16), ("section", "tensor")).astype(
        jnp.float32
    )
    grad_final, grad_gains = final_back(grad_normed)
    grad_final = grad_final.reshape(MB, row_micro, D)
    received = jnp.zeros((row_micro, D), jnp.float32)
    grad_input_buf = jnp.zeros((MB, row_micro, D), jnp.float32)
    totals = None
    for tick in range(ticks):
        micro = tick - (n_section - 1 - section)
        valid = (micro >= 0) & (micro < MB)
        slot = jnp.clip(micro, 0, MB - 1)
        grad_out = jnp.where(section == n_section - 1, grad_final[min(tick, MB - 1)], received)
        kept = jax.tree.map(
            lambda buffer: lax.dynamic_index_in_dim(buffer, slot, 0, False), kept_buf
        )
        resid = lax.dynamic_index_in_dim(input_buf, slot, 0, False)
        grad_part, layer_grads = block_backward(grad_out, kept, resid, weights, cosine, sine)
        grad_in = lax.psum(grad_part.astype(jnp.bfloat16), "tensor").astype(jnp.float32) + grad_out
        layer_grads = jax.tree.map(lambda item: jnp.where(valid, item, 0.0), layer_grads)
        totals = (
            layer_grads
            if totals is None
            else jax.tree.map(lambda left, right: left + right, totals, layer_grads)
        )
        grad_input_buf = store(grad_input_buf, slot, grad_in, valid & (section == 0))
        if tick + 1 < ticks:
            received = passed_along(shortened(grad_in), "section", -1).astype(grad_in.dtype)
    grad_embedded = spread_2(
        grad_input_buf.reshape(row_total, D).astype(jnp.bfloat16), "section", 0
    ).astype(jnp.float32)
    grad_embed = jax.ops.segment_sum(
        jnp.where(inside[:, None], grad_embedded, 0.0), safe_ids, vocab_shard
    )
    grad_cols, grad_rows, grad_bias, grad_norms, grad_outbias = totals
    grad_vector = jnp.concatenate(
        [grad_norms, (grad_outbias * first_tensor)[None], (grad_outbias * first_tensor)[None]], 0
    )
    vec_sum, final_sum, loss_sum = (
        taken_together(grad_vector, ("tensor", "dp")),
        taken_together(grad_gains * first_tensor, ("tensor", "dp")),
        taken_together(loss_part * first_tensor, ("tensor", "dp")),
    )
    full_in = grad_cols + w_in_err[0, 0]
    full_back = grad_rows + w_back_err[0, 0]
    full_tab = jnp.stack([grad_embed, grad_table]) + tables_err[0]
    left_in = jnp.einsum("dn,nr->dr", full_in, w_in_fac[0], precision=HIGH)
    left_back = jnp.einsum("nd,nr->dr", full_back, w_back_fac[0], precision=HIGH)
    left_tab = jnp.einsum("bnd,bnr->bdr", full_tab, tables_fac, precision=HIGH)
    left_in, left_back, left_tab, bias_sum = (
        taken_together(left_in, "dp"),
        taken_together(left_back, "dp"),
        taken_together(left_tab, "dp"),
        taken_together(grad_bias, "dp"),
    )
    basis_in = orthonormal(left_in)
    basis_back = orthonormal(left_back)
    basis_tab = orthonormal(left_tab)
    right_in = jnp.einsum("dn,dr->nr", full_in, basis_in, precision=HIGH)
    right_back = jnp.einsum("nd,dr->nr", full_back, basis_back, precision=HIGH)
    right_tab = jnp.einsum("bnd,bdr->bnr", full_tab, basis_tab, precision=HIGH)
    sum_in, sum_back, sum_tab = (
        over_copies(right_in.astype(jnp.bfloat16), "dp").astype(jnp.float32),
        over_copies(right_back.astype(jnp.bfloat16), "dp").astype(jnp.float32),
        over_copies(right_tab.astype(jnp.bfloat16), "dp").astype(jnp.float32),
    )
    red_in = jnp.einsum("dr,nr->dn", basis_in, sum_in, precision=HIGH)
    red_back = jnp.einsum("nr,dr->nd", sum_back, basis_back, precision=HIGH)
    red_tab = jnp.einsum("bnr,bdr->bnd", sum_tab, basis_tab, precision=HIGH)
    red_tab_own = lax.dynamic_slice_in_dim(red_tab, replica * own_cols, own_cols, 2)
    err_in_new = full_in - jnp.einsum("dr,nr->dn", basis_in, right_in, precision=HIGH)
    err_back_new = full_back - jnp.einsum("nr,dr->nd", right_back, basis_back, precision=HIGH)
    err_tab_new = full_tab - jnp.einsum("bnr,bdr->bnd", right_tab, basis_tab, precision=HIGH)
    token_count = n_replica * seq_rep * LENGTH
    rate_layer = 2.0 * math.sqrt(token_count)
    rate_vector = 6.0 * math.sqrt(token_count)
    rate_table = jnp.array([50.0, 0.5], jnp.float32).reshape(2, 1, 1) * math.sqrt(
        token_count * VOCAB
    )
    in_w, in_m, in_e = momentum_step(w_in, w_in_mom, w_in_ema, red_in[None], rate_layer)
    back_w, back_m, back_e = momentum_step(
        w_back, w_back_mom, w_back_ema, red_back[None], rate_layer
    )
    tab_w, tab_m, tab_e = momentum_step(tables, tables_mom, tables_ema, red_tab_own, rate_table)
    bias_w, bias_m, bias_e = momentum_step(b_in, b_in_mom, b_in_ema, bias_sum[None], rate_layer)
    vec_w, vec_m, vec_e = momentum_step(vecs, vecs_mom, vecs_ema, vec_sum[None], rate_vector)
    fin_w, fin_m, fin_e = momentum_step(final_norm, final_mom, final_ema, final_sum, rate_layer)
    return (
        loss_sum,
        weight_total,
        in_w,
        back_w,
        tab_w,
        bias_w,
        vec_w,
        fin_w,
        in_m,
        back_m,
        tab_m,
        bias_m,
        vec_m,
        fin_m,
        in_e,
        back_e,
        tab_e,
        bias_e,
        vec_e,
        fin_e,
        err_in_new[None, None],
        err_back_new[None, None],
        err_tab_new[None],
        sum_in[None],
        sum_back[None],
        sum_tab[0],
        sum_tab[1],
    )


def solution(mesh):
    in_specs = (
        P("dp", None),
        P(),
        P(),
        P(),
        P("section", None, "tensor"),
        P("section", "tensor", None),
        P(None, ("section", "tensor"), "dp"),
        P("section", "tensor"),
        P("section", None, None),
        P(),
        P("section", None, "tensor"),
        P("section", "tensor", None),
        P(None, ("section", "tensor"), "dp"),
        P("section", "tensor"),
        P("section", None, None),
        P(),
        P("section", None, "tensor"),
        P("section", "tensor", None),
        P(None, ("section", "tensor"), "dp"),
        P("section", "tensor"),
        P("section", None, None),
        P(),
        P("dp", "section", None, "tensor"),
        P("dp", "section", "tensor", None),
        P("dp", None, ("section", "tensor"), None),
        P("section", "tensor", None),
        P("section", "tensor", None),
        P(None, ("section", "tensor"), None),
    )
    out_specs = (
        P(),
        P(),
        P("section", None, "tensor"),
        P("section", "tensor", None),
        P(None, ("section", "tensor"), "dp"),
        P("section", "tensor"),
        P("section", None, None),
        P(),
        P("section", None, "tensor"),
        P("section", "tensor", None),
        P(None, ("section", "tensor"), "dp"),
        P("section", "tensor"),
        P("section", None, None),
        P(),
        P("section", None, "tensor"),
        P("section", "tensor", None),
        P(None, ("section", "tensor"), "dp"),
        P("section", "tensor"),
        P("section", None, None),
        P(),
        P("dp", "section", None, "tensor"),
        P("dp", "section", "tensor", None),
        P("dp", None, ("section", "tensor"), None),
        P("section", "tensor", None),
        P("section", "tensor", None),
        P(("section", "tensor"), None),
        P(("section", "tensor"), None),
    )
    return jax.shard_map(
        on_device, mesh=mesh, in_specs=in_specs, out_specs=out_specs, check_vma=False
    )
```

profile of v0, /device:TPU:0, one launch (start us, length us, event | category | flops | bytes accessed | tf_op | source)
XLA Modules:
  0.0 2937.9 jit_solution(3119650309963240854)
XLA Ops:
  11.2 71.5 %all-gather.4.cloned.1.call-done = bf16[2,1572,512]{2,0,1:T(2,128)(2,1)} async-done(((bf16[2,1572,128]{2,0,1:T(2,128)(2,1)}), bf16[2,1572,512]{2,0,1:T(2,128)(2,1)}) %all-gather.4.cloned.1.call-update) | async-done | bytes 3219472 | tf_op jit(solution)/shard_map/all_gather | solution.py:370
  117.0 110.7 %all-reduce.47.cloned.1.call-done = bf16[4096,512]{1,0:T(8,128)(2,1)} async-done(((bf16[4096,512]{1,0:T(8,128)(2,1)}), bf16[4096,512]{1,0:T(8,128)(2,1)}) %all-reduce.47.cloned.1.call-update) | async-done | bytes 4194320 | tf_op jit(solution)/shard_map/psum | solution.py:389
  255.9 87.4 %all-reduce.49.cloned.1.call-done = bf16[1024,512]{1,0:T(8,128)(2,1)} async-done(((bf16[1024,512]{1,0:T(8,128)(2,1)}), bf16[1024,512]{1,0:T(8,128)(2,1)}) %all-reduce.49.cloned.1.call-update) | async-done | bytes 1048592 | tf_op jit(solution)/shard_map/psum | solution.py:408
  389.8 89.7 %all-reduce.51.cloned.1.call-done = bf16[1024,512]{1,0:T(8,128)(2,1)} async-done(((bf16[1024,512]{1,0:T(8,128)(2,1)}), bf16[1024,512]{1,0:T(8,128)(2,1)}) %all-reduce.51.cloned.1.call-update) | async-done | bytes 1048592 | tf_op jit(solution)/shard_map/psum | solution.py:408
  523.9 95.9 %all-reduce.53.cloned.1.call-done = bf16[1024,512]{1,0:T(8,128)(2,1)} async-done(((bf16[1024,512]{1,0:T(8,128)(2,1)}), bf16[1024,512]{1,0:T(8,128)(2,1)}) %all-reduce.53.cloned.1.call-update) | async-done | bytes 1048592 | tf_op jit(solution)/shard_map/psum | solution.py:408
  664.5 95.7 %all-reduce.55.cloned.1.call-done = bf16[1024,512]{1,0:T(8,128)(2,1)} async-done(((bf16[1024,512]{1,0:T(8,128)(2,1)}), bf16[1024,512]{1,0:T(8,128)(2,1)}) %all-reduce.55.cloned.1.call-update) | async-done | bytes 1048592 | tf_op jit(solution)/shard_map/psum | solution.py:408
  809.2 95.9 %all-reduce.57.cloned.1.call-done = bf16[1024,512]{1,0:T(8,128)(2,1)} async-done(((bf16[1024,512]{1,0:T(8,128)(2,1)}), bf16[1024,512]{1,0:T(8,128)(2,1)}) %all-reduce.57.cloned.1.call-update) | async-done | bytes 1048592 | tf_op jit(solution)/shard_map/psum | solution.py:408
  954.6 96.0 %all-reduce.59.cloned.1.call-done = bf16[1024,512]{1,0:T(8,128)(2,1)} async-done(((bf16[1024,512]{1,0:T(8,128)(2,1)}), bf16[1024,512]{1,0:T(8,128)(2,1)}) %all-reduce.59.cloned.1.call-update) | async-done | bytes 1048592 | tf_op jit(solution)/shard_map/psum | solution.py:408
  1130.0 71.1 %all-reduce.61.cloned.1.call-done = bf16[1024,512]{1,0:T(8,128)(2,1)} async-done(((bf16[1024,512]{1,0:T(8,128)(2,1)}), bf16[1024,512]{1,0:T(8,128)(2,1)}) %all-reduce.61.cloned.1.call-update) | async-done | bytes 1048592 | tf_op jit(solution)/shard_map/psum | solution.py:408
  1219.9 34.2 %reduce-scatter.3.cloned.1.call-done = bf16[1024,512]{1,0:T(8,128)(2,1)} async-done(((bf16[4096,512]{1,0:T(8,128)(2,1)}), bf16[1024,512]{1,0:T(8,128)(2,1)}) %reduce-scatter.3.cloned.1.call-update) | async-done | bytes 1048592 | tf_op jit(solution)/shard_map/reduce_scatter | solution.py:40
  1279.2 23.6 all-gather.6.cloned.1.call-done
  1420.1 95.9 %all-reduce.63.cloned.1.call-done = bf16[4096,512]{1,0:T(8,128)(2,1)} async-done(((bf16[4096,512]{1,0:T(8,128)(2,1)}), bf16[4096,512]{1,0:T(8,128)(2,1)}) %all-reduce.63.cloned.1.call-update) | async-done | bytes 4194320 | tf_op jit(solution)/shard_map/psum | solution.py:447
  1588.8 73.2 %all-reduce.65.cloned.1.call-done = bf16[1024,512]{1,0:T(8,128)(2,1)} async-done(((bf16[1024,512]{1,0:T(8,128)(2,1)}), bf16[1024,512]{1,0:T(8,128)(2,1)}) %all-reduce.65.cloned.1.call-update) | async-done | bytes 1048592 | tf_op jit(solution)/shard_map/psum | solution.py:465
  1682.0 23.6 while.197
  1737.9 75.8 %all-reduce.67.cloned.1.call-done = bf16[1024,512]{1,0:T(8,128)(2,1)} async-done(((bf16[1024,512]{1,0:T(8,128)(2,1)}), bf16[1024,512]{1,0:T(8,128)(2,1)}) %all-reduce.67.cloned.1.call-update) | async-done | bytes 1048592 | tf_op jit(solution)/shard_map/psum | solution.py:465
  1831.2 23.7 while.198
  1891.6 74.4 %all-reduce.69.cloned.1.call-done = bf16[1024,512]{1,0:T(8,128)(2,1)} async-done(((bf16[1024,512]{1,0:T(8,128)(2,1)}), bf16[1024,512]{1,0:T(8,128)(2,1)}) %all-reduce.69.cloned.1.call-update) | async-done | bytes 1048592 | tf_op jit(solution)/shard_map/psum | solution.py:465
  1987.8 23.7 while.199
  2064.3 58.4 %all-reduce.71.cloned.1.call-done = bf16[1024,512]{1,0:T(8,128)(2,1)} async-done(((bf16[1024,512]{1,0:T(8,128)(2,1)}), bf16[1024,512]{1,0:T(8,128)(2,1)}) %all-reduce.71.cloned.1.call-update) | async-done | bytes 1048592 | tf_op jit(solution)/shard_map/psum | solution.py:465
  2200.8 76.1 %all-reduce.73.cloned.1.call-done = bf16[1024,512]{1,0:T(8,128)(2,1)} async-done(((bf16[1024,512]{1,0:T(8,128)(2,1)}), bf16[1024,512]{1,0:T(8,128)(2,1)}) %all-reduce.73.cloned.1.call-update) | async-done | bytes 1048592 | tf_op jit(solution)/shard_map/psum | solution.py:465
  2297.9 23.1 while.201
  2354.6 76.0 %all-reduce.75.cloned.1.call-done = bf16[1024,512]{1,0:T(8,128)(2,1)} async-done(((bf16[1024,512]{1,0:T(8,128)(2,1)}), bf16[1024,512]{1,0:T(8,128)(2,1)}) %all-reduce.75.cloned.1.call-update) | async-done | bytes 1048592 | tf_op jit(solution)/shard_map/psum | solution.py:465
  2504.9 74.8 %all-reduce.77.cloned.1.call-done = bf16[1024,512]{1,0:T(8,128)(2,1)} async-done(((bf16[1024,512]{1,0:T(8,128)(2,1)}), bf16[1024,512]{1,0:T(8,128)(2,1)}) %all-reduce.77.cloned.1.call-update) | async-done | bytes 1048592 | tf_op jit(solution)/shard_map/psum | solution.py:465
  2812.4 31.9 %scatter_custom_fusion = f32[1572,512]{1,0:T(8,128)S(1)} fusion(s32[4096]{0:T(1024)} %bitcast.2707, bf16[4096,512]{1,0:T(8,128)(2,1)} %all-gather.8.cloned.1.call-done, f32[]{:T(128)} %constant.1030.clone.1, pred[4096]{0:T(1024)(128)(4,1)S(1)} %copy-done.291), kind=kCustom, calls=%fused_computation.342 | custom fusion | flops 6291456 | bytes 7418880 | tf_op jit(solution)/shard_map/scatter-add | solution.py:478
  (1894 shorter events, 1509.4 us)
Async XLA Ops:
  7.2 75.4 %all-gather.4.cloned.1.call-start = ((), (), s32[]{:S(2)}) async-start(), calls=%async_computation.13 | async-start | bytes 4024320 | tf_op jit(solution)/shard_map/all_gather | solution.py:370
  9.8 218.0 %all-reduce.47.cloned.1.call-start = ((), (), s32[]{:S(2)}) async-start(), calls=%async_computation.14 | async-start | bytes 8388608 | tf_op jit(solution)/shard_map/psum | solution.py:389
  114.7 228.5 %all-reduce.49.cloned.1.call-start = ((), (), s32[]{:S(2)}) async-start(), calls=%async_computation.15 | async-start | bytes 2097152 | tf_op jit(solution)/shard_map/psum | solution.py:408
  255.6 223.9 %all-reduce.51.cloned.1.call-start = ((), (), s32[]{:S(2)}) async-start(), calls=%async_computation.16 | async-start | bytes 2097152 | tf_op jit(solution)/shard_map/psum | solution.py:408
  389.8 230.0 %all-reduce.53.cloned.1.call-start = ((), (), s32[]{:S(2)}) async-start(), calls=%async_computation.17 | async-start | bytes 2097152 | tf_op jit(solution)/shard_map/psum | solution.py:408
  523.8 236.4 %all-reduce.55.cloned.1.call-start = ((), (), s32[]{:S(2)}) async-start(), calls=%async_computation.18 | async-start | bytes 2097152 | tf_op jit(solution)/shard_map/psum | solution.py:408
  664.5 240.6 %all-reduce.57.cloned.1.call-start = ((), (), s32[]{:S(2)}) async-start(), calls=%async_computation.19 | async-start | bytes 2097152 | tf_op jit(solution)/shard_map/psum | solution.py:408
  809.1 241.6 %all-reduce.59.cloned.1.call-start = ((), (), s32[]{:S(2)}) async-start(), calls=%async_computation.20 | async-start | bytes 2097152 | tf_op jit(solution)/shard_map/psum | solution.py:408
  954.6 246.4 %all-reduce.61.cloned.1.call-start = ((), (), s32[]{:S(2)}) async-start(), calls=%async_computation.21 | async-start | bytes 2097152 | tf_op jit(solution)/shard_map/psum | solution.py:408
  1105.2 148.9 %reduce-scatter.3.cloned.1.call-start = ((), (), s32[]{:S(2)}) async-start(), calls=%async_computation.22 | async-start | bytes 5242880 | tf_op jit(solution)/shard_map/reduce_scatter | solution.py:40
  1210.7 92.2 %all-gather.6.cloned.1.call-start = ((), (), s32[]{:S(2)}) async-start(), calls=%async_computation.23 | async-start | bytes 5242880 | tf_op jit(solution)/shard_map/all_gather | solution.py:41
  1341.5 174.4 %all-reduce.63.cloned.1.call-start = ((), (), s32[]{:S(2)}) async-start(), calls=%async_computation.24 | async-start | bytes 8388608 | tf_op jit(solution)/shard_map/psum | solution.py:447
  1405.9 256.1 %all-reduce.65.cloned.1.call-start = ((), (), s32[]{:S(2)}) async-start(), calls=%async_computation.25 | async-start | bytes 2097152 | tf_op jit(solution)/shard_map/psum | solution.py:465
  1574.4 239.3 %all-reduce.67.cloned.1.call-start = ((), (), s32[]{:S(2)}) async-start(), calls=%async_computation.26 | async-start | bytes 2097152 | tf_op jit(solution)/shard_map/psum | solution.py:465
  1724.7 241.4 %all-reduce.69.cloned.1.call-start = ((), (), s32[]{:S(2)}) async-start(), calls=%async_computation.27 | async-start | bytes 2097152 | tf_op jit(solution)/shard_map/psum | solution.py:465
  1976.7 68.9 %all-to-all-start.1 = ((f32[32,1,1]{2,1,0:T(1,128)}), f32[32,1,1]{2,1,0:T(1,128)}, u32[]{:S(2)}, u32[]{:S(2)}) async-start(f32[32,1,1]{2,1,0:T(1,128)} %broadcast_in_dim.569), calls=%async_computation.2 | async-start | bytes 32768 | tf_op jit(solution)/shard_map/all_to_all | solution.py:46
  1983.2 139.5 %all-reduce.71.cloned.1.call-start = ((), (), s32[]{:S(2)}) async-start(), calls=%async_computation.28 | async-start | bytes 2097152 | tf_op jit(solution)/shard_map/psum | solution.py:465
  2048.3 84.4 %all-to-all-start.10 = ((f32[32,2,512]{2,1,0:T(2,128)}), f32[32,2,512]{2,1,0:T(2,128)}, u32[]{:S(2)}, u32[]{:S(2)}) async-start(f32[32,2,512]{2,1,0:T(2,128)} %broadcast_in_dim.1052), calls=%async_computation.12 | async-start | bytes 262144 | tf_op jit(solution)/shard_map/all_to_all | solution.py:46
  2058.2 218.8 %all-reduce.73.cloned.1.call-start = ((), (), s32[]{:S(2)}) async-start(), calls=%async_computation.29 | async-start | bytes 2097152 | tf_op jit(solution)/shard_map/psum | solution.py:465
  2189.5 241.1 %all-reduce.75.cloned.1.call-start = ((), (), s32[]{:S(2)}) async-start(), calls=%async_computation.30 | async-start | bytes 2097152 | tf_op jit(solution)/shard_map/psum | solution.py:465
  2341.7 238.0 %all-reduce.77.cloned.1.call-start = ((), (), s32[]{:S(2)}) async-start(), calls=%async_computation.31 | async-start | bytes 2097152 | tf_op jit(solution)/shard_map/psum | solution.py:465
  2491.1 186.9 %reduce-scatter.5.cloned.1.call-start = ((), (), s32[]{:S(2)}) async-start(), calls=%async_computation.32 | async-start | bytes 5242880 | tf_op jit(solution)/shard_map/reduce_scatter | solution.py:40
  2650.5 161.9 %all-gather.8.cloned.1.call-start = ((), (), s32[]{:S(2)}) async-start(), calls=%async_computation.33 | async-start | bytes 5242880 | tf_op jit(solution)/shard_map/all_gather | solution.py:41
  2713.7 70.5 %all-to-all-start.5 = ((bf16[4,320,8]{1,2,0:T(8,128)(2,1)}), bf16[4,320,8]{1,2,0:T(8,128)(2,1)S(1)}, u32[]{:S(2)}, u32[]{:S(2)}) async-start(bf16[4,320,8]{1,2,0:T(8,128)(2,1)} %broadcast_in_dim.1032), calls=%async_computation.6 | async-start | bytes 49152 | tf_op jit(solution)/shard_map/all_to_all | solution.py:46
  (430 other events, 11249.9 us)
Sparse Core Ops, SparseCore 0:
  10.3 72.3 all-gather.3
  114.8 112.8 all-reduce.46
  255.8 87.4 all-reduce.48
  389.9 89.5 all-reduce.50
  523.9 95.8 all-reduce.52
  664.6 95.5 all-reduce.54
  809.2 95.8 all-reduce.56
  954.7 95.9 all-reduce.58
  1105.3 95.6 all-reduce.60
  1210.8 43.2 reduce-scatter.2
  1255.9 46.9 all-gather.5
  1406.0 109.8 all-reduce.62
  1574.5 87.4 all-reduce.64
  1724.8 88.8 all-reduce.66
  1874.1 91.9 all-reduce.68
  2030.9 91.8 all-reduce.70
  2189.6 87.3 all-reduce.72
  2341.8 88.7 all-reduce.74
  2491.2 88.4 all-reduce.76
  2590.1 43.2 reduce-scatter.4
  2678.1 44.3 all-gather.7
where the time goes:
time: 2960 us; the launch traced here: 2940 us
  waiting for transfers between devices  1510 us (51%)
  other arithmetic  523 us (18%)
  local copies, waits for them, and re-layouts  409 us (14%)
  matrix products  362 us (12%)
  starting transfers between devices  83.7 us (3%)
  between operations  32.2 us (1%)
    psum x7, waiting for transfers between devices, on_device(): lax.psum(branch.astype(jnp.bfloat16), 'tensor').astype(jnp.float32)  632 us
    psum x7, waiting for transfers between devices, on_device(): lax.psum(grad_part.astype(jnp.bfloat16), 'tensor').astype(jnp.float32)  509 us
    dynamic_update_slice x67, other arithmetic, store(): lax.dynamic_update_index_in_dim(buffer, jnp.where(valid, value, old_value...  113 us
    psum x1, waiting for transfers between devices, on_device(): lax.psum(jnp.where(inside[:, None], looked, 0.0).astype(jnp.bfloat16), ('...  111 us
    psum x1, waiting for transfers between devices, on_device(): lax.psum(grad_normed.astype(jnp.bfloat16), ('section', 'tensor'))  95.9 us
    dynamic_slice x41, local copies, waits for them, and re-layouts, store(): old_value = lax.dynamic_index_in_dim(buffer, slot, 0, False)  87.8 us
    dot_general x29, matrix products, dot_cols(): lax.dot_general(left, right, (((1,), (1,)), ((), ())), preferred_element_...  76.8 us
    all_gather x1, waiting for transfers between devices, on_device(): lax.all_gather(tables.astype(jnp.bfloat16), 'dp', axis=2, tiled=True)  71.5 us
  transfers between devices with their start and end apart: 44, of which 24 were waited for; matrix products, arithmetic and copies ran while one was open for 17% of the time, Pallas kernels for 0%

commit v1 on v0

v1 whole, which is shorter than its diff:
```python
import functools
import math

import jax
import jax.numpy as jnp
import numpy as np
from jax import lax
from jax.experimental import pallas as pl
from jax.experimental.pallas import tpu as pltpu
from jax.sharding import Mesh
from jax.sharding import PartitionSpec as P

D = 512
HEAD = 64
ROT = 16
VOCAB = 50304
LAYERS = 4
LENGTH = 1024
RANK = 8
STEP = 5
BLOCK = 128

EPS_NORM = 1e-05
MOMENTUM = 0.9
NEG_BIG = -1e30
HIGH = lax.Precision.HIGHEST
BF = jnp.bfloat16
F32 = jnp.float32
MESH_ID = pl.DeviceIdType.MESH
FAR = (2, 1, 3)
PLANE = [(2, 2), (2, 1), (2, 3), (1, 2), (3, 2), (2, 0), (0, 2), (1, 1), (1, 3), (3, 1), (3, 3), (1, 0), (3, 0), (0, 1), (0, 3)]


def where_am_i():
    core, z = lax.axis_index("co"), lax.axis_index("zz")
    y = lax.axis_index("yh") * 2 + lax.axis_index("yl")
    return y, core, z


def at_chip(y, z):
    return {"yh": y // 2, "yl": lax.rem(y, 2), "zz": z}


def send(src, dst, sems, at, device):
    copy = pltpu.make_async_remote_copy(
        src_ref=src,
        dst_ref=dst,
        send_sem=sems[0].at[at],
        recv_sem=sems[1].at[at],
        device_id=device,
        device_id_type=MESH_ID,
    )
    copy.start()
    return copy


def greet(devices):
    barrier = pltpu.get_barrier_semaphore()
    for device in devices:
        pl.semaphore_signal(barrier, inc=1, device_id=device, device_id_type=MESH_ID)
    pl.semaphore_wait(barrier, len(devices))


def sem_pairs(*counts):
    return [pltpu.SemaphoreType.DMA((n,)) for n in counts for _ in range(2)]


VMEM_SPEC = pl.BlockSpec(memory_space=pltpu.VMEM)


def kernel_call(body, out_shape, args, scratch, cid=None, limit=48):
    many = isinstance(out_shape, (list, tuple))
    return pl.pallas_call(
        body,
        out_shape=out_shape,
        in_specs=[VMEM_SPEC] * len(args),
        out_specs=[VMEM_SPEC] * len(out_shape) if many else VMEM_SPEC,
        scratch_shapes=scratch,
        compiler_params=pltpu.CompilerParams(
            collective_id=cid, has_side_effects=cid is not None, vmem_limit_bytes=limit * 2**20
        ),
    )(*args)


def normed_rows(values):
    center = values - jnp.mean(values, -1, keepdims=True)
    spread = jnp.mean(center * center, -1, keepdims=True)
    scale = lax.rsqrt(spread + EPS_NORM)
    return center * scale, scale


def norm_back(values, grad):
    hat, scale = normed_rows(values)
    return scale * (
        grad
        - jnp.mean(grad, -1, keepdims=True)
        - hat * jnp.mean(grad * hat, -1, keepdims=True)
    )


def row_sum(part, r1, s, r2, sems1, sems2):
    y, core, z = where_am_i()
    first = []
    for i, k in enumerate(FAR + (0,)):
        zz = lax.rem(z + k, 4)
        first.append(send(part.at[(1 - core) * 4 + zz], r1.at[i], sems1, i, {"co": 1 - core}))
    second = []
    for i, k in enumerate(FAR):
        zz = lax.rem(z + k, 4)
        first[i].wait_recv()
        s[i] = (part[core * 4 + zz].astype(F32) + r1[i].astype(F32)).astype(BF)
        second.append(send(s.at[i], r2.at[i], sems2, i, {"zz": zz}))
    first[3].wait_recv()
    total = part[core * 4 + z].astype(F32) + r1[3].astype(F32)
    for i in range(3):
        second[i].wait_recv()
        total = total + r2[i].astype(F32)
    for copy in first + second:
        copy.wait_send()
    return total


def row_gather(everyone, sems3, sems4):
    y, core, z = where_am_i()
    own = everyone.at[core * 4 + z]
    third = [
        send(own, own, sems3, i, {"zz": lax.rem(z + k, 4)}) for i, k in enumerate(FAR)
    ]
    fourth = [send(own, own, sems4, 3, {"co": 1 - core})]
    for i, k in enumerate(FAR):
        third[i].wait_recv()
        came = everyone.at[core * 4 + lax.rem(z + 4 - k, 4)]
        fourth.append(send(came, came, sems4, i, {"co": 1 - core}))
    for copy in third:
        copy.wait_send()
    for copy in fourth:
        copy.wait()


def row_peers():
    y, core, z = where_am_i()
    return [{"co": 1 - core}] + [{"zz": lax.rem(z + k, 4)} for k in FAR]


SUM_SCRATCH = [
    pltpu.VMEM((4, BLOCK, D), BF),
    pltpu.VMEM((3, BLOCK, D), BF),
    pltpu.VMEM((3, BLOCK, D), BF),
] + sem_pairs(4, 3)
GATHER_SCRATCH = sem_pairs(3, 4)


def first_body(x, everyone, a, b, c, d):
    y, core, z = where_am_i()
    greet(row_peers())
    everyone[core * 4 + z] = normed_rows(x[...])[0].astype(BF)
    row_gather(everyone, (a, b), (c, d))


def first_hat(x):
    return kernel_call(
        first_body, jax.ShapeDtypeStruct((8, BLOCK, D), BF), (x,), GATHER_SCRATCH, 1
    )


def forward_body(part, x, shift, everyone, x_new, r1, s, r2, e, f, g, h, a, b, c, d):
    y, core, z = where_am_i()
    greet(row_peers())
    after = x[...] + row_sum(part, r1, s, r2, (e, f), (g, h)) + shift[0:1]
    x_new[...] = after
    everyone[core * 4 + z] = normed_rows(after)[0].astype(BF)
    row_gather(everyone, (a, b), (c, d))


def next_hat(part, x, shift):
    return kernel_call(
        forward_body,
        [jax.ShapeDtypeStruct((8, BLOCK, D), BF), jax.ShapeDtypeStruct((BLOCK, D), F32)],
        (part, x, shift),
        SUM_SCRATCH + GATHER_SCRATCH,
        2,
    )


def last_body(part, x, shift, gains, x_new, normed, r1, s, r2, e, f, g, h):
    greet(row_peers())
    after = x[...] + row_sum(part, r1, s, r2, (e, f), (g, h)) + shift[0:1]
    x_new[...] = after
    normed[...] = (normed_rows(after)[0] * gains[0:1] + gains[1:2]).astype(BF)


def last_normed(part, x, shift, gains):
    return kernel_call(
        last_body,
        [jax.ShapeDtypeStruct((BLOCK, D), F32), jax.ShapeDtypeStruct((BLOCK, D), BF)],
        (part, x, shift, gains),
        SUM_SCRATCH,
        3,
    )


def spread_body(grad, everyone, a, b, c, d):
    y, core, z = where_am_i()
    greet(row_peers())
    everyone[core * 4 + z] = grad[...].astype(BF)
    row_gather(everyone, (a, b), (c, d))


def spread_grad(grad):
    return kernel_call(
        spread_body, jax.ShapeDtypeStruct((8, BLOCK, D), BF), (grad,), GATHER_SCRATCH, 4
    )


def backward_body(part, x, grad, everyone, g_new, r1, s, r2, e, f, g, h, a, b, c, d):
    y, core, z = where_am_i()
    greet(row_peers())
    after = grad[...] + norm_back(x[...], row_sum(part, r1, s, r2, (e, f), (g, h)))
    g_new[...] = after
    everyone[core * 4 + z] = after.astype(BF)
    row_gather(everyone, (a, b), (c, d))


def next_grad(part, x, grad):
    return kernel_call(
        backward_body,
        [jax.ShapeDtypeStruct((8, BLOCK, D), BF), jax.ShapeDtypeStruct((BLOCK, D), F32)],
        (part, x, grad),
        SUM_SCRATCH + GATHER_SCRATCH,
        5,
    )


def lowest_body(part, x, grad, low, r1, s, r2, e, f, g, h):
    greet(row_peers())
    after = grad[...] + norm_back(x[...], row_sum(part, r1, s, r2, (e, f), (g, h)))
    low[...] = after.astype(BF)


def lowest_grad(part, x, grad):
    return kernel_call(
        lowest_body, jax.ShapeDtypeStruct((BLOCK, D), BF), (part, x, grad), SUM_SCRATCH, 6
    )


def plane_peers():
    y, core, z = where_am_i()
    return [{"co": 1 - core}] + [
        at_chip(lax.rem(y + dy, 4), lax.rem(z + dz, 4)) for dy, dz in PLANE
    ]


def plane_sum_body(part, out, r1, s, r2, a, b, c, d):
    y, core, z = where_am_i()
    greet(plane_peers())
    first = []
    for i, (dy, dz) in enumerate(PLANE + [(0, 0)]):
        at = lax.rem(y + dy, 4) * 8 + lax.rem(z + dz, 4)
        first.append(send(part.at[at + 4 * (1 - core)], r1.at[i], (a, b), i, {"co": 1 - core}))
    second = []
    for i, (dy, dz) in enumerate(PLANE):
        yy, zz = lax.rem(y + dy, 4), lax.rem(z + dz, 4)
        first[i].wait_recv()
        s[i] = (part[yy * 8 + core * 4 + zz].astype(F32) + r1[i].astype(F32)).astype(BF)
        second.append(send(s.at[i], r2.at[i], (c, d), i, at_chip(yy, zz)))
    first[15].wait_recv()
    total = part[y * 8 + core * 4 + z].astype(F32) + r1[15].astype(F32)
    for i in range(15):
        second[i].wait_recv()
        total = total + r2[i].astype(F32)
    for copy in first + second:
        copy.wait_send()
    out[...] = total


def plane_sum(part):
    return kernel_call(
        plane_sum_body,
        jax.ShapeDtypeStruct((BLOCK, D), F32),
        (part,),
        [
            pltpu.VMEM((16, BLOCK, D), BF),
            pltpu.VMEM((15, BLOCK, D), BF),
            pltpu.VMEM((15, BLOCK, D), BF),
        ]
        + sem_pairs(16, 15),
        7,
    )


def plane_gather_body(block, everyone, a, b, c, d):
    y, core, z = where_am_i()
    greet(plane_peers())
    own = everyone.at[y * 8 + core * 4 + z]
    everyone[y * 8 + core * 4 + z] = block[...]
    first = [
        send(own, own, (a, b), i, at_chip(lax.rem(y + dy, 4), lax.rem(z + dz, 4)))
        for i, (dy, dz) in enumerate(PLANE)
    ]
    second = [send(own, own, (c, d), 15, {"co": 1 - core})]
    for i, (dy, dz) in reversed(list(enumerate(PLANE))):
        first[i].wait_recv()
        came = everyone.at[lax.rem(y + 4 - dy, 4) * 8 + core * 4 + lax.rem(z + 4 - dz, 4)]
        second.append(send(came, came, (c, d), i, {"co": 1 - core}))
    for copy in first:
        copy.wait_send()
    for copy in second:
        copy.wait()


def plane_gather(block):
    return kernel_call(
        plane_gather_body,
        jax.ShapeDtypeStruct((32, BLOCK, D), BF),
        (block,),
        sem_pairs(15, 16),
        8,
    )


def stats_body(stats, result, came, everyone, a, b, c, d):
    y, core, z = where_am_i()
    me = y * 8 + core * 4 + z
    peers = []
    for k in range(1, 32):
        p = lax.rem(me + k, 32)
        peers.append((p, {**at_chip(p // 8, lax.rem(p, 4)), "co": lax.rem(p // 4, 2)}))
    greet([device for _, device in peers])
    copies = [
        send(stats.at[p], came.at[me], (a, b), k, device) for k, (p, device) in enumerate(peers)
    ]
    came[me] = stats[me]
    for copy in copies:
        copy.wait_recv()
    top = jnp.max(came[:, 0, :], 0, keepdims=True)
    total = jnp.sum(came[:, 1, :] * jnp.exp(came[:, 0, :] - top), 0, keepdims=True)
    target = jnp.sum(came[:, 2, :], 0, keepdims=True)
    lse = top + jnp.log(total)
    everyone[me] = jnp.concatenate([lse, lse - target, jnp.zeros((6, BLOCK), F32)], 0)
    own = everyone.at[me]
    for copy in copies:
        copy.wait_send()
    copies = [send(own, own, (c, d), k, device) for k, (_, device) in enumerate(peers)]
    for copy in copies:
        copy.wait()
    result[...] = everyone[...]


def joined_stats(stats):
    return kernel_call(
        stats_body,
        jax.ShapeDtypeStruct((32, 8, BLOCK), F32),
        (stats,),
        [pltpu.VMEM((32, 8, BLOCK), F32), pltpu.VMEM((32, 8, BLOCK), F32)] + sem_pairs(31, 31),
        9,
    )


def column_peers():
    y, core, z = where_am_i()
    return [{"co": 1 - core}] + [
        {**at_chip(lax.rem(y + dy, 4), z), "co": c} for dy in FAR for c in (0, 1)
    ]


def weights_body(cols, rows, all_cols, all_rows, a, b, c, d):
    y, core, z = where_am_i()
    greet(column_peers())
    layer = lax.rem(y, 2) * 2 + core
    home = y // 2 == core
    pairs = ((cols, all_cols, a, b), (rows, all_rows, c, d))

    def out_copy(src, dst, s, r, dy):
        return pltpu.make_async_remote_copy(
            src_ref=src,
            dst_ref=dst.at[layer],
            send_sem=s.at[dy],
            recv_sem=r.at[layer],
            device_id={**at_chip(lax.rem(y + dy, 4), z), "co": y // 2},
            device_id_type=MESH_ID,
        )

    for dy in FAR:
        for src, dst, s, r in pairs:
            out_copy(src, dst, s, r, dy).start()
    for src, dst, s, r in pairs:

        @pl.when(home)
        def _():
            pltpu.make_async_copy(src, dst.at[layer], r.at[layer]).start()

        @pl.when(jnp.logical_not(home))
        def _():
            out_copy(src, dst, s, r, 0).start()
            out_copy(src, dst, s, r, 0).wait_send()

    for dy in FAR:
        for src, dst, s, r in pairs:
            out_copy(src, dst, s, r, dy).wait_send()
    for index in range(LAYERS):
        for src, dst, s, r in pairs:
            pltpu.make_async_copy(src, dst.at[index], r.at[index]).wait()


def gathered_weights(cols, rows):
    return pl.pallas_call(
        weights_body,
        out_shape=[
            jax.ShapeDtypeStruct((LAYERS, *cols.shape), BF),
            jax.ShapeDtypeStruct((LAYERS, *rows.shape), BF),
        ],
        in_specs=[pl.BlockSpec(memory_space=pl.ANY)] * 2,
        out_specs=[pl.BlockSpec(memory_space=pl.ANY)] * 2,
        scratch_shapes=sem_pairs(4, 4),
        compiler_params=pltpu.CompilerParams(collective_id=10, has_side_effects=True),
    )(cols, rows)


def grads_body(count, *refs):
    sources, landed, sems = refs[:count], refs[count : 2 * count], refs[2 * count :]
    y, core, z = where_am_i()
    greet(column_peers())
    own_layer = lax.rem(y, 2) * 2 + core
    home = y // 2 == core

    def out_copy(n, layer):
        return pltpu.make_async_remote_copy(
            src_ref=sources[n].at[layer],
            dst_ref=landed[n].at[y],
            send_sem=sems[2 * n].at[layer],
            recv_sem=sems[2 * n + 1].at[y],
            device_id={**at_chip(core * 2 + layer // 2, z), "co": layer % 2},
            device_id_type=MESH_ID,
        )

    def both(layer, act):
        local = jnp.logical_and(home, own_layer == layer)
        for n in range(count):

            @pl.when(jnp.logical_not(local))
            def _():
                act(out_copy(n, layer))

    for layer in range(LAYERS):
        both(layer, lambda copy: copy.start())
    for n in range(count):

        @pl.when(home)
        def _():
            pltpu.make_async_copy(
                sources[n].at[own_layer], landed[n].at[y], sems[2 * n + 1].at[y]
            ).start()

    for layer in range(LAYERS):
        both(layer, lambda copy: copy.wait_send())
    for index in range(4):
        for n in range(count):
            pltpu.make_async_copy(
                sources[n].at[0], landed[n].at[index], sems[2 * n + 1].at[index]
            ).wait()


def returned_grads(*grads):
    return pl.pallas_call(
        functools.partial(grads_body, len(grads)),
        out_shape=[jax.ShapeDtypeStruct(g.shape, g.dtype) for g in grads],
        in_specs=[pl.BlockSpec(memory_space=pl.ANY)] * len(grads),
        out_specs=[pl.BlockSpec(memory_space=pl.ANY)] * len(grads),
        scratch_shapes=sem_pairs(*[4] * len(grads)),
        compiler_params=pltpu.CompilerParams(collective_id=11, has_side_effects=True),
    )(*grads)


def replicas_peers():
    x = lax.axis_index("xx")
    return [(lax.rem(x + k, 4), {"xx": lax.rem(x + k, 4)}) for k in FAR]


def replicas_exchange(block, everyone, a, b):
    x = lax.axis_index("xx")
    copies = [
        send(block, everyone.at[x], (a, b), i, device)
        for i, (_, device) in enumerate(replicas_peers())
    ]
    return copies


def features_body(block, everyone, a, b, own_sem):
    greet([device for _, device in replicas_peers()])
    copies = replicas_exchange(block, everyone, a, b)
    own = pltpu.make_async_copy(block, everyone.at[lax.axis_index("xx")], own_sem)
    own.start()
    own.wait()
    for copy in copies:
        copy.wait()


def all_features(block):
    return pl.pallas_call(
        features_body,
        out_shape=jax.ShapeDtypeStruct((4, *block.shape), block.dtype),
        in_specs=[pl.BlockSpec(memory_space=pl.ANY)],
        out_specs=pl.BlockSpec(memory_space=pl.ANY),
        scratch_shapes=sem_pairs(3) + [pltpu.SemaphoreType.DMA],
        compiler_params=pltpu.CompilerParams(collective_id=12, has_side_effects=True),
    )(block)


def left_body(left, extra, basis, extra_sum, came, came_extra, work, a, b, c, d):
    x = lax.axis_index("xx")
    greet([device for _, device in replicas_peers()])
    copies = replicas_exchange(left, came, a, b) + replicas_exchange(extra, came_extra, c, d)
    came[x] = left[...]
    came_extra[x] = extra[...]
    for copy in copies:
        copy.wait()
    extra_sum[...] = jnp.sum(came_extra[...], 0)
    work[...] = jnp.sum(came[...], 0)
    rows = lax.broadcasted_iota(jnp.int32, (1, RANK, 1), 1)
    for index in range(RANK):
        columns = work[...]
        one = columns[:, index : index + 1, :]
        one = one * lax.rsqrt(jnp.sum(one * one, -1, keepdims=True) + 1e-30)
        shares = jnp.sum(columns * one, -1, keepdims=True)
        work[...] = jnp.where(rows > index, columns - shares * one, columns)
        basis[:, index : index + 1, :] = one


def orthonormal_sum(left, extra):
    return kernel_call(
        left_body,
        [
            jax.ShapeDtypeStruct(left.shape, F32),
            jax.ShapeDtypeStruct(extra.shape, F32),
        ],
        (left, extra),
        [
            pltpu.VMEM((4, *left.shape), F32),
            pltpu.VMEM((4, *extra.shape), F32),
            pltpu.VMEM(left.shape, F32),
        ]
        + sem_pairs(3, 3),
        13,
    )


def right_body(right, total, came, a, b):
    x = lax.axis_index("xx")
    greet([device for _, device in replicas_peers()])
    copies = replicas_exchange(right, came, a, b)
    came[x] = right[...]
    for copy in copies:
        copy.wait()
    total[...] = jnp.sum(came[...].astype(F32), 0)


def right_sum(right):
    return kernel_call(
        right_body,
        jax.ShapeDtypeStruct(right.shape, F32),
        (right,),
        [pltpu.VMEM((4, *right.shape), BF)] + sem_pairs(3),
        14,
    )


def ema_decay():
    return min(0.999, (1.0 + STEP) / (10.0 + STEP))


def rotary_tables():
    half_rot = ROT // 2
    inverse = 10000.0 ** (-jnp.arange(half_rot, dtype=F32) * (2.0 / ROT))
    angles = jnp.arange(LENGTH, dtype=F32)[:, None] * inverse[None, :]
    return (jnp.cos(angles), jnp.sin(angles))


def rotate(heads, cosine, sine):
    half_rot = ROT // 2
    first = heads[..., :half_rot]
    second = heads[..., half_rot:ROT]
    return jnp.concatenate(
        [first * cosine - second * sine, second * cosine + first * sine, heads[..., ROT:]], -1
    )


def dot_rows(left, right):
    return lax.dot_general(
        left, right, (((0,), (0,)), ((), ())), preferred_element_type=F32
    )


def dot_cols(left, right):
    return lax.dot_general(
        left, right, (((1,), (1,)), ((), ())), preferred_element_type=F32
    )


def dot_plain(left, right):
    return jnp.dot(left, right, preferred_element_type=F32)


ATT_BLOCK = 512


def causal(start, stop):
    rows = start + lax.broadcasted_iota(jnp.int32, (stop - start, stop), 0)
    return rows >= lax.broadcasted_iota(jnp.int32, (stop - start, stop), 1)


def attention_forward(q_rot, k_rot, v_val):
    outputs, all_lse = [], []
    for start in range(0, LENGTH, ATT_BLOCK):
        stop = start + ATT_BLOCK
        scores = dot_cols(q_rot[start:stop], k_rot[:stop]) * HEAD ** (-0.5)
        scores = jnp.where(causal(start, stop), scores, NEG_BIG)
        top = jnp.max(scores, -1, keepdims=True)
        expo = jnp.exp(scores - top)
        total = jnp.sum(expo, -1, keepdims=True)
        probs = (expo / total).astype(BF)
        outputs.append(dot_plain(probs, v_val[:stop]))
        all_lse.append(top + jnp.log(total))
    return (jnp.concatenate(outputs, 0), jnp.concatenate(all_lse, 0))


def attention_backward(q_rot, k_rot, v_val, lse, grad_out):
    scale = HEAD ** (-0.5)
    grad_query, grad_key, grad_value = [], 0.0, 0.0
    for start in range(0, LENGTH, ATT_BLOCK):
        stop = start + ATT_BLOCK
        spare = ((0, LENGTH - stop), (0, 0))
        scores = dot_cols(q_rot[start:stop], k_rot[:stop]) * scale
        probs = jnp.where(causal(start, stop), jnp.exp(scores - lse[start:stop]), 0.0)
        grad_probs = dot_cols(grad_out[start:stop], v_val[:stop])
        grad_scores = (
            probs * (grad_probs - jnp.sum(grad_probs * probs, -1, keepdims=True))
        ).astype(BF)
        grad_query.append(dot_plain(grad_scores, k_rot[:stop]) * scale)
        grad_key = grad_key + jnp.pad(dot_rows(grad_scores, q_rot[start:stop]), spare) * scale
        grad_value = grad_value + jnp.pad(
            dot_rows(probs.astype(BF), grad_out[start:stop]), spare
        )
    return (jnp.concatenate(grad_query, 0), grad_key, grad_value)


def block_forward(hat, weights, cosine, sine):
    w_cols, w_rows, bias, vector = weights
    wide = hat.astype(F32)
    first_in = (wide * vector[0] + vector[1]).astype(BF)
    second_in = (wide * vector[2] + vector[3]).astype(BF)
    qkv = dot_plain(first_in, w_cols[:, : 3 * HEAD]) + bias[: 3 * HEAD]
    up_val = dot_plain(second_in, w_cols[:, 3 * HEAD :]) + bias[3 * HEAD :]
    q_rot = rotate(qkv[:, :HEAD], cosine, sine).astype(BF)
    k_rot = rotate(qkv[:, HEAD : 2 * HEAD], cosine, sine).astype(BF)
    v_val = qkv[:, 2 * HEAD :].astype(BF)
    attended, lse = attention_forward(q_rot, k_rot, v_val)
    attended = attended.astype(BF)
    hidden = jax.nn.gelu(up_val, approximate=False).astype(BF)
    branch = dot_plain(attended, w_rows[:HEAD]) + dot_plain(hidden, w_rows[HEAD:])
    return (
        branch.astype(BF),
        (hat, first_in, second_in, q_rot, k_rot, v_val, lse, attended, up_val, hidden),
    )


def gelu_exact(values):
    return jax.nn.gelu(values, approximate=False)


def block_backward(grad_low, kept, weights, cosine, sine):
    w_cols, w_rows, bias, vector = weights
    hat, first_in, second_in, q_rot, k_rot, v_val, lse, attended, up_val, hidden = kept
    grad_rows = jnp.concatenate([dot_rows(attended, grad_low), dot_rows(hidden, grad_low)], 0)
    grad_att = dot_cols(grad_low, w_rows[:HEAD]).astype(BF)
    grad_hidden = dot_cols(grad_low, w_rows[HEAD:])
    grad_up = jax.vjp(gelu_exact, up_val)[1](grad_hidden)[0].astype(BF)
    grad_query, grad_key, grad_value = attention_backward(q_rot, k_rot, v_val, lse, grad_att)
    grad_query = rotate(grad_query, cosine, -sine)
    grad_key = rotate(grad_key, cosine, -sine)
    grad_qkv = jnp.concatenate([grad_query, grad_key, grad_value], 1).astype(BF)
    grad_cols = jnp.concatenate([dot_rows(first_in, grad_qkv), dot_rows(second_in, grad_up)], 1)
    grad_bias = jnp.concatenate(
        [jnp.sum(grad_qkv.astype(F32), 0), jnp.sum(grad_up.astype(F32), 0)]
    )
    grad_first = dot_cols(grad_qkv, w_cols[:, : 3 * HEAD])
    grad_second = dot_cols(grad_up, w_cols[:, 3 * HEAD :])
    wide = hat.astype(F32)
    grad_norms = jnp.stack(
        [
            jnp.sum(grad_first * wide, 0),
            jnp.sum(grad_first, 0),
            jnp.sum(grad_second * wide, 0),
            jnp.sum(grad_second, 0),
        ]
    )
    grad_hat = grad_first * vector[0] + grad_second * vector[2]
    return (grad_hat.astype(BF), (grad_cols.astype(BF), grad_rows.astype(BF), grad_bias, grad_norms))


def momentum_step(weight, moment, average, grad, rate):
    decay = ema_decay()
    new_moment = MOMENTUM * moment + (1.0 - MOMENTUM) * grad
    new_weight = weight - rate * new_moment
    return (new_weight, new_moment, decay * average + (1.0 - decay) * new_weight)


def on_device(
    tokens,
    groups,
    counts,
    domain,
    w_in,
    w_back,
    tables,
    b_in,
    vecs,
    final_norm,
    w_in_mom,
    w_back_mom,
    tables_mom,
    b_in_mom,
    vecs_mom,
    final_mom,
    w_in_ema,
    w_back_ema,
    tables_ema,
    b_in_ema,
    vecs_ema,
    final_ema,
    w_in_err,
    w_back_err,
    tables_err,
    w_in_fac,
    w_back_fac,
    tables_fac,
):
    y, core, z = where_am_i()
    replica = lax.axis_index("xx")
    section = lax.axis_index("yl") * 2 + core
    vocab_part = section * 8 + lax.axis_index("yh") * 4 + z
    shard = core * 4 + z
    seq_rep = tokens.shape[0]
    row_total = seq_rep * LENGTH
    vocab_shard = tables.shape[1]
    own_cols = tables.shape[2]
    cosine, sine = rotary_tables()

    seq_index = jnp.arange(groups.shape[0], dtype=jnp.int32)
    live = seq_index % seq_rep < counts[seq_index // seq_rep]
    domain_hit = groups[:, None] == jnp.arange(domain.shape[0], dtype=jnp.int32)[None, :]
    seq_weight = jnp.where(live, jnp.sum(jnp.where(domain_hit, domain[None, :], 0.0), 1), 0.0)
    weight_total = jnp.sum(seq_weight)
    own_weight = lax.dynamic_slice_in_dim(seq_weight, replica * seq_rep, seq_rep, 0)
    token_ids = tokens[:, :LENGTH].reshape(-1)
    target_ids = tokens[:, 1:].reshape(-1)
    local_ids = token_ids - vocab_part * vocab_shard
    local_targets = target_ids - vocab_part * vocab_shard

    short = tables.astype(BF)
    spare = -vocab_shard % 16
    embed_low = all_features(jnp.pad(short[0], ((0, spare), (0, 0))))
    embed_low = jnp.transpose(embed_low, (1, 0, 2)).reshape(vocab_shard + spare, D)
    head_low = lax.all_gather(short[1], "xx", axis=1, tiled=True)
    all_cols, all_rows = gathered_weights(w_in[0].astype(BF), w_back[0].astype(BF))
    small = jnp.concatenate([vecs[0].reshape(-1), b_in[0]])
    small = lax.all_gather(small, ("yl", "co", "yh", "zz"), axis=0, tiled=False)
    small = small.reshape(LAYERS, 8, -1)
    all_vecs = small[:, 0, : 6 * D].reshape(LAYERS, 6, D)
    all_bias = lax.dynamic_index_in_dim(small[:, :, 6 * D :], shard, 1, False)

    vocab_ids = jnp.arange(vocab_shard + spare, dtype=jnp.int32)
    looked = dot_plain((local_ids[:, None] == vocab_ids[None, :]).astype(BF), embed_low)
    x = plane_sum(looked.astype(BF).reshape(32, BLOCK, D))
    hat = first_hat(x).reshape(LENGTH, D)

    weights = [
        (all_cols[index], all_rows[index], all_bias[index], all_vecs[index])
        for index in range(LAYERS)
    ]
    shifts = [
        jnp.broadcast_to((all_vecs[index, 4] + all_vecs[index, 5])[None], (8, D))
        for index in range(LAYERS)
    ]
    gains = jnp.pad(final_norm, ((0, 6), (0, 0)))
    kept, before = [], []
    for index in range(LAYERS):
        before.append(x)
        branch, keep = block_forward(hat, weights[index], cosine, sine)
        kept.append(keep)
        branch = branch.reshape(8, BLOCK, D)
        if index + 1 < LAYERS:
            hat, x = next_hat(branch, x, shifts[index])
            hat = hat.reshape(LENGTH, D)
        else:
            x, normed_own = last_normed(branch, x, shifts[index], gains)

    normed = plane_gather(normed_own).reshape(row_total, D)
    logits = dot_cols(normed, head_low)
    target_hit = local_targets[:, None] == jnp.arange(vocab_shard, dtype=jnp.int32)[None, :]
    top_local = jnp.max(logits, 1)
    total_local = jnp.sum(jnp.exp(logits - top_local[:, None]), 1)
    target_local = jnp.sum(jnp.where(target_hit, logits, 0.0), 1)
    stats = jnp.stack([top_local, total_local, target_local]).reshape(3, 32, BLOCK)
    stats = jnp.pad(jnp.transpose(stats, (1, 0, 2)), ((0, 0), (0, 5), (0, 0)))
    joined = joined_stats(stats)
    lse_all = joined[:, 0, :].reshape(-1)
    losses = joined[:, 1, :].reshape(seq_rep, LENGTH)
    loss_part = jnp.sum(own_weight * jnp.mean(losses, 1))
    row_coef = jnp.repeat(own_weight / (weight_total * LENGTH), LENGTH)
    grad_logits = (
        (jnp.exp(logits - lse_all[:, None]) - target_hit.astype(F32)) * row_coef[:, None]
    ).astype(BF)
    grad_normed = plane_sum(dot_plain(grad_logits, head_low).astype(BF).reshape(32, BLOCK, D))
    grad_table = dot_rows(grad_logits, normed)

    hat_own, _ = normed_rows(x)
    grad_gains = jnp.stack([jnp.sum(grad_normed * hat_own, 0), jnp.sum(grad_normed, 0)])
    grad = norm_back(x, grad_normed * final_norm[0])
    grad_all = spread_grad(grad)
    layer_grads = [None] * LAYERS
    grad_outbias = [None] * LAYERS
    for index in reversed(range(LAYERS)):
        grad_outbias[index] = jnp.sum(grad, 0)
        grad_hat, layer_grads[index] = block_backward(
            grad_all.reshape(LENGTH, D), kept[index], weights[index], cosine, sine
        )
        grad_hat = grad_hat.reshape(8, BLOCK, D)
        if index:
            grad_all, grad = next_grad(grad_hat, before[index], grad)
        else:
            grad_low = lowest_grad(grad_hat, before[index], grad)
    grad_embedded = plane_gather(grad_low).reshape(row_total, D)
    grad_embed = dot_rows(
        (local_ids[:, None] == jnp.arange(vocab_shard, dtype=jnp.int32)[None, :]).astype(BF),
        grad_embedded,
    )

    cols_came, rows_came, bias_came = returned_grads(
        jnp.stack([g[0] for g in layer_grads]),
        jnp.stack([g[1] for g in layer_grads]),
        jnp.stack([jnp.pad(g[2].reshape(1, -1), ((0, 7), (0, 64))) for g in layer_grads]),
    )
    bias_part = jnp.sum(bias_came, 0)
    loss_row = jnp.zeros((1, D), F32).at[0, 0].set(jnp.where(shard + y * 8 == 0, loss_part, 0.0))
    vector_parts = jnp.concatenate(
        [
            jnp.concatenate([layer_grads[index][3], grad_outbias[index][None], grad_outbias[index][None]])
            for index in range(LAYERS)
        ]
        + [grad_gains, loss_row],
        0,
    )
    vector_sums = lax.psum(vector_parts, ("yl", "co", "yh", "zz", "xx"))
    vec_sum = lax.dynamic_slice_in_dim(vector_sums, section * 6, 6, 0)
    final_sum = vector_sums[6 * LAYERS : 6 * LAYERS + 2]
    loss_sum = vector_sums[6 * LAYERS + 2, 0]

    full_in = jnp.sum(cols_came.astype(F32), 0) + w_in_err[0, 0]
    full_back = jnp.sum(rows_came.astype(F32), 0) + w_back_err[0, 0]
    full_embed = grad_embed + tables_err[0, 0]
    full_head = grad_table + tables_err[0, 1]
    left = jnp.stack(
        [
            jnp.einsum("dn,nr->rd", full_in, w_in_fac[0], precision=HIGH),
            jnp.einsum("nd,nr->rd", full_back, w_back_fac[0], precision=HIGH),
            jnp.einsum("nd,nr->rd", full_embed, tables_fac[0], precision=HIGH),
            jnp.einsum("nd,nr->rd", full_head, tables_fac[1], precision=HIGH),
        ]
    )
    basis, bias_sum = orthonormal_sum(left, bias_part)
    bias_sum = bias_sum[:1, : b_in.shape[1]]
    right_in = jnp.einsum("dn,rd->rn", full_in, basis[0], precision=HIGH)
    right_back = jnp.einsum("nd,rd->rn", full_back, basis[1], precision=HIGH)
    right_embed = jnp.einsum("nd,rd->rn", full_embed, basis[2], precision=HIGH)
    right_head = jnp.einsum("nd,rd->rn", full_head, basis[3], precision=HIGH)
    rights = [right_in, right_back, right_embed, right_head]
    joint = jnp.concatenate(rights, 1).astype(BF)
    width = joint.shape[1]
    joint = right_sum(jnp.pad(joint, ((0, 8), (0, -width % 128))))[:8]
    sums, at = [], 0
    for right in rights:
        sums.append(joint[:, at : at + right.shape[1]])
        at += right.shape[1]
    sum_in, sum_back, sum_embed, sum_head = sums
    red_in = jnp.einsum("rd,rn->dn", basis[0], sum_in, precision=HIGH)
    red_back = jnp.einsum("rn,rd->nd", sum_back, basis[1], precision=HIGH)
    own_basis = lax.dynamic_slice_in_dim(basis[2:], replica * own_cols, own_cols, 2)
    red_tab = jnp.stack(
        [
            jnp.einsum("rn,rd->nd", sum_embed, own_basis[0], precision=HIGH),
            jnp.einsum("rn,rd->nd", sum_head, own_basis[1], precision=HIGH),
        ]
    )
    err_in_new = full_in - jnp.einsum("rd,rn->dn", basis[0], right_in, precision=HIGH)
    err_back_new = full_back - jnp.einsum("rn,rd->nd", right_back, basis[1], precision=HIGH)
    err_tab_new = jnp.stack(
        [
            full_embed - jnp.einsum("rn,rd->nd", right_embed, basis[2], precision=HIGH),
            full_head - jnp.einsum("rn,rd->nd", right_head, basis[3], precision=HIGH),
        ]
    )
    token_count = lax.axis_size("xx") * seq_rep * LENGTH
    rate_layer = 2.0 * math.sqrt(token_count)
    rate_vector = 6.0 * math.sqrt(token_count)
    rate_table = jnp.array([50.0, 0.5], F32).reshape(2, 1, 1) * math.sqrt(token_count * VOCAB)
    in_w, in_m, in_e = momentum_step(w_in, w_in_mom, w_in_ema, red_in[None], rate_layer)
    back_w, back_m, back_e = momentum_step(
        w_back, w_back_mom, w_back_ema, red_back[None], rate_layer
    )
    tab_w, tab_m, tab_e = momentum_step(tables, tables_mom, tables_ema, red_tab, rate_table)
    bias_w, bias_m, bias_e = momentum_step(b_in, b_in_mom, b_in_ema, bias_sum, rate_layer)
    vec_w, vec_m, vec_e = momentum_step(vecs, vecs_mom, vecs_ema, vec_sum[None], rate_vector)
    fin_w, fin_m, fin_e = momentum_step(final_norm, final_mom, final_ema, final_sum, rate_layer)
    return (
        loss_sum,
        weight_total,
        in_w,
        back_w,
        tab_w,
        bias_w,
        vec_w,
        fin_w,
        in_m,
        back_m,
        tab_m,
        bias_m,
        vec_m,
        fin_m,
        in_e,
        back_e,
        tab_e,
        bias_e,
        vec_e,
        fin_e,
        err_in_new[None, None],
        err_back_new[None, None],
        err_tab_new[None],
        sum_in.T[None],
        sum_back.T[None],
        sum_embed.T,
        sum_head.T,
    )


def solution(mesh):
    fine = Mesh(
        np.asarray(mesh.devices).reshape(2, 2, 2, 4, 4), ("yl", "co", "yh", "zz", "xx")
    )
    names = {"section": ("yl", "co"), "tensor": ("yh", "zz"), "dp": ("xx",)}

    def spec(*axes):
        return P(*[None if a is None else sum((names[n] for n in a.split()), ()) for a in axes])

    layer_in, layer_back = spec("section", None, "tensor"), spec("section", "tensor", None)
    table, bias = spec(None, "section tensor", "dp"), spec("section", "tensor")
    vector = spec("section", None, None)
    params = (layer_in, layer_back, table, bias, vector, P())
    errors = (
        spec("dp", "section", None, "tensor"),
        spec("dp", "section", "tensor", None),
        spec("dp", None, "section tensor", None),
    )
    in_specs = (
        (spec("dp", None), P(), P(), P())
        + params * 3
        + errors
        + (layer_back, layer_back, spec(None, "section tensor", None))
    )
    out_specs = (
        (P(), P())
        + params * 3
        + errors
        + (layer_back, layer_back, spec("section tensor", None), spec("section tensor", None))
    )
    return jax.shard_map(
        on_device, mesh=fine, in_specs=in_specs, out_specs=out_specs, check_vma=False
    )
```

time: 2960 us -> 861 us (0.29)
  waiting for transfers between devices: 1510 us -> 0.06 us
  other arithmetic: 523 us -> 58.2 us
  Pallas kernels: 0 us -> 455 us
  local copies, waits for them, and re-layouts: 409 us -> 78.9 us
  matrix products: 362 us -> 173 us
  starting transfers between devices: 83.7 us -> 0.08 us
  blocking collectives: 0 us -> 64.8 us
    psum x16 -> x0, waiting for transfers between devices: 1350 us -> none  [the longest x7 632 us: on_device(): lax.psum(branch.astype(jnp.bfloat16), 'tensor').astype(jnp.float32)]
    pallas_call x0 -> x20, Pallas kernels: none -> 455 us  [the longest x17 345 us: kernel_call(): pl.pallas_call(body, out_shape=out_shape, in_specs=[VMEM_SPEC] * len(args...]
    reduce_sum x104 -> x25, other arithmetic: 163 us -> 14.7 us  [the longest x4 3.77 us: on_device(): grad_outbias[index] = jnp.sum(grad, 0)]
    dot_general x139 -> x50, matrix products: 216 us -> 85.6 us  [the longest x34 52.9 us: dot_plain(): return jnp.dot(left, right, preferred_element_type=F32)]
    dynamic_update_slice x67 -> x0, other arithmetic: 113 us -> none  [store(): lax.dynamic_update_index_in_dim(buffer, jnp.where(valid, value, old_value...]
    dynamic_slice x83 -> x0, local copies, waits for them, and re-layouts: 112 us -> none  [the longest x41 87.8 us: store(): old_value = lax.dynamic_index_in_dim(buffer, slot, 0, False)]
    convert_element_type x49 -> x13, other arithmetic: 104 us -> 7.56 us  [the longest x8 3.68 us: attention_backward(): grad_scores = (probs * (grad_probs - jnp.sum(grad_probs * probs, -1, keep...]
    all_gather x3 -> x1, waiting for transfers between devices: 95.1 us -> 0.01 us  [on_device(): head_low = lax.all_gather(short[1], 'xx', axis=1, tiled=True)]
  transfers between devices with their start and end apart: 44 -> 2, of which waited for: 24 -> 0; matrix products, arithmetic and copies ran while one was open for 17% -> 9% of each run, Pallas kernels for 0% -> 27%
where the time goes in v1:
time: 861 us; the launch traced here: 852 us
  Pallas kernels  455 us (53%)
  matrix products  173 us (20%)
  local copies, waits for them, and re-layouts  78.9 us (9%)
  blocking collectives  64.8 us (8%)
  other arithmetic  58.2 us (7%)
  between operations  22 us (3%)
    pallas_call x17, Pallas kernels, kernel_call(): pl.pallas_call(body, out_shape=out_shape, in_specs=[VMEM_SPEC] * len(args...  345 us
    psum x1, blocking collectives, on_device(): vector_sums = lax.psum(vector_parts, ('yl', 'co', 'yh', 'zz', 'xx'))  64.8 us
    dot_general x34, matrix products, dot_plain(): return jnp.dot(left, right, preferred_element_type=F32)  52.9 us
    unnamed x564, local copies, waits for them, and re-layouts  52.6 us
    dot_general x34, matrix products, dot_rows(): lax.dot_general(left, right, (((0,), (0,)), ((), ())), preferred_element_...  47.6 us
    pallas_call x1, Pallas kernels, gathered_weights(): pl.pallas_call(weights_body, out_shape=[jax.ShapeDtypeStruct((LAYERS, *co...  41.1 us
    pallas_call x1, Pallas kernels, returned_grads(): pl.pallas_call(functools.partial(grads_body, len(grads)), out_shape=[jax....  40.3 us
    dot_general x33, matrix products, dot_cols(): lax.dot_general(left, right, (((1,), (1,)), ((), ())), preferred_element_...  40.2 us
  transfers between devices with their start and end apart: 2, of which 0 were waited for; matrix products, arithmetic and copies ran while one was open for 9% of the time, Pallas kernels for 27%

profile of v1, /device:TPU:0, one launch (start us, length us, event | category | flops | bytes accessed | tf_op | source)
XLA Modules:
  0.0 852.4 jit_solution(1354551371952038861)
XLA Ops:
  16.3 28.6 %shard_map.484 = bf16[4,1584,128]{2,1,0:T(8,128)(2,1)} custom-call(bf16[1584,128]{1,0:T(8,128)(2,1)} %pad.60.block), custom_call_target="tpu_custom_call" | custom-call | tf_op jit(solution)/shard_map/pallas_call | solution.py:499
  56.0 37.8 %shard_map.485.x = f32[128,512]{1,0:T(8,128)S(1)} custom-call(bf16[32,128,512]{2,1,0:T(8,128)(2,1)S(1)} %bitcast.503), custom_call_target="tpu_custom_call" | custom-call | tf_op jit(solution)/shard_map/pallas_call | solution.py:73
  93.8 11.8 %shard_map.486 = bf16[8,128,512]{2,1,0:T(8,128)(2,1)S(1)} custom-call(f32[128,512]{1,0:T(8,128)S(1)} %shard_map.485.x), custom_call_target="tpu_custom_call" | custom-call | tf_op jit(solution)/shard_map/pallas_call | solution.py:73
  107.6 41.1 %shard_map.487 = (bf16[4,512,448]{2,1,0:T(8,128)(2,1)}, bf16[4,320,512]{2,1,0:T(8,128)(2,1)}) custom-call(bf16[512,448]{1,0:T(8,128)(2,1)} %bitcast.514, bf16[320,512]{1,0:T(8,128)(2,1)} %convert_bitcast_fusion.1.rows), custom_call_target="tpu_custom_call" | custom-call | tf_op jit(solution)/shard_map/pallas_call | solution.py:406
  183.4 20.2 %shard_map.488 = (bf16[8,128,512]{2,1,0:T(8,128)(2,1)S(1)}, f32[128,512]{1,0:T(8,128)S(1)}) custom-call(bf16[8,128,512]{2,1,0:T(8,128)(2,1)S(1)} %bitcast.508, f32[128,512]{1,0:T(8,128)S(1)} %shard_map.485.x, f32[8,512]{1,0:T(8,128)S(1)} %broadcast_in_dim.77.shift), custom_call_target="tpu_custom_call" | custom-call | tf_op jit(solution)/shard_map/pallas_call | solution.py:73
  214.0 21.5 %shard_map.489 = (bf16[8,128,512]{2,1,0:T(8,128)(2,1)S(1)}, f32[128,512]{1,0:T(8,128)S(1)}) custom-call(bf16[8,128,512]{2,1,0:T(8,128)(2,1)S(1)} %bitcast.506, f32[128,512]{1,0:T(8,128)S(1)} %get-tuple-element.63.x, f32[8,512]{1,0:T(8,128)S(1)} %broadcast_in_dim.78.shift), custom_call_target="tpu_custom_call" | custom-call | tf_op jit(solution)/shard_map/pallas_call | solution.py:73
  245.5 20.7 %shard_map.490 = (bf16[8,128,512]{2,1,0:T(8,128)(2,1)S(1)}, f32[128,512]{1,0:T(8,128)S(1)}) custom-call(bf16[8,128,512]{2,1,0:T(8,128)(2,1)S(1)} %bitcast.507, f32[128,512]{1,0:T(8,128)S(1)} %get-tuple-element.65.x, f32[8,512]{1,0:T(8,128)S(1)} %broadcast_in_dim.79.shift), custom_call_target="tpu_custom_call" | custom-call | tf_op jit(solution)/shard_map/pallas_call | solution.py:73
  275.9 11.9 %shard_map.491 = (f32[128,512]{1,0:T(8,128)S(1)}, bf16[128,512]{1,0:T(8,128)(2,1)S(1)}) custom-call(bf16[8,128,512]{2,1,0:T(8,128)(2,1)S(1)} %bitcast.505, f32[128,512]{1,0:T(8,128)S(1)} %get-tuple-element.67.x, f32[8,512]{1,0:T(8,128)S(1)} %broadcast_in_dim.80.shift, f32[8,512]{1,0:T(8,128)S(1)} %pad.61.gains), custom_call_target="tpu_custom_call" | custom-call | tf_op jit(solution)/shard_map/pallas_call | solution.py:73
  287.9 32.3 %shard_map.492 = bf16[32,128,512]{2,1,0:T(8,128)(2,1)S(1)} custom-call(bf16[128,512]{1,0:T(8,128)(2,1)S(1)} %get-tuple-element.69.block), custom_call_target="tpu_custom_call" | custom-call | tf_op jit(solution)/shard_map/pallas_call | solution.py:73
  326.7 14.1 %fusion.400 = (f32[4096]{0:T(1024)S(1)}, f32[4096,1572]{0,1:T(8,128)}) fusion(bf16[4096,512]{1,0:T(8,128)(2,1)} %bitcast.500, bf16[1,1572,512]{2,1,0:T(8,128)(2,1)} %all-gather.4.cloned.1.call-done), kind=kOutput, calls=%fused_computation.768 | convolution fusion | flops 6599880704 | bytes 31576064 | tf_op jit(solution)/shard_map/dot_general | solution.py:594
  340.8 12.1 %exponential_reduce_fusion = (f32[4096]{0:T(1024)S(1)}, f32[4096]{0:T(1024)S(1)}) fusion(f32[4096,1572]{0,1:T(8,128)} %get-tuple-element.411, f32[4096]{0:T(1024)S(1)} %get-tuple-element.410, s32[4096]{0:T(1024)S(1)} %bitcast.519), kind=kLoop, calls=%fused_computation.7 | loop fusion | flops 32186368 | bytes 25821184 | tf_op jit(solution)/shard_map/reduce_sum | solution.py:801
  353.1 16.8 %shard_map.493 = f32[32,8,128]{2,1,0:T(8,128)S(1)} custom-call(f32[32,8,128]{2,1,0:T(8,128)S(1)} %pad.62.stats), custom_call_target="tpu_custom_call" | custom-call | tf_op jit(solution)/shard_map/pallas_call | solution.py:73
  371.2 15.0 %convolution_convert_fusion = bf16[4096,512]{1,0:T(8,128)(2,1)S(1)} fusion(bf16[1,1572,512]{2,1,0:T(8,128)(2,1)} %all-gather.4.cloned.1.call-done, f32[4096,1572]{0,1:T(8,128)} %get-tuple-element.411, f32[4096]{0:T(1024)S(1)} %bitcast.535, f32[4096]{0:T(1024)S(1)} %bitcast.531, s32[4096]{0:T(1024)S(1)} %bitcast.520), kind=kOutput, calls=%fused_computation.14 | convolution fusion | flops 6634176512 | bytes 31608832 | tf_op jit(solution)/shard_map/dot_general | solution.py:600
  386.2 33.6 %shard_map.494 = f32[128,512]{1,0:T(8,128)S(1)} custom-call(bf16[32,128,512]{2,1,0:T(8,128)(2,1)S(1)} %bitcast.504), custom_call_target="tpu_custom_call" | custom-call | tf_op jit(solution)/shard_map/pallas_call | solution.py:73
  422.2 11.8 %shard_map.495 = bf16[8,128,512]{2,1,0:T(8,128)(2,1)S(1)} custom-call(f32[128,512]{1,0:T(8,128)S(1)} %get-tuple-element.283.grad), custom_call_target="tpu_custom_call" | custom-call | tf_op jit(solution)/shard_map/pallas_call | solution.py:73
  445.5 20.9 %shard_map.496 = (bf16[8,128,512]{2,1,0:T(8,128)(2,1)S(1)}, f32[128,512]{1,0:T(8,128)S(1)}) custom-call(bf16[8,128,512]{2,1,0:T(8,128)(2,1)S(1)} %bitcast.509, f32[128,512]{1,0:T(8,128)S(1)} %copy-done.15, f32[128,512]{1,0:T(8,128)S(1)} %get-tuple-element.283.grad), custom_call_target="tpu_custom_call" | custom-call | tf_op jit(solution)/shard_map/pallas_call | solution.py:73
  477.9 21.1 %shard_map.497 = (bf16[8,128,512]{2,1,0:T(8,128)(2,1)S(1)}, f32[128,512]{1,0:T(8,128)S(1)}) custom-call(bf16[8,128,512]{2,1,0:T(8,128)(2,1)S(1)} %bitcast.510, f32[128,512]{1,0:T(8,128)S(1)} %get-tuple-element.65.x, f32[128,512]{1,0:T(8,128)S(1)} %get-tuple-element.71.grad), custom_call_target="tpu_custom_call" | custom-call | tf_op jit(solution)/shard_map/pallas_call | solution.py:73
  510.5 21.1 %shard_map.498 = (bf16[8,128,512]{2,1,0:T(8,128)(2,1)S(1)}, f32[128,512]{1,0:T(8,128)S(1)}) custom-call(bf16[8,128,512]{2,1,0:T(8,128)(2,1)S(1)} %bitcast.511, f32[128,512]{1,0:T(8,128)S(1)} %copy-done.13, f32[128,512]{1,0:T(8,128)S(1)} %get-tuple-element.73.grad), custom_call_target="tpu_custom_call" | custom-call | tf_op jit(solution)/shard_map/pallas_call | solution.py:73
  576.5 40.3 %shard_map.499 = (bf16[4,512,448]{2,1,0:T(8,128)(2,1)}, bf16[4,320,512]{2,1,0:T(8,128)(2,1)}, f32[4,8,512]{2,1,0:T(8,128)}) custom-call(bf16[4,512,448]{2,1,0:T(8,128)(2,1)} %maximum_maximum_fusion.refs_0_, bf16[4,320,512]{2,1,0:T(8,128)(2,1)} %maximum_maximum_fusion.1.refs_1_, f32[4,8,512]{2,1,0:T(8,128)} %pad_maximum_fusion.28.refs_2_), custom_call_target="tpu_custom_call" | custom-call | tf_op jit(solution)/shard_map/pallas_call | solution.py:464
  618.9 14.8 %convolution_add_fusion = f32[1572,512]{1,0:T(8,128)S(1)} fusion(bf16[4096,512]{1,0:T(8,128)(2,1)} %bitcast.501, f32[1,1,1572,512]{3,1,2,0:T(1,128)} %get-tuple-element.295, f32[4096,1572]{0,1:T(8,128)} %get-tuple-element.411, f32[4096]{0:T(1024)S(1)} %bitcast.536, f32[4096]{0:T(1024)S(1)} %bitcast.532, s32[4096]{0:T(1024)S(1)} %bitcast.521), kind=kOutput, calls=%fused_computation.35 | convolution fusion | flops 6632884224 | bytes 36438016 | tf_op jit(solution)/shard_map/dot_general | solution.py:588
  633.7 13.7 %shard_map.500.block = bf16[128,512]{1,0:T(8,128)(2,1)S(1)} custom-call(bf16[8,128,512]{2,1,0:T(8,128)(2,1)S(1)} %bitcast.512, f32[128,512]{1,0:T(8,128)S(1)} %copy-done.7, f32[128,512]{1,0:T(8,128)S(1)} %get-tuple-element.75.grad), custom_call_target="tpu_custom_call" | custom-call | tf_op jit(solution)/shard_map/pallas_call | solution.py:73
  647.3 31.4 %shard_map.501 = bf16[32,128,512]{2,1,0:T(8,128)(2,1)S(1)} custom-call(bf16[128,512]{1,0:T(8,128)(2,1)S(1)} %shard_map.500.block), custom_call_target="tpu_custom_call" | custom-call | tf_op jit(solution)/shard_map/pallas_call | solution.py:73
  727.2 64.8 %psum.7 = f32[27,512]{1,0:T(8,128)S(1)} all-reduce(f32[27,512]{1,0:T(8,128)S(1)} %concatenate.242), channel_id=1, replica_groups=mesh['yl'=2,'co'=2,'yh'=2,'zz'=4,'xx'=4] {'yl','co','yh','zz','xx'}, use_global_device_ids=true, to_apply=%region_59.60 | all-reduce | flops 13824 | bytes 110592 | tf_op jit(solution)/shard_map/psum | solution.py:853
  822.5 13.3 %copy.210 = f32[1,2,1572,512]{3,1,2,0:T(2,128)} copy(f32[1,2,1572,512]{3,2,1,0:T(8,128)S(1)} %maximum_bitcast_fusion) | data formatting | bytes 12877824
  (826 shorter events, 259.7 us)
Async XLA Ops:
  8.0 683.9 %copy-start = (f32[1,448,8]{1,2,0:T(8,128)S(1)}, f32[1,448,8]{1,2,0:T(8,128)}, u32[]{:S(2)}) copy-start(f32[1,448,8]{1,2,0:T(8,128)} %param.56) | copy-start | bytes 43012
  8.0 159.4 %all-reduce.20.cloned.1.call-start = ((), (), s32[]{:S(2)}) async-start(), calls=%async_computation.1 | async-start | bytes 901120
  11.7 315.0 %all-gather.4.cloned.1.call-start = ((), (), s32[]{:S(2)}) async-start(), calls=%async_computation | async-start | bytes 2017280 | tf_op jit(solution)/shard_map/all_gather | solution.py:763
  56.0 49.7 %copy-start.50 = (f32[1,512,448]{1,2,0:T(8,128)S(1)}, f32[1,512,448]{1,2,0:T(8,128)}, u32[]{:S(2)}) copy-start(f32[1,512,448]{1,2,0:T(8,128)} %param.35) | copy-start | bytes 2752516
  93.8 89.5 %copy-start.6 = (f32[128,512]{1,0:T(8,128)}, f32[128,512]{1,0:T(8,128)S(1)}, u32[]{:S(2)}) copy-start(f32[128,512]{1,0:T(8,128)S(1)} %shard_map.485.x) | copy-start | bytes 786436
  105.7 65.0 %copy-start.1 = (bf16[8,128,512]{2,1,0:T(8,128)(2,1)}, bf16[8,128,512]{2,1,0:T(8,128)(2,1)S(1)}, u32[]{:S(2)}) copy-start(bf16[8,128,512]{2,1,0:T(8,128)(2,1)S(1)} %shard_map.486) | copy-start | bytes 3145732
  151.4 25.6 %copy-start.58 = (bf16[512,448]{1,0:T(8,128)(2,1)}, bf16[512,448]{1,0:T(8,128)(2,1)S(1)}, u32[]{:S(2)}) copy-start(bf16[512,448]{1,0:T(8,128)(2,1)S(1)} %get-tuple-element.311) | copy-start | bytes 1376260
  151.4 57.5 %copy-start.60 = (bf16[512,448]{1,0:T(8,128)(2,1)}, bf16[512,448]{1,0:T(8,128)(2,1)S(1)}, u32[]{:S(2)}) copy-start(bf16[512,448]{1,0:T(8,128)(2,1)S(1)} %get-tuple-element.310) | copy-start | bytes 1376260
  169.2 34.3 %copy-start.199 = (f32[1,1,512]{2,1,0:T(1,128)}, f32[1,1,512]{2,1,0:T(1,128)S(1)}, u32[]{:S(2)}) copy-start(f32[1,1,512]{2,1,0:T(1,128)S(1)} %get-tuple-element.347) | copy-start | bytes 6148
  169.2 34.3 %copy-start.201 = (f32[1,1,512]{2,1,0:T(1,128)}, f32[1,1,512]{2,1,0:T(1,128)S(1)}, u32[]{:S(2)}) copy-start(f32[1,1,512]{2,1,0:T(1,128)S(1)} %get-tuple-element.349) | copy-start | bytes 6148
  213.2 22.3 %copy-start.203 = (f32[1,1,512]{2,1,0:T(1,128)S(1)}, f32[1,1,512]{2,1,0:T(1,128)}, u32[]{:S(2)}) copy-start(f32[1,1,512]{2,1,0:T(1,128)} %get-tuple-element.343) | copy-start | bytes 6148
  213.2 22.3 %copy-start.205 = (f32[1,1,512]{2,1,0:T(1,128)S(1)}, f32[1,1,512]{2,1,0:T(1,128)}, u32[]{:S(2)}) copy-start(f32[1,1,512]{2,1,0:T(1,128)} %get-tuple-element.345) | copy-start | bytes 6148
  213.3 22.3 %copy-start.221 = (f32[1,1,512]{2,1,0:T(1,128)S(1)}, f32[1,1,512]{2,1,0:T(1,128)}, u32[]{:S(2)}) copy-start(f32[1,1,512]{2,1,0:T(1,128)} %get-tuple-element.342) | copy-start | bytes 6148
  213.3 22.3 %copy-start.222 = (f32[1,1,512]{2,1,0:T(1,128)S(1)}, f32[1,1,512]{2,1,0:T(1,128)}, u32[]{:S(2)}) copy-start(f32[1,1,512]{2,1,0:T(1,128)} %get-tuple-element.344) | copy-start | bytes 6148
  214.0 22.1 %copy-start.62 = (bf16[512,448]{1,0:T(8,128)(2,1)S(1)}, bf16[512,448]{1,0:T(8,128)(2,1)}, u32[]{:S(2)}) copy-start(bf16[512,448]{1,0:T(8,128)(2,1)} %get-tuple-element.309) | copy-start | bytes 1376260
  214.0 22.2 %copy-start.227 = (f32[1,1,192]{2,1,0:T(1,128)S(1)}, f32[1,1,192]{2,1,0:T(1,128)}, u32[]{:S(2)}) copy-start(f32[1,1,192]{2,1,0:T(1,128)} %get-tuple-element.371) | copy-start | bytes 2308
  287.9 37.7 %copy-start.214 = (f32[512]{0:T(512)S(1)}, f32[512]{0:T(512)}, u32[]{:S(2)}) copy-start(f32[512]{0:T(512)} %copy-done.213) | copy-start | bytes 6148
  287.9 37.7 %copy-start.216 = (f32[512]{0:T(512)S(1)}, f32[512]{0:T(512)}, u32[]{:S(2)}) copy-start(f32[512]{0:T(512)} %copy-done.215) | copy-start | bytes 6148
  287.9 38.2 %copy-start.212 = (f32[512]{0:T(512)S(1)}, f32[512]{0:T(512)}, u32[]{:S(2)}) copy-start(f32[512]{0:T(512)} %copy-done.211) | copy-start | bytes 6148
  287.9 38.2 %copy-start.218 = (f32[512]{0:T(512)S(1)}, f32[512]{0:T(512)}, u32[]{:S(2)}) copy-start(f32[512]{0:T(512)} %copy-done.217) | copy-start | bytes 6148
  340.8 29.6 %copy-start.248 = (f32[16]{0:T(128)S(1)}, f32[16]{0:T(128)}, u32[]{:S(2)}) copy-start(f32[16]{0:T(128)} %get-tuple-element.285) | copy-start | bytes 196
  633.6 45.1 %copy-start.17 = (f32[1572,512]{1,0:T(8,128)}, f32[1572,512]{1,0:T(8,128)S(1)}, u32[]{:S(2)}) copy-start(f32[1572,512]{1,0:T(8,128)S(1)} %convolution_add_fusion) | copy-start | bytes 9658372
  647.3 31.4 %copy-start.168 = (f32[2,1572,8]{1,2,0:T(8,128)S(1)}, f32[2,1572,8]{1,2,0:T(8,128)}, u32[]{:S(2)}) copy-start(f32[2,1572,8]{1,2,0:T(8,128)} %param.58) | copy-start | bytes 301828
  718.3 74.1 %copy-start.256 = (f32[2]{0:T(128)S(1)}, f32[2]{0:T(128)}, u32[]{:S(2)}) copy-start(f32[2]{0:T(128)} %constant.292) | copy-start | bytes 28
  (251 other events, 1220.7 us)
Sparse Core Ops, SparseCore 0:
  12.7 128.9 all-reduce.19
Sparse Core Ops, SparseCore 1:
  14.3 39.6 all-gather.3

commit v2 on v1

--- a/solution.py
+++ b/solution.py
@@ -150,35 +150,187 @@
 GATHER_SCRATCH = sem_pairs(3, 4)
 
 
-def first_body(x, everyone, a, b, c, d):
-    y, core, z = where_am_i()
-    greet(row_peers())
+def pair_peer():
+    return [{"co": 1 - lax.axis_index("co")}]
+
+
+def column_peers():
+    y, core, z = where_am_i()
+    return [{**at_chip(lax.rem(y + dy, 4), z), "co": c} for dy in FAR for c in (0, 1)]
+
+
+def home_and_layer():
+    y, core, z = where_am_i()
+    return y // 2 == core, lax.rem(y, 2) * 2 + core
+
+
+def take_copies(sources, places, sems, dy):
+    y, core, z = where_am_i()
+    return [
+        pltpu.make_async_remote_copy(
+            src_ref=src,
+            dst_ref=dst,
+            send_sem=sems[2 * n].at[dy],
+            recv_sem=sems[2 * n + 1].at[0],
+            device_id={**at_chip(lax.rem(y + dy, 4), z), "co": y // 2},
+            device_id_type=MESH_ID,
+        )
+        for n, (src, dst) in enumerate(zip(sources, places))
+    ]
+
+
+def take_local(sources, places, sems):
+    return [
+        pltpu.make_async_copy(src, dst, sems[2 * n + 1].at[0])
+        for n, (src, dst) in enumerate(zip(sources, places))
+    ]
+
+
+def take_start(layer, sources, places, sems):
+    home, own = home_and_layer()
+
+    @pl.when(own == layer)
+    def _():
+        for dy in FAR:
+            for copy in take_copies(sources, places, sems, dy):
+                copy.start()
+
+    @pl.when(jnp.logical_and(own == layer, home))
+    def _():
+        for copy in take_local(sources, places, sems):
+            copy.start()
+
+    @pl.when(jnp.logical_and(own == layer, jnp.logical_not(home)))
+    def _():
+        for copy in take_copies(sources, places, sems, 0):
+            copy.start()
+
+
+def take_finish(layer, sources, places, sems):
+    home, own = home_and_layer()
+
+    @pl.when(own == layer)
+    def _():
+        for dy in FAR:
+            for copy in take_copies(sources, places, sems, dy):
+                copy.wait_send()
+
+    @pl.when(jnp.logical_and(own == layer, jnp.logical_not(home)))
+    def _():
+        for copy in take_copies(sources, places, sems, 0):
+            copy.wait_send()
+
+    for copy in take_local(sources, places, sems):
+        copy.wait()
+
+
+def take_scratch(count):
+    return [pltpu.SemaphoreType.DMA((n,)) for _ in range(count) for n in (4, 1)]
+
+
+def give_copies(layer, sources, landed, sems):
+    y, core, z = where_am_i()
+    return [
+        pltpu.make_async_remote_copy(
+            src_ref=src,
+            dst_ref=dst.at[y],
+            send_sem=sems[2 * n].at[0],
+            recv_sem=sems[2 * n + 1].at[y],
+            device_id={**at_chip(core * 2 + layer // 2, z), "co": layer % 2},
+            device_id_type=MESH_ID,
+        )
+        for n, (src, dst) in enumerate(zip(sources, landed))
+    ]
+
+
+def give_start(layer, sources, landed, sems):
+    y, core, z = where_am_i()
+    home, own = home_and_layer()
+    local = jnp.logical_and(home, own == layer)
+
+    @pl.when(jnp.logical_not(local))
+    def _():
+        for copy in give_copies(layer, sources, landed, sems):
+            copy.start()
+
+    @pl.when(local)
+    def _():
+        for n, (src, dst) in enumerate(zip(sources, landed)):
+            pltpu.make_async_copy(src, dst.at[y], sems[2 * n + 1].at[y]).start()
+
+
+def give_finish(layer, sources, landed, sums, sems):
+    home, own = home_and_layer()
+
+    @pl.when(own == layer)
+    def _():
+        for n, (src, dst) in enumerate(zip(sources, landed)):
+            for index in range(4):
+                pltpu.make_async_copy(src, dst.at[index], sems[2 * n + 1].at[index]).wait()
+            total = dst[0].astype(F32)
+            for index in range(1, 4):
+                total = total + dst[index].astype(F32)
+            sums[n][...] = total
+
+    @pl.when(jnp.logical_not(jnp.logical_and(home, own == layer)))
+    def _():
+        for copy in give_copies(layer, sources, landed, sems):
+            copy.wait_send()
+
+
+def give_scratch(grads):
+    return [pltpu.VMEM((4, *g.shape), g.dtype) for g in grads] + [
+        pltpu.SemaphoreType.DMA((n,)) for _ in grads for n in (1, 4)
+    ]
+
+
+def first_body(layer, x, *refs):
+    sources, everyone, places, sems = refs[:3], refs[3], refs[4:7], refs[7:]
+    y, core, z = where_am_i()
+    greet(row_peers() + column_peers())
     everyone[core * 4 + z] = normed_rows(x[...])[0].astype(BF)
-    row_gather(everyone, (a, b), (c, d))
-
-
-def first_hat(x):
+    take_start(layer, sources, places, sems[4:])
+    row_gather(everyone, sems[:2], sems[2:4])
+    take_finish(layer, sources, places, sems[4:])
+
+
+def first_hat(layer, x, sources):
     return kernel_call(
-        first_body, jax.ShapeDtypeStruct((8, BLOCK, D), BF), (x,), GATHER_SCRATCH, 1
-    )
-
-
-def forward_body(part, x, shift, everyone, x_new, r1, s, r2, e, f, g, h, a, b, c, d):
-    y, core, z = where_am_i()
-    greet(row_peers())
+        functools.partial(first_body, layer),
+        [jax.ShapeDtypeStruct((8, BLOCK, D), BF)]
+        + [jax.ShapeDtypeStruct(a.shape, a.dtype) for a in sources],
+        (x, *sources),
+        GATHER_SCRATCH + take_scratch(3),
+        1,
+    )
+
+
+def forward_body(layer, part, x, shift, *refs):
+    sources, refs = (refs[:3], refs[3:]) if layer is not None else ((), refs)
+    everyone, x_new, refs = refs[0], refs[1], refs[2:]
+    places, refs = (refs[:3], refs[3:]) if layer is not None else ((), refs)
+    r1, s, r2, e, f, g, h, a, b, c, d = refs[:11]
+    sems = refs[11:]
+    y, core, z = where_am_i()
+    greet(row_peers() + (column_peers() if layer is not None else []))
+    if layer is not None:
+        take_start(layer, sources, places, sems)
     after = x[...] + row_sum(part, r1, s, r2, (e, f), (g, h)) + shift[0:1]
     x_new[...] = after
     everyone[core * 4 + z] = normed_rows(after)[0].astype(BF)
     row_gather(everyone, (a, b), (c, d))
-
-
-def next_hat(part, x, shift):
+    if layer is not None:
+        take_finish(layer, sources, places, sems)
+
+
+def next_hat(part, x, shift, layer=None, sources=()):
     return kernel_call(
-        forward_body,
-        [jax.ShapeDtypeStruct((8, BLOCK, D), BF), jax.ShapeDtypeStruct((BLOCK, D), F32)],
-        (part, x, shift),
-        SUM_SCRATCH + GATHER_SCRATCH,
-        2,
+        functools.partial(forward_body, layer),
+        [jax.ShapeDtypeStruct((8, BLOCK, D), BF), jax.ShapeDtypeStruct((BLOCK, D), F32)]
+        + [jax.ShapeDtypeStruct(a.shape, a.dtype) for a in sources],
+        (part, x, shift, *sources),
+        SUM_SCRATCH + GATHER_SCRATCH + take_scratch(len(sources)),
+        10 + (layer or 0),
     )
 
 
@@ -212,34 +364,49 @@
     )
 
 
-def backward_body(part, x, grad, everyone, g_new, r1, s, r2, e, f, g, h, a, b, c, d):
-    y, core, z = where_am_i()
-    greet(row_peers())
+def backward_body(layer, part, x, grad, *refs):
+    sources, everyone, g_new, sums, landed = refs[:3], refs[3], refs[4], refs[5:8], refs[8:11]
+    give_sems = refs[11:17]
+    r1, s, r2, e, f, g, h, a, b, c, d = refs[17:]
+    y, core, z = where_am_i()
+    greet(row_peers() + column_peers())
+    give_start(layer, sources, landed, give_sems)
     after = grad[...] + norm_back(x[...], row_sum(part, r1, s, r2, (e, f), (g, h)))
     g_new[...] = after
     everyone[core * 4 + z] = after.astype(BF)
     row_gather(everyone, (a, b), (c, d))
-
-
-def next_grad(part, x, grad):
+    give_finish(layer, sources, landed, sums, give_sems)
+
+
+def next_grad(layer, part, x, grad, sources):
     return kernel_call(
-        backward_body,
-        [jax.ShapeDtypeStruct((8, BLOCK, D), BF), jax.ShapeDtypeStruct((BLOCK, D), F32)],
-        (part, x, grad),
-        SUM_SCRATCH + GATHER_SCRATCH,
-        5,
-    )
-
-
-def lowest_body(part, x, grad, low, r1, s, r2, e, f, g, h):
-    greet(row_peers())
+        functools.partial(backward_body, layer),
+        [jax.ShapeDtypeStruct((8, BLOCK, D), BF), jax.ShapeDtypeStruct((BLOCK, D), F32)]
+        + [jax.ShapeDtypeStruct(a.shape, F32) for a in sources],
+        (part, x, grad, *sources),
+        give_scratch(sources) + SUM_SCRATCH + GATHER_SCRATCH,
+        20 + layer,
+    )
+
+
+def lowest_body(layer, part, x, grad, *refs):
+    sources, low, sums, landed, give_sems = refs[:3], refs[3], refs[4:7], refs[7:10], refs[10:16]
+    r1, s, r2, e, f, g, h = refs[16:]
+    greet(row_peers() + column_peers())
+    give_start(layer, sources, landed, give_sems)
     after = grad[...] + norm_back(x[...], row_sum(part, r1, s, r2, (e, f), (g, h)))
     low[...] = after.astype(BF)
-
-
-def lowest_grad(part, x, grad):
+    give_finish(layer, sources, landed, sums, give_sems)
+
+
+def lowest_grad(layer, part, x, grad, sources):
     return kernel_call(
-        lowest_body, jax.ShapeDtypeStruct((BLOCK, D), BF), (part, x, grad), SUM_SCRATCH, 6
+        functools.partial(lowest_body, layer),
+        [jax.ShapeDtypeStruct((BLOCK, D), BF)]
+        + [jax.ShapeDtypeStruct(a.shape, F32) for a in sources],
+        (part, x, grad, *sources),
+        give_scratch(sources) + SUM_SCRATCH,
+        6,
     )
 
 
@@ -356,121 +523,6 @@
     )
 
 
-def column_peers():
-    y, core, z = where_am_i()
-    return [{"co": 1 - core}] + [
-        {**at_chip(lax.rem(y + dy, 4), z), "co": c} for dy in FAR for c in (0, 1)
-    ]
-
-
-def weights_body(cols, rows, all_cols, all_rows, a, b, c, d):
-    y, core, z = where_am_i()
-    greet(column_peers())
-    layer = lax.rem(y, 2) * 2 + core
-    home = y // 2 == core
-    pairs = ((cols, all_cols, a, b), (rows, all_rows, c, d))
-
-    def out_copy(src, dst, s, r, dy):
-        return pltpu.make_async_remote_copy(
-            src_ref=src,
-            dst_ref=dst.at[layer],
-            send_sem=s.at[dy],
-            recv_sem=r.at[layer],
-            device_id={**at_chip(lax.rem(y + dy, 4), z), "co": y // 2},
-            device_id_type=MESH_ID,
-        )
-
-    for dy in FAR:
-        for src, dst, s, r in pairs:
-            out_copy(src, dst, s, r, dy).start()
-    for src, dst, s, r in pairs:
-
-        @pl.when(home)
-        def _():
-            pltpu.make_async_copy(src, dst.at[layer], r.at[layer]).start()
-
-        @pl.when(jnp.logical_not(home))
-        def _():
-            out_copy(src, dst, s, r, 0).start()
-            out_copy(src, dst, s, r, 0).wait_send()
-
-    for dy in FAR:
-        for src, dst, s, r in pairs:
-            out_copy(src, dst, s, r, dy).wait_send()
-    for index in range(LAYERS):
-        for src, dst, s, r in pairs:
-            pltpu.make_async_copy(src, dst.at[index], r.at[index]).wait()
-
-
-def gathered_weights(cols, rows):
-    return pl.pallas_call(
-        weights_body,
-        out_shape=[
-            jax.ShapeDtypeStruct((LAYERS, *cols.shape), BF),
-            jax.ShapeDtypeStruct((LAYERS, *rows.shape), BF),
-        ],
-        in_specs=[pl.BlockSpec(memory_space=pl.ANY)] * 2,
-        out_specs=[pl.BlockSpec(memory_space=pl.ANY)] * 2,
-        scratch_shapes=sem_pairs(4, 4),
-        compiler_params=pltpu.CompilerParams(collective_id=10, has_side_effects=True),
-    )(cols, rows)
-
-
-def grads_body(count, *refs):
-    sources, landed, sems = refs[:count], refs[count : 2 * count], refs[2 * count :]
-    y, core, z = where_am_i()
-    greet(column_peers())
-    own_layer = lax.rem(y, 2) * 2 + core
-    home = y // 2 == core
-
-    def out_copy(n, layer):
-        return pltpu.make_async_remote_copy(
-            src_ref=sources[n].at[layer],
-            dst_ref=landed[n].at[y],
-            send_sem=sems[2 * n].at[layer],
-            recv_sem=sems[2 * n + 1].at[y],
-            device_id={**at_chip(core * 2 + layer // 2, z), "co": layer % 2},
-            device_id_type=MESH_ID,
-        )
-
-    def both(layer, act):
-        local = jnp.logical_and(home, own_layer == layer)
-        for n in range(count):
-
-            @pl.when(jnp.logical_not(local))
-            def _():
-                act(out_copy(n, layer))
-
-    for layer in range(LAYERS):
-        both(layer, lambda copy: copy.start())
-    for n in range(count):
-
-        @pl.when(home)
-        def _():
-            pltpu.make_async_copy(
-                sources[n].at[own_layer], landed[n].at[y], sems[2 * n + 1].at[y]
-            ).start()
-
-    for layer in range(LAYERS):
-        both(layer, lambda copy: copy.wait_send())
-    for index in range(4):
-        for n in range(count):
-            pltpu.make_async_copy(
-                sources[n].at[0], landed[n].at[index], sems[2 * n + 1].at[index]
-            ).wait()
-
-
-def returned_grads(*grads):
-    return pl.pallas_call(
-        functools.partial(grads_body, len(grads)),
-        out_shape=[jax.ShapeDtypeStruct(g.shape, g.dtype) for g in grads],
-        in_specs=[pl.BlockSpec(memory_space=pl.ANY)] * len(grads),
-        out_specs=[pl.BlockSpec(memory_space=pl.ANY)] * len(grads),
-        scratch_shapes=sem_pairs(*[4] * len(grads)),
-        compiler_params=pltpu.CompilerParams(collective_id=11, has_side_effects=True),
-    )(*grads)
-
-
 def replicas_peers():
     x = lax.axis_index("xx")
     return [(lax.rem(x + k, 4), {"xx": lax.rem(x + k, 4)}) for k in FAR]
@@ -485,87 +537,276 @@
     return copies
 
 
-def features_body(block, everyone, a, b, own_sem):
-    greet([device for _, device in replicas_peers()])
-    copies = replicas_exchange(block, everyone, a, b)
+def features_body(layers, count, block, *refs):
+    sources, everyone = refs[:count], refs[count]
+    places, sems = refs[count + 1 : -1], refs[-1 - 2 - 2 * count * len(layers) : -1]
+    places = places[: count * len(layers)]
+    own_sem = refs[-1]
+    greet([device for _, device in replicas_peers()] + pair_peer() + column_peers())
+    copies = replicas_exchange(block, everyone, *sems[:2])
     own = pltpu.make_async_copy(block, everyone.at[lax.axis_index("xx")], own_sem)
     own.start()
+    parts = [
+        (layer, sources, places[count * n : count * (n + 1)],
+         sems[2 + 2 * count * n : 2 + 2 * count * (n + 1)])
+        for n, layer in enumerate(layers)
+    ]
+    for part in parts:
+        take_start(*part)
     own.wait()
     for copy in copies:
         copy.wait()
-
-
-def all_features(block):
+    for part in parts:
+        take_finish(*part)
+
+
+def all_features(block, layers, sources):
+    count = len(sources)
     return pl.pallas_call(
-        features_body,
-        out_shape=jax.ShapeDtypeStruct((4, *block.shape), block.dtype),
-        in_specs=[pl.BlockSpec(memory_space=pl.ANY)],
-        out_specs=pl.BlockSpec(memory_space=pl.ANY),
-        scratch_shapes=sem_pairs(3) + [pltpu.SemaphoreType.DMA],
-        compiler_params=pltpu.CompilerParams(collective_id=12, has_side_effects=True),
-    )(block)
-
-
-def left_body(left, extra, basis, extra_sum, came, came_extra, work, a, b, c, d):
+        functools.partial(features_body, layers, count),
+        out_shape=[jax.ShapeDtypeStruct((4, *block.shape), block.dtype)]
+        + [jax.ShapeDtypeStruct(a.shape, a.dtype) for _ in layers for a in sources],
+        in_specs=[pl.BlockSpec(memory_space=pl.ANY)] * (1 + count),
+        out_specs=[pl.BlockSpec(memory_space=pl.ANY)] * (1 + count * len(layers)),
+        scratch_shapes=sem_pairs(3)
+        + take_scratch(count * len(layers))
+        + [pltpu.SemaphoreType.DMA],
+        compiler_params=pltpu.CompilerParams(collective_id=31, has_side_effects=True),
+    )(block, *sources)
+
+
+CHUNK = 128
+TILES = D // 128
+
+
+def exact_dot(left, right, contract):
+    return lax.dot_general(
+        left, right, (contract, ((), ())), preferred_element_type=F32, precision=HIGH
+    )
+
+
+def factor_places(cols, rows, vocab):
+    def up(n):
+        return -(-n // 128) * 128
+
+    half = max(up(cols) + up(vocab), up(rows) + up(vocab))
+    return half, ((0, 0, cols), (1, 0, rows), (0, up(cols), vocab), (1, up(rows), vocab))
+
+
+def compress_body(
+    vocab, g_embed, g_head, err, m_in, m_back, q_in, q_back, q_embed, q_head, bias, vectors,
+    m_embed, m_head, basis, own, sums, bias_sum, vector_sum,
+    left, left_came, bias_came, joint, joint_came, work, vec_came, vec_mine, vec_sums, vec_all,
+    *sems,
+):
+    y, core, z = where_am_i()
     x = lax.axis_index("xx")
-    greet([device for _, device in replicas_peers()])
-    copies = replicas_exchange(left, came, a, b) + replicas_exchange(extra, came_extra, c, d)
-    came[x] = left[...]
-    came_extra[x] = extra[...]
-    for copy in copies:
+    me = y * 8 + core * 4 + z
+    peers = []
+    for k in range(1, 32):
+        p = lax.rem(me + k, 32)
+        peers.append((p, {**at_chip(p // 8, lax.rem(p, 4)), "co": lax.rem(p // 4, 2)}))
+    greet([device for _, device in peers] + [device for _, device in replicas_peers()])
+    pairs = [(sems[2 * n], sems[2 * n + 1]) for n in range(len(sems) // 2)]
+    vec_first = [
+        send(vectors.at[p], vec_came.at[me], pairs[0], k, device)
+        for k, (p, device) in enumerate(peers)
+    ]
+    vec_came[me] = vectors[me]
+
+    half, places = factor_places(m_in.shape[1], m_back.shape[0], vocab)
+    chunks = m_embed.shape[0] // CHUNK
+    whole = vocab // CHUNK
+    left[...] = jnp.zeros(left.shape, F32)
+
+    def add_rows(start, count):
+        for b, (grad, out) in enumerate(((g_embed, m_embed), (g_head, m_head))):
+            for tile in range(TILES):
+                place = (pl.ds(start, count), pl.ds(tile * 128, 128))
+                far = pl.ds(start * (2 * TILES) + 2 * tile + b, count, stride=2 * TILES)
+                out[place] = grad[place] + err[far, :]
+
+    @pl.loop(0, whole)
+    def _(c):
+        add_rows(pl.multiple_of(c * CHUNK, CHUNK), CHUNK)
+
+    m_embed[pl.ds(whole * CHUNK, (chunks - whole) * CHUNK), :] = jnp.zeros(
+        ((chunks - whole) * CHUNK, D), F32
+    )
+    m_head[pl.ds(whole * CHUNK, (chunks - whole) * CHUNK), :] = jnp.zeros(
+        ((chunks - whole) * CHUNK, D), F32
+    )
+    add_rows(whole * CHUNK, vocab - whole * CHUNK)
+    left[0] = exact_dot(q_in[...], m_in[...], ((1,), (1,)))
+    left[1] = exact_dot(q_back[...], m_back[...], ((1,), (0,)))
+
+    @pl.loop(0, chunks)
+    def _(c):
+        rows = pl.ds(pl.multiple_of(c * CHUNK, CHUNK), CHUNK)
+        left[2] += exact_dot(q_embed[:, rows], m_embed[rows, :], ((1,), (0,)))
+        left[3] += exact_dot(q_head[:, rows], m_head[rows, :], ((1,), (0,)))
+
+    for copy in vec_first:
+        copy.wait_recv()
+    vec_mine[...] = jnp.sum(vec_came[...], 0)
+    second = []
+    for n, (src, dst) in enumerate(
+        ((left, left_came), (bias, bias_came), (vec_mine, vec_sums))
+    ):
+        second += replicas_exchange(src, dst, *pairs[1 + n])
+    left_came[x] = left[...]
+    bias_came[x] = bias[...]
+    vec_sums[x] = vec_mine[...]
+    for copy in second:
         copy.wait()
-    extra_sum[...] = jnp.sum(came_extra[...], 0)
-    work[...] = jnp.sum(came[...], 0)
-    rows = lax.broadcasted_iota(jnp.int32, (1, RANK, 1), 1)
+    bias_sum[...] = jnp.sum(bias_came[...], 0)
+    vec_all[me] = jnp.sum(vec_sums[...], 0)
+    mine = vec_all.at[me]
+    third = [send(mine, mine, pairs[4], k, device) for k, (_, device) in enumerate(peers)]
+    work[...] = jnp.sum(left_came[...], 0)
+    order = lax.broadcasted_iota(jnp.int32, (1, RANK, 1), 1)
     for index in range(RANK):
         columns = work[...]
         one = columns[:, index : index + 1, :]
         one = one * lax.rsqrt(jnp.sum(one * one, -1, keepdims=True) + 1e-30)
         shares = jnp.sum(columns * one, -1, keepdims=True)
-        work[...] = jnp.where(rows > index, columns - shares * one, columns)
+        work[...] = jnp.where(order > index, columns - shares * one, columns)
         basis[:, index : index + 1, :] = one
 
-
-def orthonormal_sum(left, extra):
+    own[...] = jnp.zeros(own.shape, F32)
+    own[0, :, pl.ds(places[0][1], places[0][2])] = exact_dot(basis[0], m_in[...], ((1,), (0,)))
+    own[1, :, pl.ds(places[1][1], places[1][2])] = exact_dot(basis[1], m_back[...], ((1,), (1,)))
+
+    @pl.loop(0, chunks)
+    def _(c):
+        start = pl.multiple_of(c * CHUNK, CHUNK)
+        for b, matrix in ((2, m_embed), (3, m_head)):
+            at = pl.ds(pl.multiple_of(places[b][1] + start, 128), CHUNK)
+            own[places[b][0], :, at] = exact_dot(
+                basis[b], matrix[pl.ds(start, CHUNK), :], ((1,), (1,))
+            )
+
+    joint[...] = own[...].reshape(joint.shape).astype(BF)
+    fourth = replicas_exchange(joint, joint_came, *pairs[5])
+    joint_came[x] = joint[...]
+    for copy in fourth:
+        copy.wait()
+    total = jnp.sum(joint_came[...].astype(F32), 0)
+    sums[...] = total.reshape(sums.shape)
+    for copy in vec_first:
+        copy.wait_send()
+    for copy in third:
+        copy.wait()
+    vector_sum[...] = vec_all[...]
+
+
+def compressed(vocab, g_embed, g_head, err, m_in, m_back, facs, bias, vectors):
+    half, _ = factor_places(m_in.shape[1], m_back.shape[0], vocab)
+    tall = g_embed.shape
     return kernel_call(
-        left_body,
+        functools.partial(compress_body, vocab),
         [
-            jax.ShapeDtypeStruct(left.shape, F32),
-            jax.ShapeDtypeStruct(extra.shape, F32),
+            jax.ShapeDtypeStruct(s, F32)
+            for s in (tall, tall, (4, 8, D), (2, 8, half), (2, 8, half), bias.shape, vectors.shape)
         ],
-        (left, extra),
+        (g_embed, g_head, err, m_in, m_back, *facs, bias, vectors),
         [
-            pltpu.VMEM((4, *left.shape), F32),
-            pltpu.VMEM((4, *extra.shape), F32),
-            pltpu.VMEM(left.shape, F32),
+            pltpu.VMEM((4, 8, D), F32),
+            pltpu.VMEM((4, 4, 8, D), F32),
+            pltpu.VMEM((4, *bias.shape), F32),
+            pltpu.VMEM((16, half), BF),
+            pltpu.VMEM((4, 16, half), BF),
+            pltpu.VMEM((4, 8, D), F32),
+            pltpu.VMEM(vectors.shape, F32),
+            pltpu.VMEM(vectors.shape[1:], F32),
+            pltpu.VMEM((4, *vectors.shape[1:]), F32),
+            pltpu.VMEM(vectors.shape, F32),
         ]
-        + sem_pairs(3, 3),
-        13,
-    )
-
-
-def right_body(right, total, came, a, b):
-    x = lax.axis_index("xx")
-    greet([device for _, device in replicas_peers()])
-    copies = replicas_exchange(right, came, a, b)
-    came[x] = right[...]
-    for copy in copies:
-        copy.wait()
-    total[...] = jnp.sum(came[...].astype(F32), 0)
-
-
-def right_sum(right):
-    return kernel_call(
-        right_body,
-        jax.ShapeDtypeStruct(right.shape, F32),
-        (right,),
-        [pltpu.VMEM((4, *right.shape), BF)] + sem_pairs(3),
-        14,
+        + sem_pairs(31, 3, 3, 3, 31, 3),
+        30,
+        56,
     )
 
 
 def ema_decay():
     return min(0.999, (1.0 + STEP) / (10.0 + STEP))
+
+
+def stepped(rate, weight, moment, average, grad):
+    decay = ema_decay()
+    new_moment = MOMENTUM * moment + (1.0 - MOMENTUM) * grad
+    new_weight = weight - rate * new_moment
+    return new_weight, new_moment, decay * average + (1.0 - decay) * new_weight
+
+
+def update_body(
+    vocab, rate_layer, rate_tables, m_embed, m_head, m_in, m_back, basis, own, sums,
+    in_w, in_m, in_e, back_w, back_m, back_e, tab_w, tab_m, tab_e,
+    err_tab, err_in, err_back, o_in_w, o_in_m, o_in_e, o_back_w, o_back_m, o_back_e,
+    o_tab_w, o_tab_m, o_tab_e,
+):
+    x = lax.axis_index("xx")
+    half, places = factor_places(m_in.shape[1], m_back.shape[0], vocab)
+    whole = vocab // CHUNK
+    own_cols = pl.ds(pl.multiple_of(x * 128, 128), 128)
+
+    def part(ref, b, start, count):
+        return ref[places[b][0], :, pl.ds(pl.multiple_of(places[b][1] + start, 128), count)]
+
+    def table_rows(start, count):
+        for b, matrix in ((2, m_embed), (3, m_head)):
+            span = CHUNK
+            product = exact_dot(part(own, b, start, span), basis[b], ((0,), (0,)))
+            for tile in range(TILES):
+                far = pl.ds(start * (2 * TILES) + 2 * tile + b - 2, count, stride=2 * TILES)
+                err_tab[far, :] = (
+                    matrix[pl.ds(start, count), pl.ds(tile * 128, 128)]
+                    - product[:count, tile * 128 : (tile + 1) * 128]
+                )
+            reduced = exact_dot(part(sums, b, start, span), basis[b, :, own_cols], ((0,), (0,)))
+            near = pl.ds(start * 2 + b - 2, count, stride=2)
+            new = stepped(
+                rate_tables[b - 2], tab_w[near, :], tab_m[near, :], tab_e[near, :], reduced[:count]
+            )
+            for out, value in zip((o_tab_w, o_tab_m, o_tab_e), new):
+                out[near, :] = value
+
+    @pl.loop(0, whole)
+    def _(c):
+        table_rows(pl.multiple_of(c * CHUNK, CHUNK), CHUNK)
+
+    if vocab > whole * CHUNK:
+        table_rows(whole * CHUNK, vocab - whole * CHUNK)
+
+    cols, rows = places[0][2], places[1][2]
+
+    @pl.loop(0, D // CHUNK)
+    def _(c):
+        at = pl.ds(pl.multiple_of(c * CHUNK, CHUNK), CHUNK)
+        left = basis[0, :, at]
+        err_in[at, :] = m_in[at, :] - exact_dot(left, part(own, 0, 0, cols), ((0,), (0,)))
+        reduced = exact_dot(left, part(sums, 0, 0, cols), ((0,), (0,)))
+        new = stepped(rate_layer, in_w[at, :], in_m[at, :], in_e[at, :], reduced)
+        for out, value in zip((o_in_w, o_in_m, o_in_e), new):
+            out[at, :] = value
+
+    err_back[...] = m_back[...] - exact_dot(part(own, 1, 0, rows), basis[1], ((0,), (0,)))
+    reduced = exact_dot(part(sums, 1, 0, rows), basis[1], ((0,), (0,)))
+    new = stepped(rate_layer, back_w[...], back_m[...], back_e[...], reduced)
+    for out, value in zip((o_back_w, o_back_m, o_back_e), new):
+        out[...] = value
+
+
+def updated(vocab, rates, m_tables, m_in, m_back, basis, own, sums, params, err):
+    outs = [err, m_in, m_back] + list(params)
+    return kernel_call(
+        functools.partial(update_body, vocab, rates[0], rates[1]),
+        [jax.ShapeDtypeStruct(a.shape, F32) for a in outs],
+        (*m_tables, m_in, m_back, basis, own, sums, *params),
+        [],
+        None,
+        56,
+    )
 
 
 def rotary_tables():
@@ -695,13 +936,6 @@
     )
     grad_hat = grad_first * vector[0] + grad_second * vector[2]
     return (grad_hat.astype(BF), (grad_cols.astype(BF), grad_rows.astype(BF), grad_bias, grad_norms))
-
-
-def momentum_step(weight, moment, average, grad, rate):
-    decay = ema_decay()
-    new_moment = MOMENTUM * moment + (1.0 - MOMENTUM) * grad
-    new_weight = weight - rate * new_moment
-    return (new_weight, new_moment, decay * average + (1.0 - decay) * new_weight)
 
 
 def on_device(
@@ -758,41 +992,39 @@
 
     short = tables.astype(BF)
     spare = -vocab_shard % 16
-    embed_low = all_features(jnp.pad(short[0], ((0, spare), (0, 0))))
+    small = jnp.concatenate(
+        [
+            jnp.pad(vecs[0], ((0, 2), (0, 0))),
+            jnp.pad(b_in, ((0, 7), (0, D - b_in.shape[1]))),
+        ]
+    )
+    sources = (w_in[0].astype(BF), w_back[0].astype(BF), small)
+    embed_low, *taken = all_features(jnp.pad(short[0], ((0, spare), (0, 0))), (0,), sources)
+    packs = {0: taken}
     embed_low = jnp.transpose(embed_low, (1, 0, 2)).reshape(vocab_shard + spare, D)
     head_low = lax.all_gather(short[1], "xx", axis=1, tiled=True)
-    all_cols, all_rows = gathered_weights(w_in[0].astype(BF), w_back[0].astype(BF))
-    small = jnp.concatenate([vecs[0].reshape(-1), b_in[0]])
-    small = lax.all_gather(small, ("yl", "co", "yh", "zz"), axis=0, tiled=False)
-    small = small.reshape(LAYERS, 8, -1)
-    all_vecs = small[:, 0, : 6 * D].reshape(LAYERS, 6, D)
-    all_bias = lax.dynamic_index_in_dim(small[:, :, 6 * D :], shard, 1, False)
 
     vocab_ids = jnp.arange(vocab_shard + spare, dtype=jnp.int32)
     looked = dot_plain((local_ids[:, None] == vocab_ids[None, :]).astype(BF), embed_low)
     x = plane_sum(looked.astype(BF).reshape(32, BLOCK, D))
-    hat = first_hat(x).reshape(LENGTH, D)
-
-    weights = [
-        (all_cols[index], all_rows[index], all_bias[index], all_vecs[index])
-        for index in range(LAYERS)
-    ]
-    shifts = [
-        jnp.broadcast_to((all_vecs[index, 4] + all_vecs[index, 5])[None], (8, D))
-        for index in range(LAYERS)
-    ]
+    hat, *packs[1] = first_hat(1, x, sources)
+
     gains = jnp.pad(final_norm, ((0, 6), (0, 0)))
-    kept, before = [], []
+    weights, kept, before = [], [], []
     for index in range(LAYERS):
+        cols, rows, rest = packs[index]
+        weights.append((cols, rows, rest[8, : cols.shape[1]], rest))
+        shift = jnp.broadcast_to((rest[4] + rest[5])[None], (8, D))
         before.append(x)
-        branch, keep = block_forward(hat, weights[index], cosine, sine)
+        branch, keep = block_forward(hat.reshape(LENGTH, D), weights[index], cosine, sine)
         kept.append(keep)
         branch = branch.reshape(8, BLOCK, D)
-        if index + 1 < LAYERS:
-            hat, x = next_hat(branch, x, shifts[index])
-            hat = hat.reshape(LENGTH, D)
+        if index + 2 < LAYERS:
+            hat, x, *packs[index + 2] = next_hat(branch, x, shift, index + 2, sources)
+        elif index + 1 < LAYERS:
+            hat, x = next_hat(branch, x, shift)
         else:
-            x, normed_own = last_normed(branch, x, shifts[index], gains)
+            x, normed_own = last_normed(branch, x, shift, gains)
 
     normed = plane_gather(normed_own).reshape(row_total, D)
     logits = dot_cols(normed, head_low)
@@ -817,100 +1049,90 @@
     grad_gains = jnp.stack([jnp.sum(grad_normed * hat_own, 0), jnp.sum(grad_normed, 0)])
     grad = norm_back(x, grad_normed * final_norm[0])
     grad_all = spread_grad(grad)
-    layer_grads = [None] * LAYERS
-    grad_outbias = [None] * LAYERS
+    pad_ids = -vocab_shard % 128
+    tall_ids = jnp.arange(vocab_shard + pad_ids, dtype=jnp.int32)
+    vector_rows = [None] * LAYERS
+    returned = [None] * LAYERS
     for index in reversed(range(LAYERS)):
-        grad_outbias[index] = jnp.sum(grad, 0)
-        grad_hat, layer_grads[index] = block_backward(
+        outbias = jnp.sum(grad, 0)[None]
+        grad_hat, (cols, rows, bias_row, norm_rows) = block_backward(
             grad_all.reshape(LENGTH, D), kept[index], weights[index], cosine, sine
         )
+        vector_rows[index] = jnp.concatenate([norm_rows, outbias, outbias], 0)
+        given = (cols, rows, jnp.pad(bias_row[None], ((0, 7), (0, D - bias_row.shape[0]))))
         grad_hat = grad_hat.reshape(8, BLOCK, D)
         if index:
-            grad_all, grad = next_grad(grad_hat, before[index], grad)
+            grad_all, grad, *returned[index] = next_grad(
+                index, grad_hat, before[index], grad, given
+            )
         else:
-            grad_low = lowest_grad(grad_hat, before[index], grad)
+            grad_low, *returned[index] = lowest_grad(index, grad_hat, before[index], grad, given)
     grad_embedded = plane_gather(grad_low).reshape(row_total, D)
+    inside_ids = jnp.where(local_ids < vocab_shard, local_ids, -1)
     grad_embed = dot_rows(
-        (local_ids[:, None] == jnp.arange(vocab_shard, dtype=jnp.int32)[None, :]).astype(BF),
-        grad_embedded,
-    )
-
-    cols_came, rows_came, bias_came = returned_grads(
-        jnp.stack([g[0] for g in layer_grads]),
-        jnp.stack([g[1] for g in layer_grads]),
-        jnp.stack([jnp.pad(g[2].reshape(1, -1), ((0, 7), (0, 64))) for g in layer_grads]),
-    )
-    bias_part = jnp.sum(bias_came, 0)
+        (inside_ids[:, None] == tall_ids[None, :]).astype(BF), grad_embedded
+    )
+    grad_table = jnp.pad(grad_table, ((0, pad_ids), (0, 0)))
+
+    def of_own_layer(n):
+        picked = returned[LAYERS - 1][n]
+        for index in range(LAYERS - 1):
+            picked = jnp.where(section == index, returned[index][n], picked)
+        return picked
+
     loss_row = jnp.zeros((1, D), F32).at[0, 0].set(jnp.where(shard + y * 8 == 0, loss_part, 0.0))
-    vector_parts = jnp.concatenate(
-        [
-            jnp.concatenate([layer_grads[index][3], grad_outbias[index][None], grad_outbias[index][None]])
-            for index in range(LAYERS)
-        ]
-        + [grad_gains, loss_row],
-        0,
-    )
-    vector_sums = lax.psum(vector_parts, ("yl", "co", "yh", "zz", "xx"))
+    vectors = jnp.concatenate(vector_rows + [grad_gains, loss_row], 0)
+    vectors = jnp.pad(vectors, ((0, 32 - vectors.shape[0]), (0, 0))).reshape(32, D // 128, 128)
+    vectors = jnp.pad(vectors, ((0, 0), (0, 8 - D // 128), (0, 0)))
+    full_in = of_own_layer(0) + w_in_err[0, 0]
+    full_back = of_own_layer(1) + w_back_err[0, 0]
+    err = jnp.transpose(
+        tables_err.reshape(2, vocab_shard, D // 128, 128), (1, 2, 0, 3)
+    ).reshape(-1, 128)
+    facs = (
+        w_in_fac[0].T,
+        w_back_fac[0].T,
+        jnp.pad(tables_fac[0].T, ((0, 0), (0, pad_ids))),
+        jnp.pad(tables_fac[1].T, ((0, 0), (0, pad_ids))),
+    )
+    m_embed, m_head, basis, own, sums, bias_sum, vector_sums = compressed(
+        vocab_shard, grad_embed, grad_table, err, full_in, full_back, facs, of_own_layer(2), vectors
+    )
+    bias_sum = bias_sum[:1, : b_in.shape[1]]
+    vector_sums = vector_sums[:, : D // 128, :].reshape(32, D)
     vec_sum = lax.dynamic_slice_in_dim(vector_sums, section * 6, 6, 0)
     final_sum = vector_sums[6 * LAYERS : 6 * LAYERS + 2]
     loss_sum = vector_sums[6 * LAYERS + 2, 0]
 
-    full_in = jnp.sum(cols_came.astype(F32), 0) + w_in_err[0, 0]
-    full_back = jnp.sum(rows_came.astype(F32), 0) + w_back_err[0, 0]
-    full_embed = grad_embed + tables_err[0, 0]
-    full_head = grad_table + tables_err[0, 1]
-    left = jnp.stack(
-        [
-            jnp.einsum("dn,nr->rd", full_in, w_in_fac[0], precision=HIGH),
-            jnp.einsum("nd,nr->rd", full_back, w_back_fac[0], precision=HIGH),
-            jnp.einsum("nd,nr->rd", full_embed, tables_fac[0], precision=HIGH),
-            jnp.einsum("nd,nr->rd", full_head, tables_fac[1], precision=HIGH),
-        ]
-    )
-    basis, bias_sum = orthonormal_sum(left, bias_part)
-    bias_sum = bias_sum[:1, : b_in.shape[1]]
-    right_in = jnp.einsum("dn,rd->rn", full_in, basis[0], precision=HIGH)
-    right_back = jnp.einsum("nd,rd->rn", full_back, basis[1], precision=HIGH)
-    right_embed = jnp.einsum("nd,rd->rn", full_embed, basis[2], precision=HIGH)
-    right_head = jnp.einsum("nd,rd->rn", full_head, basis[3], precision=HIGH)
-    rights = [right_in, right_back, right_embed, right_head]
-    joint = jnp.concatenate(rights, 1).astype(BF)
-    width = joint.shape[1]
-    joint = right_sum(jnp.pad(joint, ((0, 8), (0, -width % 128))))[:8]
-    sums, at = [], 0
-    for right in rights:
-        sums.append(joint[:, at : at + right.shape[1]])
-        at += right.shape[1]
-    sum_in, sum_back, sum_embed, sum_head = sums
-    red_in = jnp.einsum("rd,rn->dn", basis[0], sum_in, precision=HIGH)
-    red_back = jnp.einsum("rn,rd->nd", sum_back, basis[1], precision=HIGH)
-    own_basis = lax.dynamic_slice_in_dim(basis[2:], replica * own_cols, own_cols, 2)
-    red_tab = jnp.stack(
-        [
-            jnp.einsum("rn,rd->nd", sum_embed, own_basis[0], precision=HIGH),
-            jnp.einsum("rn,rd->nd", sum_head, own_basis[1], precision=HIGH),
-        ]
-    )
-    err_in_new = full_in - jnp.einsum("rd,rn->dn", basis[0], right_in, precision=HIGH)
-    err_back_new = full_back - jnp.einsum("rn,rd->nd", right_back, basis[1], precision=HIGH)
-    err_tab_new = jnp.stack(
-        [
-            full_embed - jnp.einsum("rn,rd->nd", right_embed, basis[2], precision=HIGH),
-            full_head - jnp.einsum("rn,rd->nd", right_head, basis[3], precision=HIGH),
-        ]
-    )
+    def of_tables(arrays):
+        return [jnp.transpose(a, (1, 0, 2)).reshape(-1, 128) for a in arrays]
+
     token_count = lax.axis_size("xx") * seq_rep * LENGTH
     rate_layer = 2.0 * math.sqrt(token_count)
     rate_vector = 6.0 * math.sqrt(token_count)
-    rate_table = jnp.array([50.0, 0.5], F32).reshape(2, 1, 1) * math.sqrt(token_count * VOCAB)
-    in_w, in_m, in_e = momentum_step(w_in, w_in_mom, w_in_ema, red_in[None], rate_layer)
-    back_w, back_m, back_e = momentum_step(
-        w_back, w_back_mom, w_back_ema, red_back[None], rate_layer
-    )
-    tab_w, tab_m, tab_e = momentum_step(tables, tables_mom, tables_ema, red_tab, rate_table)
-    bias_w, bias_m, bias_e = momentum_step(b_in, b_in_mom, b_in_ema, bias_sum, rate_layer)
-    vec_w, vec_m, vec_e = momentum_step(vecs, vecs_mom, vecs_ema, vec_sum[None], rate_vector)
-    fin_w, fin_m, fin_e = momentum_step(final_norm, final_mom, final_ema, final_sum, rate_layer)
+    rate_tables = [rate * math.sqrt(token_count * VOCAB) for rate in (50.0, 0.5)]
+    params = (
+        [w_in[0], w_in_mom[0], w_in_ema[0], w_back[0], w_back_mom[0], w_back_ema[0]]
+        + of_tables((tables, tables_mom, tables_ema))
+    )
+    err_tab, err_in, err_back, *new = updated(
+        vocab_shard, (rate_layer, rate_tables), (m_embed, m_head), full_in, full_back,
+        basis, own, sums, params, err,
+    )
+    err_tab = jnp.transpose(
+        err_tab.reshape(vocab_shard, D // 128, 2, 128), (2, 0, 1, 3)
+    ).reshape(tables_err.shape)
+    in_w, in_m, in_e, back_w, back_m, back_e = [a[None] for a in new[:6]]
+    tab_w, tab_m, tab_e = [
+        jnp.transpose(a.reshape(vocab_shard, 2, own_cols), (1, 0, 2)) for a in new[6:]
+    ]
+    _, places = factor_places(full_in.shape[1], full_back.shape[0], vocab_shard)
+    fac_in, fac_back, fac_embed, fac_head = [
+        sums[half, :, at : at + width].T for half, at, width in places
+    ]
+    bias_w, bias_m, bias_e = stepped(rate_layer, b_in, b_in_mom, b_in_ema, bias_sum)
+    vec_w, vec_m, vec_e = stepped(rate_vector, vecs, vecs_mom, vecs_ema, vec_sum[None])
+    fin_w, fin_m, fin_e = stepped(rate_layer, final_norm, final_mom, final_ema, final_sum)
     return (
         loss_sum,
         weight_total,
@@ -932,13 +1154,13 @@
         bias_e,
         vec_e,
         fin_e,
-        err_in_new[None, None],
-        err_back_new[None, None],
-        err_tab_new[None],
-        sum_in.T[None],
-        sum_back.T[None],
-        sum_embed.T,
-        sum_head.T,
+        err_in[None, None],
+        err_back[None, None],
+        err_tab,
+        fac_in[None],
+        fac_back[None],
+        fac_embed,
+        fac_head,
     )
 
 

time: 861 us -> 733 us (0.85)
  blocking collectives: 64.8 us -> 0 us
  matrix products: 173 us -> 140 us
  local copies, waits for them, and re-layouts: 78.9 us -> 47.6 us
  Pallas kernels: 455 us -> 464 us
    pallas_call x17, Pallas kernels: 345 us -> 421 us  [kernel_call(): pl.pallas_call(body, out_shape=out_shape, in_specs=[VMEM_SPEC] * len(args...]
    pallas_call x3 -> x1, Pallas kernels: 110 us -> 43.7 us  [all_features(): pl.pallas_call(functools.partial(features_body, layers, count), out_shape...]
    psum x1 -> x0, blocking collectives: 64.8 us -> none  [on_device(): vector_sums = lax.psum(vector_parts, ('yl', 'co', 'yh', 'zz', 'xx'))]
    dot_general x16 -> x0, matrix products: 32.8 us -> none  [the longest x1 2.82 us: on_device(): jnp.einsum('rn,rd->nd', right_embed, basis[2], precision=HIGH)]
    unnamed x564 -> x499, local copies, waits for them, and re-layouts: 52.6 us -> 30.1 us
    slice x5 -> x1, local copies, waits for them, and re-layouts: 12.2 us -> 0.91 us  [on_device(): vector_sums = vector_sums[:, :D // 128, :].reshape(32, D)]
  transfers between devices with their start and end apart: 2 -> 1, of which waited for: 0 -> 0; matrix products, arithmetic and copies ran while one was open for 9% -> 10% of each run, Pallas kernels for 27% -> 29%
where the time goes in v2:
time: 733 us; the launch traced here: 725 us
  Pallas kernels  464 us (63%)
  matrix products  140 us (19%)
  other arithmetic  53.5 us (7%)
  local copies, waits for them, and re-layouts  47.6 us (6%)
  between operations  19.8 us (3%)
    pallas_call x17, Pallas kernels, kernel_call(): pl.pallas_call(body, out_shape=out_shape, in_specs=[VMEM_SPEC] * len(args...  421 us
    dot_general x34, matrix products, dot_plain(): return jnp.dot(left, right, preferred_element_type=F32)  51.4 us
    dot_general x34, matrix products, dot_rows(): lax.dot_general(left, right, (((0,), (0,)), ((), ())), preferred_element_...  47.6 us
    pallas_call x1, Pallas kernels, all_features(): pl.pallas_call(functools.partial(features_body, layers, count), out_shape...  43.7 us
    dot_general x33, matrix products, dot_cols(): lax.dot_general(left, right, (((1,), (1,)), ((), ())), preferred_element_...  40.9 us
    unnamed x499, local copies, waits for them, and re-layouts  30.1 us
  transfers between devices with their start and end apart: 1, of which 0 were waited for; matrix products, arithmetic and copies ran while one was open for 10% of the time, Pallas kernels for 29%

profile of v2, /device:TPU:0, one launch (start us, length us, event | category | flops | bytes accessed | tf_op | source)
XLA Modules:
  0.0 725.1 jit_solution(15595348486589459238)
XLA Ops:
  13.3 43.7 %shard_map.475 = (bf16[4,1584,128]{2,1,0:T(8,128)(2,1)}, bf16[512,448]{1,0:T(8,128)(2,1)}, bf16[320,512]{1,0:T(8,128)(2,1)}, f32[16,512]{1,0:T(8,128)}) custom-call(bf16[1584,128]{1,0:T(8,128)(2,1)} %pad.82.block, bf16[512,448]{1,0:T(8,128)(2,1)} %bitcast_convert_fusion.1.refs_0_, bf16[320,512]{1,0:T(8,128)(2,1)} %bitcast_convert_fusion.refs_1_, ...), custom_call_target="tpu_custom_call" | custom-call | tf_op jit(solution)/shard_map/pallas_call | solution.py:565
  62.9 8.2 %fusion.6 = bf16[4096,512]{1,0:T(8,128)(2,1)S(1)} fusion(bf16[1584,512]{0,1:T(8,128)(2,1)S(1)} %bitcast.338, s32[4096]{0:T(1024)S(1)} %bitcast.372), kind=kOutput, calls=%fused_computation.12 | convolution fusion | flops 6658850816 | bytes 5832704 | tf_op jit(solution)/shard_map/dot_general | solution.py:841
  71.1 32.5 %shard_map.476.x = f32[128,512]{1,0:T(8,128)S(1)} custom-call(bf16[32,128,512]{2,1,0:T(8,128)(2,1)S(1)} %bitcast.322), custom_call_target="tpu_custom_call" | custom-call | tf_op jit(solution)/shard_map/pallas_call | solution.py:73
  103.6 12.7 %shard_map.477 = (bf16[8,128,512]{2,1,0:T(8,128)(2,1)S(1)}, bf16[512,448]{1,0:T(8,128)(2,1)S(1)}, bf16[320,512]{1,0:T(8,128)(2,1)S(1)}, f32[16,512]{1,0:T(8,128)S(1)}) custom-call(f32[128,512]{1,0:T(8,128)S(1)} %shard_map.476.x, bf16[512,448]{1,0:T(8,128)(2,1)S(1)} %copy-done.2, bf16[320,512]{1,0:T(8,128)(2,1)S(1)} %copy-done.3, f32[16,512]{1,0:T(8,128)S(1)} %copy-done.23), custom_call_target="tpu_custom_call" | custom-call | tf_op jit(solution)/shard_map/pallas_call | solution.py:73
  125.6 35.2 %shard_map.478 = (bf16[8,128,512]{2,1,0:T(8,128)(2,1)S(1)}, f32[128,512]{1,0:T(8,128)S(1)}, bf16[512,448]{1,0:T(8,128)(2,1)S(1)}, bf16[320,512]{1,0:T(8,128)(2,1)S(1)}, f32[16,512]{1,0:T(8,128)S(1)}) custom-call(bf16[8,128,512]{2,1,0:T(8,128)(2,1)S(1)} %bitcast.325, f32[128,512]{1,0:T(8,128)S(1)} %shard_map.476.x, f32[8,512]{1,0:T(8,128)S(1)} %broadcast_in_dim.197.shift, ...), custom_call_target="tpu_custom_call" | custom-call | tf_op jit(solution)/shard_map/pallas_call | solution.py:73
  170.6 22.5 %shard_map.479 = (bf16[8,128,512]{2,1,0:T(8,128)(2,1)S(1)}, f32[128,512]{1,0:T(8,128)S(1)}, bf16[512,448]{1,0:T(8,128)(2,1)S(1)}, bf16[320,512]{1,0:T(8,128)(2,1)S(1)}, f32[16,512]{1,0:T(8,128)S(1)}) custom-call(bf16[8,128,512]{2,1,0:T(8,128)(2,1)S(1)} %bitcast.324, f32[128,512]{1,0:T(8,128)S(1)} %get-tuple-element.108.x, ...), custom_call_target="tpu_custom_call" | custom-call | tf_op jit(solution)/shard_map/pallas_call | solution.py:73
  203.5 20.8 %shard_map.480 = (bf16[8,128,512]{2,1,0:T(8,128)(2,1)S(1)}, f32[128,512]{1,0:T(8,128)S(1)}) custom-call(bf16[8,128,512]{2,1,0:T(8,128)(2,1)S(1)} %bitcast.327, f32[128,512]{1,0:T(8,128)S(1)} %get-tuple-element.113.x, f32[8,512]{1,0:T(8,128)S(1)} %broadcast_in_dim.201.shift), custom_call_target="tpu_custom_call" | custom-call | tf_op jit(solution)/shard_map/pallas_call | solution.py:73
  234.1 11.9 %shard_map.481 = (f32[128,512]{1,0:T(8,128)S(1)}, bf16[128,512]{1,0:T(8,128)(2,1)S(1)}) custom-call(bf16[8,128,512]{2,1,0:T(8,128)(2,1)S(1)} %bitcast.326, f32[128,512]{1,0:T(8,128)S(1)} %get-tuple-element.118.x, f32[8,512]{1,0:T(8,128)S(1)} %broadcast_in_dim.203.shift, f32[8,512]{1,0:T(8,128)S(1)} %pad.85.gains), custom_call_target="tpu_custom_call" | custom-call | tf_op jit(solution)/shard_map/pallas_call | solution.py:73
  248.0 31.4 %shard_map.482 = bf16[32,128,512]{2,1,0:T(8,128)(2,1)S(1)} custom-call(bf16[128,512]{1,0:T(8,128)(2,1)S(1)} %get-tuple-element.120.block), custom_call_target="tpu_custom_call" | custom-call | tf_op jit(solution)/shard_map/pallas_call | solution.py:73
  296.1 14.2 %fusion.312 = (f32[4096]{0:T(1024)S(1)}, f32[4096,1572]{0,1:T(8,128)}) fusion(bf16[4096,512]{1,0:T(8,128)(2,1)} %bitcast.319, bf16[1,1572,512]{2,1,0:T(8,128)(2,1)} %all-gather.3.cloned.1.call-done), kind=kOutput, calls=%fused_computation.651 | convolution fusion | flops 6599880704 | bytes 31576064 | tf_op jit(solution)/shard_map/dot_general | solution.py:835
  310.3 11.9 %exponential_reduce_fusion = (f32[4096]{0:T(1024)S(1)}, f32[4096]{0:T(1024)S(1)}) fusion(f32[4096,1572]{0,1:T(8,128)} %get-tuple-element.415, f32[4096]{0:T(1024)S(1)} %get-tuple-element.414, s32[4096]{0:T(1024)S(1)} %bitcast.354), kind=kLoop, calls=%fused_computation.8 | loop fusion | flops 32186368 | bytes 25821184 | tf_op jit(solution)/shard_map/reduce_sum | solution.py:1033
  322.3 17.0 %shard_map.483 = f32[32,8,128]{2,1,0:T(8,128)S(1)} custom-call(f32[32,8,128]{2,1,0:T(8,128)S(1)} %pad.86.stats), custom_call_target="tpu_custom_call" | custom-call | tf_op jit(solution)/shard_map/pallas_call | solution.py:73
  340.7 14.9 %convolution_convert_fusion = bf16[4096,512]{1,0:T(8,128)(2,1)S(1)} fusion(bf16[1,1572,512]{2,1,0:T(8,128)(2,1)} %all-gather.3.cloned.1.call-done, f32[4096,1572]{0,1:T(8,128)} %get-tuple-element.415, f32[4096]{0:T(1024)S(1)} %bitcast.370, f32[4096]{0:T(1024)S(1)} %bitcast.368, s32[4096]{0:T(1024)S(1)} %bitcast.355), kind=kOutput, calls=%fused_computation.13 | convolution fusion | flops 6634176512 | bytes 31608832 | tf_op jit(solution)/shard_map/dot_general | solution.py:841
  355.6 32.4 %shard_map.484 = f32[128,512]{1,0:T(8,128)S(1)} custom-call(bf16[32,128,512]{2,1,0:T(8,128)(2,1)S(1)} %bitcast.323), custom_call_target="tpu_custom_call" | custom-call | tf_op jit(solution)/shard_map/pallas_call | solution.py:73
  389.6 12.9 %shard_map.485 = bf16[8,128,512]{2,1,0:T(8,128)(2,1)S(1)} custom-call(f32[128,512]{1,0:T(8,128)S(1)} %get-tuple-element.299.grad), custom_call_target="tpu_custom_call" | custom-call | tf_op jit(solution)/shard_map/pallas_call | solution.py:73
  421.2 21.9 %shard_map.486 = (bf16[8,128,512]{2,1,0:T(8,128)(2,1)S(1)}, f32[128,512]{1,0:T(8,128)S(1)}, f32[512,448]{1,0:T(8,128)S(1)}, f32[320,512]{1,0:T(8,128)S(1)}, f32[8,512]{1,0:T(8,128)S(1)}) custom-call(bf16[8,128,512]{2,1,0:T(8,128)(2,1)S(1)} %bitcast.328, f32[128,512]{1,0:T(8,128)S(1)} %get-tuple-element.118.x, f32[128,512]{1,0:T(8,128)S(1)} %get-tuple-element.299.grad, ...), custom_call_target="tpu_custom_call" | custom-call | tf_op jit(solution)/shard_map/pallas_call | solution.py:73
  461.8 23.0 %shard_map.487 = (bf16[8,128,512]{2,1,0:T(8,128)(2,1)S(1)}, f32[128,512]{1,0:T(8,128)S(1)}, f32[512,448]{1,0:T(8,128)S(1)}, f32[320,512]{1,0:T(8,128)S(1)}, f32[8,512]{1,0:T(8,128)S(1)}) custom-call(bf16[8,128,512]{2,1,0:T(8,128)(2,1)S(1)} %bitcast.330, f32[128,512]{1,0:T(8,128)S(1)} %copy-done.16, f32[128,512]{1,0:T(8,128)S(1)} %get-tuple-element.122.grad, ...), custom_call_target="tpu_custom_call" | custom-call | tf_op jit(solution)/shard_map/pallas_call | solution.py:73
  501.5 24.0 %shard_map.488 = (bf16[8,128,512]{2,1,0:T(8,128)(2,1)S(1)}, f32[128,512]{1,0:T(8,128)S(1)}, f32[512,448]{1,0:T(8,128)S(1)}, f32[320,512]{1,0:T(8,128)S(1)}, f32[8,512]{1,0:T(8,128)S(1)}) custom-call(bf16[8,128,512]{2,1,0:T(8,128)(2,1)S(1)} %bitcast.331, f32[128,512]{1,0:T(8,128)S(1)} %get-tuple-element.108.x, f32[128,512]{1,0:T(8,128)S(1)} %get-tuple-element.124.grad, ...), custom_call_target="tpu_custom_call" | custom-call | tf_op jit(solution)/shard_map/pallas_call | solution.py:73
  537.9 14.1 %fusion.288 = f32[1572,512]{1,0:T(8,128)} fusion(bf16[4096,512]{1,0:T(8,128)(2,1)S(1)} %bitcast.320, f32[4096,1572]{0,1:T(8,128)} %get-tuple-element.415, f32[4096]{0:T(1024)S(1)} %bitcast.371, f32[4096]{0:T(1024)S(1)} %bitcast.369, s32[4096]{0:T(1024)S(1)} %bitcast.356), kind=kOutput, calls=%fused_computation.631 | convolution fusion | flops 6632079360 | bytes 33218560 | tf_op jit(solution)/shard_map/dot_general | solution.py:829
  557.9 25.7 %shard_map.489 = (bf16[128,512]{1,0:T(8,128)(2,1)S(1)}, f32[512,448]{1,0:T(8,128)S(1)}, f32[320,512]{1,0:T(8,128)S(1)}, f32[8,512]{1,0:T(8,128)S(1)}) custom-call(bf16[8,128,512]{2,1,0:T(8,128)(2,1)S(1)} %bitcast.329, f32[128,512]{1,0:T(8,128)S(1)} %copy-done.5, f32[128,512]{1,0:T(8,128)S(1)} %get-tuple-element.126.grad, ...), custom_call_target="tpu_custom_call" | custom-call | tf_op jit(solution)/shard_map/pallas_call | solution.py:73
  583.6 29.6 %shard_map.490 = bf16[32,128,512]{2,1,0:T(8,128)(2,1)S(1)} custom-call(bf16[128,512]{1,0:T(8,128)(2,1)S(1)} %get-tuple-element.127.block), custom_call_target="tpu_custom_call" | custom-call | tf_op jit(solution)/shard_map/pallas_call | solution.py:73
  618.5 12.2 %fusion.g_embed = f32[1664,512]{1,0:T(8,128)} fusion(bf16[4096,512]{1,0:T(8,128)(2,1)} %bitcast.321, s32[4096]{0:T(1024)S(1)} %copy-done.171), kind=kOutput, calls=%fused_computation.2 | convolution fusion | flops 6986137600 | bytes 7618560 | tf_op jit(solution)/shard_map/dot_general | solution.py:829
  634.4 42.0 %shard_map.491 = (f32[1664,512]{1,0:T(8,128)}, f32[1664,512]{1,0:T(8,128)}, f32[4,8,512]{2,1,0:T(8,128)}, f32[2,8,2176]{2,1,0:T(8,128)}, f32[2,8,2176]{2,1,0:T(8...) custom-call(f32[1664,512]{1,0:T(8,128)} %fusion.g_embed, f32[1664,512]{1,0:T(8,128)} %pad.99.g_head, ...), custom_call_target="tpu_custom_call" | custom-call | tf_op jit(solution)/shard_map/pallas_call | solution.py:73
  682.7 25.1 %shard_map.492 = (f32[12576,128]{1,0:T(8,128)}, f32[512,448]{1,0:T(8,128)}, f32[320,512]{1,0:T(8,128)}, f32[512,448]{1,0:T(8,128)}, f32[512,448]{1,0:T(8,128)}, ...) custom-call(f32[1664,512]{1,0:T(8,128)} %get-tuple-element.141.m_emb, ...), custom_call_target="tpu_custom_call" | custom-call | tf_op jit(solution)/shard_map/pallas_call | solution.py:73
  (754 shorter events, 165.6 us)
Async XLA Ops:
  7.2 239.0 %copy-start = (s32[4]{0:T(128)S(1)}, s32[4]{0:T(128)}, u32[]{:S(2)}) copy-start(s32[4]{0:T(128)} %param.32) | copy-start | bytes 52
  7.2 288.9 %all-gather.3.cloned.1.call-start = ((), (), s32[]{:S(2)}) async-start(), calls=%async_computation | async-start | bytes 2017280 | tf_op jit(solution)/shard_map/all_gather | solution.py:1005
  10.1 46.8 %copy-start.50 = (f32[1,512,448]{2,1,0:T(8,128)}, f32[1,512,448]{2,1,0:T(8,128)S(1)}, u32[]{:S(2)}) copy-start(f32[1,512,448]{2,1,0:T(8,128)S(1)} %copy.115) | copy-start | bytes 2752516
  13.3 48.9 %copy-start.157 = (s32[4,1025]{1,0:T(4,128)S(1)}, s32[4,1025]{1,0:T(4,128)}, u32[]{:S(2)}) copy-start(s32[4,1025]{1,0:T(4,128)} %param.30) | copy-start | bytes 49204
  57.9 58.4 %copy-start.198 = (f32[1,512]{1,0:T(1,128)}, f32[1,512]{1,0:T(1,128)S(1)}, u32[]{:S(2)}) copy-start(f32[1,512]{1,0:T(1,128)S(1)} %get-tuple-element.379) | copy-start | bytes 6148
  57.9 58.4 %copy-start.200 = (f32[1,512]{1,0:T(1,128)}, f32[1,512]{1,0:T(1,128)S(1)}, u32[]{:S(2)}) copy-start(f32[1,512]{1,0:T(1,128)S(1)} %get-tuple-element.381) | copy-start | bytes 6148
  71.0 32.5 %copy-start.2 = (bf16[512,448]{1,0:T(8,128)(2,1)S(1)}, bf16[512,448]{1,0:T(8,128)(2,1)}, u32[]{:S(2)}) copy-start(bf16[512,448]{1,0:T(8,128)(2,1)} %bitcast_convert_fusion.1.refs_0_) | copy-start | bytes 1376260
  71.0 32.5 %copy-start.3 = (bf16[320,512]{1,0:T(8,128)(2,1)S(1)}, bf16[320,512]{1,0:T(8,128)(2,1)}, u32[]{:S(2)}) copy-start(bf16[320,512]{1,0:T(8,128)(2,1)} %bitcast_convert_fusion.refs_1_) | copy-start | bytes 983044
  71.1 32.5 %copy-start.23 = (f32[16,512]{1,0:T(8,128)S(1)}, f32[16,512]{1,0:T(8,128)}, u32[]{:S(2)}) copy-start(f32[16,512]{1,0:T(8,128)} %select_maximum_fusion.refs_2_) | copy-start | bytes 98308
  116.3 49.6 %copy-start.30 = (bf16[512,448]{1,0:T(8,128)(2,1)}, bf16[512,448]{1,0:T(8,128)(2,1)S(1)}, u32[]{:S(2)}) copy-start(bf16[512,448]{1,0:T(8,128)(2,1)S(1)} %get-tuple-element.106) | copy-start | bytes 1376260
  116.3 53.9 %copy-start.36 = (bf16[320,512]{1,0:T(8,128)(2,1)}, bf16[320,512]{1,0:T(8,128)(2,1)S(1)}, u32[]{:S(2)}) copy-start(bf16[320,512]{1,0:T(8,128)(2,1)S(1)} %get-tuple-element.107) | copy-start | bytes 983044
  116.3 44.6 %copy-start.202 = (f32[1,512]{1,0:T(1,128)}, f32[1,512]{1,0:T(1,128)S(1)}, u32[]{:S(2)}) copy-start(f32[1,512]{1,0:T(1,128)S(1)} %get-tuple-element.374) | copy-start | bytes 6148
  116.3 44.6 %copy-start.204 = (f32[1,512]{1,0:T(1,128)}, f32[1,512]{1,0:T(1,128)S(1)}, u32[]{:S(2)}) copy-start(f32[1,512]{1,0:T(1,128)S(1)} %get-tuple-element.376) | copy-start | bytes 6148
  160.9 37.5 %copy-start.32 = (bf16[512,448]{1,0:T(8,128)(2,1)}, bf16[512,448]{1,0:T(8,128)(2,1)S(1)}, u32[]{:S(2)}) copy-start(bf16[512,448]{1,0:T(8,128)(2,1)S(1)} %get-tuple-element.111) | copy-start | bytes 1376260
  160.9 42.2 %copy-start.38 = (bf16[320,512]{1,0:T(8,128)(2,1)}, bf16[320,512]{1,0:T(8,128)(2,1)S(1)}, u32[]{:S(2)}) copy-start(bf16[320,512]{1,0:T(8,128)(2,1)S(1)} %get-tuple-element.112) | copy-start | bytes 983044
  193.2 35.9 %copy-start.34 = (bf16[512,448]{1,0:T(8,128)(2,1)}, bf16[512,448]{1,0:T(8,128)(2,1)S(1)}, u32[]{:S(2)}) copy-start(bf16[512,448]{1,0:T(8,128)(2,1)S(1)} %get-tuple-element.116) | copy-start | bytes 1376260
  193.2 40.2 %copy-start.40 = (bf16[320,512]{1,0:T(8,128)(2,1)}, bf16[320,512]{1,0:T(8,128)(2,1)S(1)}, u32[]{:S(2)}) copy-start(bf16[320,512]{1,0:T(8,128)(2,1)S(1)} %get-tuple-element.117) | copy-start | bytes 983044
  225.5 178.2 %copy-start.94 = (bf16[1024,48]{0,1:T(8,128)(2,1)}, bf16[1024,48]{0,1:T(8,128)(2,1)S(1)}, u32[]{:S(2)}) copy-start(bf16[1024,48]{0,1:T(8,128)(2,1)S(1)} %get-tuple-element.348) | copy-start | bytes 294916
  248.0 43.7 %copy-start.216 = (f32[128]{0:T(128)}, f32[128]{0:T(128)S(1)}, u32[]{:S(2)}) copy-start(f32[128]{0:T(128)S(1)} %broadcast_multiply_fusion.2) | copy-start | bytes 1540
  248.0 33.5 %copy-start.156 = (s32[1,8,4,128]{3,2,1,0:T(4,128)S(1)}, s32[1,8,4,128]{3,2,1,0:T(4,128)}, u32[]{:S(2)}) copy-start(s32[1,8,4,128]{3,2,1,0:T(4,128)} %get-tuple-element.382) | copy-start | bytes 49156
  281.5 59.2 %copy-start.154 = (s32[1,8,4,128]{3,1,2,0:T(8,128)}, s32[1,8,4,128]{3,1,2,0:T(8,128)S(1)}, u32[]{:S(2)}) copy-start(s32[1,8,4,128]{3,1,2,0:T(8,128)S(1)} %copy.157) | copy-start | bytes 49156
  291.9 96.1 %copy-start.231 = (f32[128]{0:T(128)}, f32[128]{0:T(128)S(1)}, u32[]{:S(2)}) copy-start(f32[128]{0:T(128)S(1)} %add_rsqrt_fusion) | copy-start | bytes 1540
  293.8 109.7 %copy-start.168 = (f32[512]{0:T(512)}, f32[512]{0:T(512)S(1)}, u32[]{:S(2)}) copy-start(f32[512]{0:T(512)S(1)} %log_add_fusion.4) | copy-start | bytes 6148
  355.6 32.4 %copy-start.217 = (f32[128]{0:T(128)S(1)}, f32[128]{0:T(128)}, u32[]{:S(2)}) copy-start(f32[128]{0:T(128)} %copy-done.216) | copy-start | bytes 1540
  (217 other events, 1135.7 us)
Sparse Core Ops, SparseCore 0:
  10.3 42.9 all-gather.2

commit v3 on v2

v3 whole, which is shorter than its diff:
```python
import functools
import math

import jax
import jax.numpy as jnp
import numpy as np
from jax import lax
from jax.experimental import pallas as pl
from jax.experimental.pallas import tpu as pltpu
from jax.sharding import Mesh
from jax.sharding import PartitionSpec as P

D = 512
HEAD = 64
ROT = 16
VOCAB = 50304
LAYERS = 4
LENGTH = 1024
RANK = 8
STEP = 5
BLOCK = 128
CHUNK = 128
TILES = D // 128

EPS_NORM = 1e-05
MOMENTUM = 0.9
NEG_BIG = -1e30
HIGH = lax.Precision.HIGHEST
BF = jnp.bfloat16
F32 = jnp.float32
MESH_ID = pl.DeviceIdType.MESH
FAR = (2, 1, 3)


def where_am_i():
    core, z = lax.axis_index("co"), lax.axis_index("zz")
    y = lax.axis_index("yh") * 2 + lax.axis_index("yl")
    return y, core, z


def at_chip(y, z):
    return {"yh": y // 2, "yl": lax.rem(y, 2), "zz": z}


def send(src, dst, sems, at, device):
    copy = pltpu.make_async_remote_copy(
        src_ref=src,
        dst_ref=dst,
        send_sem=sems[0].at[at],
        recv_sem=sems[1].at[at],
        device_id=device,
        device_id_type=MESH_ID,
    )
    copy.start()
    return copy


def greet(devices):
    barrier = pltpu.get_barrier_semaphore()
    for device in devices:
        pl.semaphore_signal(barrier, inc=1, device_id=device, device_id_type=MESH_ID)
    pl.semaphore_wait(barrier, len(devices))


def sem_pairs(*counts):
    return [pltpu.SemaphoreType.DMA((n,)) for n in counts for _ in range(2)]


VMEM_SPEC = pl.BlockSpec(memory_space=pltpu.VMEM)


def kernel_call(
    body, out_shape, args, scratch, cid=None, limit=48, in_specs=None, out_specs=None
):
    many = isinstance(out_shape, (list, tuple))
    return pl.pallas_call(
        body,
        out_shape=out_shape,
        in_specs=in_specs or [VMEM_SPEC] * len(args),
        out_specs=out_specs or ([VMEM_SPEC] * len(out_shape) if many else VMEM_SPEC),
        scratch_shapes=scratch,
        compiler_params=pltpu.CompilerParams(
            collective_id=cid, has_side_effects=cid is not None, vmem_limit_bytes=limit * 2**20
        ),
    )(*args)


def dot_rows(left, right):
    return lax.dot_general(
        left, right, (((0,), (0,)), ((), ())), preferred_element_type=F32
    )


def dot_cols(left, right):
    return lax.dot_general(
        left, right, (((1,), (1,)), ((), ())), preferred_element_type=F32
    )


def dot_plain(left, right):
    return jnp.dot(left, right, preferred_element_type=F32)


def normed_rows(values):
    center = values - jnp.mean(values, -1, keepdims=True)
    spread = jnp.mean(center * center, -1, keepdims=True)
    scale = lax.rsqrt(spread + EPS_NORM)
    return center * scale, scale


def norm_back(values, grad):
    hat, scale = normed_rows(values)
    return scale * (
        grad
        - jnp.mean(grad, -1, keepdims=True)
        - hat * jnp.mean(grad * hat, -1, keepdims=True)
    )


def row_sum(part, r1, s, r2, sems1, sems2, meanwhile=None):
    y, core, z = where_am_i()
    first = []
    for i, k in enumerate(FAR + (0,)):
        zz = lax.rem(z + k, 4)
        first.append(send(part.at[zz * 2 + 1 - core], r1.at[i], sems1, i, {"co": 1 - core}))
    second = []
    for i, k in enumerate(FAR):
        zz = lax.rem(z + k, 4)
        first[i].wait_recv()
        s[i] = (part[zz * 2 + core].astype(F32) + r1[i].astype(F32)).astype(BF)
        second.append(send(s.at[i], r2.at[i], sems2, i, {"zz": zz}))
    if meanwhile is not None:
        meanwhile()
    first[3].wait_recv()
    total = part[z * 2 + core].astype(F32) + r1[3].astype(F32)
    for i in range(3):
        second[i].wait_recv()
        total = total + r2[i].astype(F32)
    for copy in first + second:
        copy.wait_send()
    return total


def row_gather(everyone, sems3, sems4, meanwhile=None):
    y, core, z = where_am_i()
    own = everyone.at[z * 2 + core]
    third = [
        send(own, own, sems3, i, {"zz": lax.rem(z + k, 4)}) for i, k in enumerate(FAR)
    ]
    fourth = [send(own, own, sems4, 3, {"co": 1 - core})]
    if meanwhile is not None:
        meanwhile()
    for i, k in enumerate(FAR):
        third[i].wait_recv()
        came = everyone.at[lax.rem(z + 4 - k, 4) * 2 + core]
        fourth.append(send(came, came, sems4, i, {"co": 1 - core}))
    for copy in third:
        copy.wait_send()
    for copy in fourth:
        copy.wait()


def row_peers():
    y, core, z = where_am_i()
    return [{"co": 1 - core}] + [{"zz": lax.rem(z + k, 4)} for k in FAR]


SUM_SCRATCH = [
    pltpu.VMEM((4, BLOCK, D), BF),
    pltpu.VMEM((3, BLOCK, D), BF),
    pltpu.VMEM((3, BLOCK, D), BF),
] + sem_pairs(4, 3)
GATHER_SCRATCH = sem_pairs(3, 4)


def pair_peer():
    return [{"co": 1 - lax.axis_index("co")}]


def column_peers():
    y, core, z = where_am_i()
    return [{**at_chip(lax.rem(y + dy, 4), z), "co": c} for dy in FAR for c in (0, 1)]


def column_others():
    y, core, z = where_am_i()
    return [{**at_chip(lax.rem(y + dy, 4), z), "co": 1 - core} for dy in FAR]


def home_and_layer():
    y, core, z = where_am_i()
    return y // 2 == core, lax.rem(y, 2) * 2 + core


def take_copies(sources, places, sems, dy):
    y, core, z = where_am_i()
    return [
        pltpu.make_async_remote_copy(
            src_ref=src,
            dst_ref=dst,
            send_sem=sems[2 * n].at[dy],
            recv_sem=sems[2 * n + 1].at[0],
            device_id={**at_chip(lax.rem(y + dy, 4), z), "co": y // 2},
            device_id_type=MESH_ID,
        )
        for n, (src, dst) in enumerate(zip(sources, places))
    ]


def take_local(sources, places, sems):
    return [
        pltpu.make_async_copy(src, dst, sems[2 * n + 1].at[0])
        for n, (src, dst) in enumerate(zip(sources, places))
    ]


def take_start(layer, sources, places, sems):
    home, own = home_and_layer()

    @pl.when(own == layer)
    def _():
        for dy in FAR:
            for copy in take_copies(sources, places, sems, dy):
                copy.start()

    @pl.when(jnp.logical_and(own == layer, home))
    def _():
        for copy in take_local(sources, places, sems):
            copy.start()

    @pl.when(jnp.logical_and(own == layer, jnp.logical_not(home)))
    def _():
        for copy in take_copies(sources, places, sems, 0):
            copy.start()


def take_finish(layer, sources, places, sems):
    home, own = home_and_layer()

    @pl.when(own == layer)
    def _():
        for dy in FAR:
            for copy in take_copies(sources, places, sems, dy):
                copy.wait_send()

    @pl.when(jnp.logical_and(own == layer, jnp.logical_not(home)))
    def _():
        for copy in take_copies(sources, places, sems, 0):
            copy.wait_send()

    for copy in take_local(sources, places, sems):
        copy.wait()


def take_scratch(count):
    return [pltpu.SemaphoreType.DMA((n,)) for _ in range(count) for n in (4, 1)]


def give_copies(layer, sources, landed, sems):
    y, core, z = where_am_i()
    return [
        pltpu.make_async_remote_copy(
            src_ref=src,
            dst_ref=dst.at[y],
            send_sem=sems[2 * n].at[0],
            recv_sem=sems[2 * n + 1].at[y],
            device_id={**at_chip(core * 2 + layer // 2, z), "co": layer % 2},
            device_id_type=MESH_ID,
        )
        for n, (src, dst) in enumerate(zip(sources, landed))
    ]


def give_start(layer, sources, landed, sems):
    y, core, z = where_am_i()
    home, own = home_and_layer()
    local = jnp.logical_and(home, own == layer)

    @pl.when(jnp.logical_not(local))
    def _():
        for copy in give_copies(layer, sources, landed, sems):
            copy.start()

    @pl.when(local)
    def _():
        for n, (src, dst) in enumerate(zip(sources, landed)):
            pltpu.make_async_copy(src, dst.at[y], sems[2 * n + 1].at[y]).start()


def give_finish(layer, sources, landed, sums, sems):
    home, own = home_and_layer()

    @pl.when(own == layer)
    def _():
        for n, (src, dst) in enumerate(zip(sources, landed)):
            for index in range(4):
                pltpu.make_async_copy(src, dst.at[index], sems[2 * n + 1].at[index]).wait()
            total = dst[0].astype(F32)
            for index in range(1, 4):
                total = total + dst[index].astype(F32)
            sums[n][...] = total

    @pl.when(jnp.logical_not(jnp.logical_and(home, own == layer)))
    def _():
        for copy in give_copies(layer, sources, landed, sems):
            copy.wait_send()


def give_scratch(grads):
    return [pltpu.VMEM((4, *g.shape), g.dtype) for g in grads] + [
        pltpu.SemaphoreType.DMA((n,)) for _ in grads for n in (1, 4)
    ]


def forward_body(layer, part, x, shift, *refs):
    sources, everyone, x_new, places, refs = refs[:2], refs[2], refs[3], refs[4:6], refs[6:]
    r1, s, r2, e, f, g, h, a, b, c, d = refs[:11]
    sems = refs[11:]
    y, core, z = where_am_i()
    greet(row_peers() + column_peers())
    take_start(layer, sources, places, sems)
    after = x[...] + row_sum(part, r1, s, r2, (e, f), (g, h)) + shift[0:1]
    x_new[...] = after
    everyone[z * 2 + core] = normed_rows(after)[0].astype(BF)
    row_gather(everyone, (a, b), (c, d))
    take_finish(layer, sources, places, sems)


def next_hat(part, x, shift, layer, sources):
    return kernel_call(
        functools.partial(forward_body, layer),
        [jax.ShapeDtypeStruct((8, BLOCK, D), BF), jax.ShapeDtypeStruct((BLOCK, D), F32)]
        + [jax.ShapeDtypeStruct(a.shape, a.dtype) for a in sources],
        (part, x, shift, *sources),
        SUM_SCRATCH + GATHER_SCRATCH + take_scratch(len(sources)),
        10 + layer,
    )


def backward_body(layer, table_parts, part, x, grad, *refs):
    sources, refs = refs[:2], refs[2:]
    begun, steep, tokens = (), None, None
    if table_parts:
        steep, tokens, refs = refs[0], refs[1], refs[2:]
        if table_parts[0]:
            begun, refs = refs[:1], refs[1:]
    everyone, g_new, sums, refs = refs[0], refs[1], refs[2:4], refs[4:]
    if table_parts:
        table_grad, refs = refs[0], refs[1:]
    landed, give_sems, refs = refs[:2], refs[2:6], refs[6:]
    r1, s, r2, e, f, g, h, a, b, c, d = refs[:11]
    y, core, z = where_am_i()
    greet(row_peers() + column_peers())
    hooks = [None, None]
    if table_parts:
        slopes, rows, sem_slopes, sem_rows = refs[11:]
        loads = []
        for n, q in enumerate(table_parts):
            loads.append(
                (
                    pltpu.make_async_copy(steep.at[q], slopes.at[n], sem_slopes.at[n]),
                    pltpu.make_async_copy(
                        tokens.at[pl.ds(q * 4, 4)], rows.at[pl.ds(n * 4, 4)], sem_rows.at[n]
                    ),
                )
            )
            for load in loads[n]:
                load.start()

        def table_step(n):
            for load in loads[n]:
                load.wait()
            product = dot_plain(slopes[n], rows[pl.ds(n * 4, 4)].reshape(8 * BLOCK, D))
            if n:
                table_grad[...] += product
            else:
                table_grad[...] = begun[0][...] + product if begun else product

        hooks = [lambda: table_step(0), lambda: table_step(1)]
    give_start(layer, sources, landed, give_sems)
    after = grad[...] + norm_back(x[...], row_sum(part, r1, s, r2, (e, f), (g, h), hooks[0]))
    g_new[...] = after
    everyone[z * 2 + core] = after.astype(BF)
    row_gather(everyone, (a, b), (c, d), hooks[1])
    give_finish(layer, sources, landed, sums, give_sems)


def next_grad(layer, part, x, grad, sources, table_parts=(), steep=None, tokens=None, begun=None):
    args, outs, scratch = [], [], []
    if table_parts:
        args = [steep, tokens] + ([] if begun is None else [begun])
        outs = [jax.ShapeDtypeStruct((steep.shape[1], D), F32)]
        scratch = [
            pltpu.VMEM((2, *steep.shape[1:]), BF),
            pltpu.VMEM((8, *tokens.shape[1:]), BF),
            pltpu.SemaphoreType.DMA((2,)),
            pltpu.SemaphoreType.DMA((2,)),
        ]
    specs = [VMEM_SPEC] * (3 + len(sources)) + [pl.BlockSpec(memory_space=pl.ANY)] * 2 + [VMEM_SPEC]
    return kernel_call(
        functools.partial(backward_body, layer, table_parts),
        [jax.ShapeDtypeStruct((8, BLOCK, D), BF), jax.ShapeDtypeStruct((BLOCK, D), F32)]
        + [jax.ShapeDtypeStruct(a.shape, F32) for a in sources]
        + outs,
        (part, x, grad, *sources, *args),
        give_scratch(sources) + SUM_SCRATCH + GATHER_SCRATCH + scratch,
        20 + layer,
        in_specs=specs[: 3 + len(sources) + len(args)],
    )


def offset(i):
    at = lax.rem(jnp.int32(i) * 5, 16)
    return lax.div(at, 4), lax.rem(at, 4)


def chip(i, sign):
    y, _, z = where_am_i()
    dy, dz = offset(i)
    return lax.rem(y + sign * dy + 4, 4), lax.rem(z + sign * dz + 4, 4)


def plane_peers(both_cores):
    y, core, z = where_am_i()
    found = [{"co": 1 - core}]
    for i in range(1, 16):
        for c in (core, 1 - core) if both_cores else (core,):
            found.append({**at_chip(*chip(i, 1)), "co": c})
    return found


def remote(src, dst, send_sem, recv_sem, device):
    return pltpu.make_async_remote_copy(
        src_ref=src,
        dst_ref=dst,
        send_sem=send_sem,
        recv_sem=recv_sem,
        device_id=device,
        device_id_type=MESH_ID,
    )


def core_rows(core):
    return pl.ds(pl.multiple_of(core * BLOCK, BLOCK), BLOCK)


def plane_collect(everyone, sems, on_chip):
    y, core, z = where_am_i()
    a, b, c, d = sems
    own = everyone.at[y * 4 + z, core_rows(core)]

    def direct(i):
        return remote(own, own, a.at[i], b.at[i], at_chip(*chip(i, 1)))

    def across(i):
        yy, zz = chip(i, -1)
        came = everyone.at[yy * 4 + zz, core_rows(core)]
        return remote(came, came, c.at[i], d.at[i], {"co": 1 - core})

    across(0).start()

    @pl.loop(1, 16)
    def _(i):
        direct(i).start()

    def use(i):
        across(i).wait_recv()
        yy, zz = chip(i, -1)
        on_chip(i, yy * 4 + zz)

    direct(1).wait_recv()
    across(1).start()
    use(0)

    @pl.loop(2, 16)
    def _(i):
        direct(i).wait_recv()
        across(i).start()
        use(i - 1)

    use(15)

    @pl.loop(1, 16)
    def _(i):
        direct(i).wait_send()
        across(i).wait_send()

    across(0).wait_send()


COLLECT_SEMS = sem_pairs(16, 16)


def plane_total(group, between, keep, other, r1, s, r2, sems):
    y, core, z = where_am_i()
    a, b, c, d = sems

    def pair(i):
        return remote(other.at[i], r1.at[i], a.at[i], b.at[i], {"co": 1 - core})

    def away(i):
        return remote(s.at[i], r2.at[i], c.at[i], d.at[i], at_chip(*chip(i, 1)))

    def make(i):
        yy, zz = chip(i, 1)
        part = group(yy * 4 + zz)
        low, high = part[:, :BLOCK], part[:, BLOCK:]
        keep[i] = jnp.where(core == 0, low, high).astype(BF)
        other[i] = jnp.where(core == 0, high, low).astype(BF)
        pair(i).start()

    def forward(i):
        pair(i).wait_recv()
        s[i] = (keep[i].astype(F32) + r1[i].astype(F32)).astype(BF)
        away(i).start()

    make(1)

    @pl.loop(2, 16)
    def _(i):
        make(i)
        forward(i - 1)

    forward(15)
    make(0)
    between()
    pair(0).wait_recv()
    total = keep[0].astype(F32) + r1[0].astype(F32)

    def add(i, total):
        away(i).wait_recv()
        return total + r2[i].astype(F32)

    total = lax.fori_loop(1, 16, add, total)

    @pl.loop(1, 16)
    def _(i):
        pair(i).wait_send()
        away(i).wait_send()

    pair(0).wait_send()
    return total


TOTAL_SCRATCH = [pltpu.VMEM((16, D, BLOCK), BF) for _ in range(5)] + sem_pairs(16, 16)


def vocab_rows(v, rows):
    return v * rows + lax.broadcasted_iota(jnp.int32, (rows, 1), 0)


def onehot_into(place, ids):
    rows = place.shape[0]

    @pl.loop(0, rows // 128)
    def _(v):
        hit = vocab_rows(v, 128) == ids
        place[pl.ds(pl.multiple_of(v * 128, 128), 128), :] = jnp.where(hit, 1.0, 0.0).astype(BF)


def embed_body(table, ids, x, everyone, hot, keep, other, r1, s, r2, e, f, g, h, a, b, c, d):
    y, core, z = where_am_i()
    greet(plane_peers(False))

    def group(c):
        onehot_into(hot, ids[c])
        return jnp.dot(table[...], hot[...], preferred_element_type=F32)

    total = plane_total(group, lambda: None, keep, other, r1, s, r2, (e, f, g, h))
    rows = jnp.transpose(total)
    x[...] = rows
    everyone[z * 2 + core] = normed_rows(rows)[0].astype(BF)
    row_gather(everyone, (a, b), (c, d))


def embedded(table, ids):
    return kernel_call(
        embed_body,
        [jax.ShapeDtypeStruct((BLOCK, D), F32), jax.ShapeDtypeStruct((8, BLOCK, D), BF)],
        (table, ids),
        [pltpu.VMEM((table.shape[1], 2 * BLOCK), BF)] + TOTAL_SCRATCH + GATHER_SCRATCH,
        7,
    )


def lse_body(
    vocab, part, x, shift, gains, head, targets,
    x_new, everyone, probs, stats, joined, logits, came, r1, s, r2, *sems,
):
    y, core, z = where_am_i()
    greet(plane_peers(True))
    here = y * 4 + z
    a, b, c, d = sems[8:]
    after = x[...] + row_sum(part, r1, s, r2, sems[0:2], sems[2:4]) + shift[0:1]
    x_new[...] = after
    everyone[here, core_rows(core)] = (
        normed_rows(after)[0] * gains[0:1] + gains[1:2]
    ).astype(BF)
    tall = head.shape[0]

    def stat_copy(i, flip, where):
        device = {**at_chip(*chip(i, -1)), "co": core if flip == 0 else 1 - core}
        to = core if flip == 0 else 1 - core
        return remote(
            stats.at[where, to], came.at[2 * i + flip], a.at[2 * i + flip], b.at[2 * i + flip], device
        )

    def on_chip(i, where):
        logits[...] = dot_cols(head[...], everyone[where])
        wanted = targets[where]

        def highest(v, top):
            rows = pl.ds(pl.multiple_of(v * 128, 128), 128)
            value = jnp.where(vocab_rows(v, 128) < vocab, logits[rows, :], NEG_BIG)
            logits[rows, :] = value
            return jnp.maximum(top, jnp.max(value.reshape(16, 8, 2 * BLOCK), 0))

        top = lax.fori_loop(0, tall // 128, highest, jnp.full((8, 2 * BLOCK), NEG_BIG, F32))
        top = jnp.max(top, 0, keepdims=True)

        def summed(v, carry):
            rows = pl.ds(pl.multiple_of(v * 128, 128), 128)
            value = logits[rows, :]
            expo = jnp.exp(value - top)
            probs[where, rows, :] = expo.astype(BF)
            hit = jnp.where(vocab_rows(v, 128) == wanted, value, 0.0)
            return (
                carry[0] + jnp.sum(expo.reshape(16, 8, 2 * BLOCK), 0),
                carry[1] + jnp.sum(hit.reshape(16, 8, 2 * BLOCK), 0),
            )

        zero = jnp.zeros((8, 2 * BLOCK), F32)
        total, target = lax.fori_loop(0, tall // 128, summed, (zero, zero))
        found = jnp.concatenate(
            [
                top,
                jnp.sum(total, 0, keepdims=True),
                jnp.sum(target, 0, keepdims=True),
                jnp.zeros((5, 2 * BLOCK), F32),
            ],
            0,
        )
        stats[where, 0] = found[:, :BLOCK]
        stats[where, 1] = found[:, BLOCK:]
        if isinstance(i, int) and i == 0:
            came[0] = stats[where, core]
        else:
            stat_copy(i, 0, where).start()
        stat_copy(i, 1, where).start()

    plane_collect(everyone, sems[4:8], on_chip)

    @pl.loop(1, 16)
    def _(i):
        stat_copy(i, 0, here).wait()
        stat_copy(i, 1, here).wait()

    stat_copy(0, 1, here).wait()
    top = jnp.max(came[:, 0, :], 0, keepdims=True)
    total = jnp.sum(came[:, 1, :] * jnp.exp(came[:, 0, :] - top), 0, keepdims=True)
    target = jnp.sum(came[:, 2, :], 0, keepdims=True)
    lse = top + jnp.log(total)
    joined[here, core] = jnp.concatenate([lse, lse - target, jnp.zeros((6, BLOCK), F32)], 0)
    mine = joined.at[here, core]

    def lse_copy(i, flip):
        device = {**at_chip(*chip(i, 1)), "co": core if flip == 0 else 1 - core}
        return remote(mine, mine, c.at[2 * i + flip], d.at[2 * i + flip], device)

    lse_copy(0, 1).start()

    @pl.loop(1, 16)
    def _(i):
        lse_copy(i, 0).start()
        lse_copy(i, 1).start()

    @pl.loop(1, 16)
    def _(i):
        lse_copy(i, 0).wait()
        lse_copy(i, 1).wait()

    lse_copy(0, 1).wait()


def last_and_lse(vocab, part, x, shift, gains, head, targets):
    tall = head.shape[0]
    return kernel_call(
        functools.partial(lse_body, vocab),
        [
            jax.ShapeDtypeStruct((BLOCK, D), F32),
            jax.ShapeDtypeStruct((16, 2 * BLOCK, D), BF),
            jax.ShapeDtypeStruct((16, tall, 2 * BLOCK), BF),
            jax.ShapeDtypeStruct((16, 2, 8, BLOCK), F32),
            jax.ShapeDtypeStruct((16, 2, 8, BLOCK), F32),
        ],
        (part, x, shift, gains, head, targets),
        [pltpu.VMEM((tall, 2 * BLOCK), F32), pltpu.VMEM((32, 8, BLOCK), F32)]
        + SUM_SCRATCH
        + COLLECT_SEMS
        + sem_pairs(32, 32),
        8,
        56,
    )


def loss_back_body(
    probs, stats, joined, targets, coefs, head_t, x, gains,
    steep, row_all, grad, grad_gains, slopes, keep, other, r1, s, r2, *sems,
):
    y, core, z = where_am_i()
    greet(plane_peers(False))
    tall = head_t.shape[1]
    written = pltpu.make_async_copy(slopes, steep, sems[8])

    def group(c):
        def row(ref):
            return jnp.concatenate([ref[c, 0, 0:1, :], ref[c, 1, 0:1, :]], 1)

        coef, wanted = coefs[c], targets[c]
        scale = jnp.exp(row(stats) - row(joined)) * coef
        lanes = pl.ds(pl.multiple_of(lax.rem(c, 4) * (2 * BLOCK), 2 * BLOCK), 2 * BLOCK)

        @pl.loop(0, tall // 128)
        def _(v):
            rows = pl.ds(pl.multiple_of(v * 128, 128), 128)
            hit = jnp.where(vocab_rows(v, 128) == wanted, coef, 0.0)
            slopes[lax.div(c, 4), rows, lanes] = (
                probs[c, rows, :].astype(F32) * scale - hit
            ).astype(BF)

        return jnp.dot(
            head_t[...], slopes[lax.div(c, 4), :, lanes], preferred_element_type=F32
        )

    total = plane_total(group, lambda: written.start(), keep, other, r1, s, r2, sems[:4])
    normed_grad = jnp.transpose(total)
    hat, _ = normed_rows(x[...])
    grad_gains[...] = jnp.concatenate(
        [
            jnp.sum(normed_grad * hat, 0, keepdims=True),
            jnp.sum(normed_grad, 0, keepdims=True),
            jnp.zeros((6, D), F32),
        ],
        0,
    )
    after = norm_back(x[...], normed_grad * gains[0:1])
    grad[...] = after
    row_all[z * 2 + core] = after.astype(BF)
    row_gather(row_all, sems[4:6], sems[6:8])
    written.wait()


def loss_back(probs, stats, joined, targets, coefs, head_t, x, gains):
    tall = head_t.shape[1]
    return kernel_call(
        loss_back_body,
        [
            jax.ShapeDtypeStruct((4, tall, 8 * BLOCK), BF),
            jax.ShapeDtypeStruct((8, BLOCK, D), BF),
            jax.ShapeDtypeStruct((BLOCK, D), F32),
            jax.ShapeDtypeStruct((8, D), F32),
        ],
        (probs, stats, joined, targets, coefs, head_t, x, gains),
        [pltpu.VMEM((4, tall, 8 * BLOCK), BF)]
        + TOTAL_SCRATCH
        + GATHER_SCRATCH
        + [pltpu.SemaphoreType.DMA],
        9,
        56,
        out_specs=[pl.BlockSpec(memory_space=pl.ANY)] + [VMEM_SPEC] * 3,
    )


def lowest_body(layer, part, x, grad, ids, *refs):
    sources, grad_embed, sums, landed, give_sems = (
        refs[:2], refs[2], refs[3:5], refs[5:7], refs[7:11],
    )
    r1, s, r2, e, f, g, h, everyone, hot = refs[11:20]
    y, core, z = where_am_i()
    greet(plane_peers(False) + column_others())
    give_start(layer, sources, landed, give_sems)
    after = grad[...] + norm_back(x[...], row_sum(part, r1, s, r2, (e, f), (g, h)))
    everyone[y * 4 + z, core_rows(core)] = after.astype(BF)
    grad_embed[...] = jnp.zeros(grad_embed.shape, F32)

    def on_chip(i, where):
        onehot_into(hot, ids[where])
        grad_embed[...] += jnp.dot(hot[...], everyone[where], preferred_element_type=F32)

    plane_collect(everyone, refs[20:], on_chip)
    give_finish(layer, sources, landed, sums, give_sems)


def lowest_grad(layer, part, x, grad, ids, sources, tall):
    return kernel_call(
        functools.partial(lowest_body, layer),
        [jax.ShapeDtypeStruct((tall, D), F32)]
        + [jax.ShapeDtypeStruct(a.shape, F32) for a in sources],
        (part, x, grad, ids, *sources),
        give_scratch(sources)
        + SUM_SCRATCH
        + [pltpu.VMEM((16, 2 * BLOCK, D), BF), pltpu.VMEM((tall, 2 * BLOCK), BF)]
        + COLLECT_SEMS,
        6,
        56,
    )


def replicas_peers():
    x = lax.axis_index("xx")
    return [(lax.rem(x + k, 4), {"xx": lax.rem(x + k, 4)}) for k in FAR]


def replicas_exchange(block, everyone, a, b):
    x = lax.axis_index("xx")
    copies = [
        send(block, everyone.at[x], (a, b), i, device)
        for i, (_, device) in enumerate(replicas_peers())
    ]
    return copies


def features_body(layer, vocab, block, err, *refs):
    sources, everyone, places, ordered = refs[:2], refs[2], refs[3:5], refs[5]
    mixed, own_sem, err_sem, sems = refs[6], refs[7], refs[8], refs[9:]
    load = pltpu.make_async_copy(err, mixed, err_sem)
    load.start()
    greet([device for _, device in replicas_peers()] + pair_peer() + column_peers())
    copies = replicas_exchange(block, everyone, *sems[:2])
    own = pltpu.make_async_copy(block, everyone.at[lax.axis_index("xx")], own_sem)
    own.start()
    take_start(layer, sources, places, sems[2:])
    load.wait()

    def put_rows(start, count):
        for b in range(2):
            for tile in range(TILES):
                far = pl.ds(start * (2 * TILES) + 2 * tile + b, count, stride=2 * TILES)
                ordered[b, pl.ds(start, count), pl.ds(tile * 128, 128)] = mixed[far, :]

    whole = vocab // CHUNK * CHUNK
    ordered[:, pl.ds(whole, ordered.shape[1] - whole), :] = jnp.zeros(
        (2, ordered.shape[1] - whole, D), F32
    )

    @pl.loop(0, vocab // CHUNK)
    def _(c):
        put_rows(pl.multiple_of(c * CHUNK, CHUNK), CHUNK)

    put_rows(whole, vocab - whole)
    own.wait()
    for copy in copies:
        copy.wait()
    take_finish(layer, sources, places, sems[2:])


def all_features(block, layer, sources, err, vocab, tall):
    some = pl.BlockSpec(memory_space=pl.ANY)
    return kernel_call(
        functools.partial(features_body, layer, vocab),
        [jax.ShapeDtypeStruct((4, *block.shape), block.dtype)]
        + [jax.ShapeDtypeStruct(a.shape, a.dtype) for a in sources]
        + [jax.ShapeDtypeStruct((2, tall, D), F32)],
        (block, err, *sources),
        [pltpu.VMEM(err.shape, F32), pltpu.SemaphoreType.DMA, pltpu.SemaphoreType.DMA]
        + sem_pairs(3)
        + take_scratch(2),
        31,
        in_specs=[some] * 4,
        out_specs=[some] * 3 + [VMEM_SPEC],
    )


def halves(values):
    high = values.astype(BF)
    return high, (values - high.astype(F32)).astype(BF)


def short_dot(short, tall, contract):
    high, low = halves(tall)
    both = jnp.concatenate(halves(short), 0)
    first = lax.dot_general(both, high, (contract, ((), ())), preferred_element_type=F32)
    second = lax.dot_general(both, low, (contract, ((), ())), preferred_element_type=F32)
    return first[:RANK] + first[RANK:] + second[:RANK]


def outer_dot(left, right):
    (a, b), (c, d) = halves(left), halves(right)
    return dot_rows(jnp.concatenate([a, b, a], 0), jnp.concatenate([c, c, d], 0))


def factor_places(cols, rows, vocab):
    def up(n):
        return -(-n // 128) * 128

    half = max(up(cols) + up(vocab), up(rows) + up(vocab))
    return half, ((0, 0, cols), (1, 0, rows), (0, up(cols), vocab), (1, up(rows), vocab))


def compress_body(
    vocab, g_embed, g_head, err, m_in, m_back, q_in, q_back, q_embed, q_head, bias, vectors,
    m_embed, m_head, basis, own, sums, bias_sum, vector_sum,
    left, left_came, bias_came, joint, joint_came, work, vec_came, vec_mine, vec_sums, vec_all,
    *sems,
):
    y, core, z = where_am_i()
    x = lax.axis_index("xx")
    me = y * 8 + core * 4 + z
    peers = []
    for k in range(1, 32):
        p = lax.rem(me + k, 32)
        peers.append((p, {**at_chip(p // 8, lax.rem(p, 4)), "co": lax.rem(p // 4, 2)}))
    greet([device for _, device in peers] + [device for _, device in replicas_peers()])
    pairs = [(sems[2 * n], sems[2 * n + 1]) for n in range(len(sems) // 2)]
    vec_first = [
        send(vectors.at[p], vec_came.at[me], pairs[0], k, device)
        for k, (p, device) in enumerate(peers)
    ]
    vec_came[me] = vectors[me]

    half, places = factor_places(m_in.shape[0], m_back.shape[0], vocab)
    m_embed[...] = g_embed[...] + err[0]
    m_head[...] = g_head[...] + err[1]
    blocks = (m_in, m_back, m_embed, m_head)
    for b, (factor, block) in enumerate(zip((q_in, q_back, q_embed, q_head), blocks)):
        left[b] = short_dot(factor[...], block[...], ((1,), (0,)))

    for copy in vec_first:
        copy.wait_recv()
    vec_mine[...] = jnp.sum(vec_came[...], 0)
    second = []
    for n, (src, dst) in enumerate(
        ((left, left_came), (bias, bias_came), (vec_mine, vec_sums))
    ):
        second += replicas_exchange(src, dst, *pairs[1 + n])
    left_came[x] = left[...]
    bias_came[x] = bias[...]
    vec_sums[x] = vec_mine[...]
    for copy in second:
        copy.wait()
    bias_sum[...] = jnp.sum(bias_came[...], 0)
    vec_all[me] = jnp.sum(vec_sums[...], 0)
    mine = vec_all.at[me]
    third = [send(mine, mine, pairs[4], k, device) for k, (_, device) in enumerate(peers)]
    work[...] = jnp.sum(left_came[...], 0)
    order = lax.broadcasted_iota(jnp.int32, (1, RANK, 1), 1)
    for index in range(RANK):
        columns = work[...]
        one = columns[:, index : index + 1, :]
        one = one * lax.rsqrt(jnp.sum(one * one, -1, keepdims=True) + 1e-30)
        shares = jnp.sum(columns * one, -1, keepdims=True)
        work[...] = jnp.where(order > index, columns - shares * one, columns)
        basis[:, index : index + 1, :] = one

    own[...] = jnp.zeros(own.shape, F32)
    for b, block in enumerate(blocks):
        at = pl.ds(places[b][1], block.shape[0])
        own[places[b][0], :, at] = short_dot(basis[b], block[...], ((1,), (1,)))

    joint[...] = own[...].reshape(joint.shape).astype(BF)
    fourth = replicas_exchange(joint, joint_came, *pairs[5])
    joint_came[x] = joint[...]
    for copy in fourth:
        copy.wait()
    total = jnp.sum(joint_came[...].astype(F32), 0)
    sums[...] = total.reshape(sums.shape)
    for copy in vec_first:
        copy.wait_send()
    for copy in third:
        copy.wait()
    vector_sum[...] = vec_all[...]


def compressed(vocab, g_embed, g_head, err, m_in, m_back, facs, bias, vectors):
    half, _ = factor_places(m_in.shape[0], m_back.shape[0], vocab)
    tall = g_embed.shape
    return kernel_call(
        functools.partial(compress_body, vocab),
        [
            jax.ShapeDtypeStruct(s, F32)
            for s in (tall, tall, (4, 8, D), (2, 8, half), (2, 8, half), bias.shape, vectors.shape)
        ],
        (g_embed, g_head, err, m_in, m_back, *facs, bias, vectors),
        [
            pltpu.VMEM((4, 8, D), F32),
            pltpu.VMEM((4, 4, 8, D), F32),
            pltpu.VMEM((4, *bias.shape), F32),
            pltpu.VMEM((16, half), BF),
            pltpu.VMEM((4, 16, half), BF),
            pltpu.VMEM((4, 8, D), F32),
            pltpu.VMEM(vectors.shape, F32),
            pltpu.VMEM(vectors.shape[1:], F32),
            pltpu.VMEM((4, *vectors.shape[1:]), F32),
            pltpu.VMEM(vectors.shape, F32),
        ]
        + sem_pairs(31, 3, 3, 3, 31, 3),
        30,
        56,
    )


def ema_decay():
    return min(0.999, (1.0 + STEP) / (10.0 + STEP))


def stepped(rate, weight, moment, average, grad):
    decay = ema_decay()
    new_moment = MOMENTUM * moment + (1.0 - MOMENTUM) * grad
    new_weight = weight - rate * new_moment
    return new_weight, new_moment, decay * average + (1.0 - decay) * new_weight


def update_body(
    vocab, rate_layer, rate_tables, m_embed, m_head, m_in, m_back, basis, own, sums,
    in_w, in_m, in_e, back_w, back_m, back_e, tab_w, tab_m, tab_e,
    err_tab, err_in, err_back, o_in_w, o_in_m, o_in_e, o_back_w, o_back_m, o_back_e,
    o_tab_w, o_tab_m, o_tab_e,
):
    x = lax.axis_index("xx")
    half, places = factor_places(m_in.shape[0], m_back.shape[0], vocab)
    whole = vocab // CHUNK
    own_cols = pl.ds(pl.multiple_of(x * 128, 128), 128)

    def part(ref, b, start, count):
        return ref[places[b][0], :, pl.ds(pl.multiple_of(places[b][1] + start, 128), count)]

    def table_rows(start, count):
        for b, matrix in ((2, m_embed), (3, m_head)):
            span = CHUNK
            product = outer_dot(part(own, b, start, span), basis[b])
            for tile in range(TILES):
                far = pl.ds(start * (2 * TILES) + 2 * tile + b - 2, count, stride=2 * TILES)
                err_tab[far, :] = (
                    matrix[pl.ds(start, count), pl.ds(tile * 128, 128)]
                    - product[:count, tile * 128 : (tile + 1) * 128]
                )
            reduced = outer_dot(part(sums, b, start, span), basis[b, :, own_cols])
            near = pl.ds(start * 2 + b - 2, count, stride=2)
            new = stepped(
                rate_tables[b - 2], tab_w[near, :], tab_m[near, :], tab_e[near, :], reduced[:count]
            )
            for out, value in zip((o_tab_w, o_tab_m, o_tab_e), new):
                out[near, :] = value

    @pl.loop(0, whole)
    def _(c):
        table_rows(pl.multiple_of(c * CHUNK, CHUNK), CHUNK)

    if vocab > whole * CHUNK:
        table_rows(whole * CHUNK, vocab - whole * CHUNK)

    layer_parts = (
        (m_in, err_in, (in_w, in_m, in_e), (o_in_w, o_in_m, o_in_e)),
        (m_back, err_back, (back_w, back_m, back_e), (o_back_w, o_back_m, o_back_e)),
    )
    for b, (matrix, err, olds, outs) in enumerate(layer_parts):
        for start in range(0, matrix.shape[0], CHUNK):
            count = min(CHUNK, matrix.shape[0] - start)
            at = pl.ds(start, count)
            lanes = pl.ds(places[b][1] + start, count)
            err[at, :] = matrix[at, :] - outer_dot(own[places[b][0], :, lanes], basis[b])
            reduced = outer_dot(sums[places[b][0], :, lanes], basis[b])
            new = stepped(rate_layer, *[old[at, :] for old in olds], reduced)
            for out, value in zip(outs, new):
                out[at, :] = value


def updated(vocab, rates, m_tables, m_in, m_back, basis, own, sums, params, err_shape):
    outs = [err_shape, m_in.shape, m_back.shape] + [a.shape for a in params]
    return kernel_call(
        functools.partial(update_body, vocab, rates[0], rates[1]),
        [jax.ShapeDtypeStruct(a, F32) for a in outs],
        (*m_tables, m_in, m_back, basis, own, sums, *params),
        [],
        None,
        56,
    )


def rotary_tables():
    half_rot = ROT // 2
    inverse = 10000.0 ** (-jnp.arange(half_rot, dtype=F32) * (2.0 / ROT))
    angles = jnp.arange(LENGTH, dtype=F32)[:, None] * inverse[None, :]
    return (jnp.cos(angles), jnp.sin(angles))


def rotate(heads, cosine, sine):
    half_rot = ROT // 2
    first = heads[..., :half_rot]
    second = heads[..., half_rot:ROT]
    return jnp.concatenate(
        [first * cosine - second * sine, second * cosine + first * sine, heads[..., ROT:]], -1
    )


ATT_BLOCK = 512


def causal(start, stop):
    rows = start + lax.broadcasted_iota(jnp.int32, (stop - start, stop), 0)
    return rows >= lax.broadcasted_iota(jnp.int32, (stop - start, stop), 1)


def attention_forward(q_rot, k_rot, v_val):
    outputs, all_lse = [], []
    for start in range(0, LENGTH, ATT_BLOCK):
        stop = start + ATT_BLOCK
        scores = dot_cols(q_rot[start:stop], k_rot[:stop]) * HEAD ** (-0.5)
        scores = jnp.where(causal(start, stop), scores, NEG_BIG)
        top = jnp.max(scores, -1, keepdims=True)
        expo = jnp.exp(scores - top)
        total = jnp.sum(expo, -1, keepdims=True)
        probs = (expo / total).astype(BF)
        outputs.append(dot_plain(probs, v_val[:stop]))
        all_lse.append(top + jnp.log(total))
    return (jnp.concatenate(outputs, 0), jnp.concatenate(all_lse, 0))


def attention_backward(q_rot, k_rot, v_val, lse, grad_out):
    scale = HEAD ** (-0.5)
    grad_query, grad_key, grad_value = [], 0.0, 0.0
    for start in range(0, LENGTH, ATT_BLOCK):
        stop = start + ATT_BLOCK
        spare = ((0, LENGTH - stop), (0, 0))
        scores = dot_cols(q_rot[start:stop], k_rot[:stop]) * scale
        probs = jnp.where(causal(start, stop), jnp.exp(scores - lse[start:stop]), 0.0)
        grad_probs = dot_cols(grad_out[start:stop], v_val[:stop])
        grad_scores = (
            probs * (grad_probs - jnp.sum(grad_probs * probs, -1, keepdims=True))
        ).astype(BF)
        grad_query.append(dot_plain(grad_scores, k_rot[:stop]) * scale)
        grad_key = grad_key + jnp.pad(dot_rows(grad_scores, q_rot[start:stop]), spare) * scale
        grad_value = grad_value + jnp.pad(
            dot_rows(probs.astype(BF), grad_out[start:stop]), spare
        )
    return (jnp.concatenate(grad_query, 0), grad_key, grad_value)


def block_forward(hat, weights, cosine, sine):
    w_all, bias, vector = weights
    w_cols, w_rows = w_all[: bias.shape[0]], w_all[bias.shape[0] :]
    wide = hat.astype(F32)
    first_in = (wide * vector[0] + vector[1]).astype(BF)
    second_in = (wide * vector[2] + vector[3]).astype(BF)
    qkv = dot_cols(first_in, w_cols[: 3 * HEAD]) + bias[: 3 * HEAD]
    up_val = dot_cols(second_in, w_cols[3 * HEAD :]) + bias[3 * HEAD :]
    q_rot = rotate(qkv[:, :HEAD], cosine, sine).astype(BF)
    k_rot = rotate(qkv[:, HEAD : 2 * HEAD], cosine, sine).astype(BF)
    v_val = qkv[:, 2 * HEAD :].astype(BF)
    attended, lse = attention_forward(q_rot, k_rot, v_val)
    attended = attended.astype(BF)
    hidden = jax.nn.gelu(up_val, approximate=False).astype(BF)
    branch = dot_plain(attended, w_rows[:HEAD]) + dot_plain(hidden, w_rows[HEAD:])
    return (
        branch.astype(BF),
        (hat, first_in, second_in, q_rot, k_rot, v_val, lse, attended, up_val, hidden),
    )


def gelu_exact(values):
    return jax.nn.gelu(values, approximate=False)


def block_backward(grad_low, kept, weights, cosine, sine):
    w_all, bias, vector = weights
    w_cols, w_rows = w_all[: bias.shape[0]], w_all[bias.shape[0] :]
    hat, first_in, second_in, q_rot, k_rot, v_val, lse, attended, up_val, hidden = kept
    grad_att = dot_cols(grad_low, w_rows[:HEAD]).astype(BF)
    grad_hidden = dot_cols(grad_low, w_rows[HEAD:])
    grad_up = jax.vjp(gelu_exact, up_val)[1](grad_hidden)[0].astype(BF)
    grad_query, grad_key, grad_value = attention_backward(q_rot, k_rot, v_val, lse, grad_att)
    grad_query = rotate(grad_query, cosine, -sine)
    grad_key = rotate(grad_key, cosine, -sine)
    grad_qkv = jnp.concatenate([grad_query, grad_key, grad_value], 1).astype(BF)
    grad_weights = jnp.concatenate(
        [
            dot_rows(grad_qkv, first_in).astype(BF),
            dot_rows(grad_up, second_in).astype(BF),
            dot_rows(attended, grad_low).astype(BF),
            dot_rows(hidden, grad_low).astype(BF),
        ]
    )
    grad_bias = jnp.concatenate(
        [jnp.sum(grad_qkv.astype(F32), 0), jnp.sum(grad_up.astype(F32), 0)]
    )
    grad_first = dot_plain(grad_qkv, w_cols[: 3 * HEAD])
    grad_second = dot_plain(grad_up, w_cols[3 * HEAD :])
    wide = hat.astype(F32)
    grad_norms = jnp.stack(
        [
            jnp.sum(grad_first * wide, 0),
            jnp.sum(grad_first, 0),
            jnp.sum(grad_second * wide, 0),
            jnp.sum(grad_second, 0),
        ]
    )
    grad_hat = grad_first * vector[0] + grad_second * vector[2]
    return (grad_hat.astype(BF), (grad_weights, grad_bias, grad_norms))


def on_device(
    tokens,
    groups,
    counts,
    domain,
    w_in,
    w_back,
    tables,
    b_in,
    vecs,
    final_norm,
    w_in_mom,
    w_back_mom,
    tables_mom,
    b_in_mom,
    vecs_mom,
    final_mom,
    w_in_ema,
    w_back_ema,
    tables_ema,
    b_in_ema,
    vecs_ema,
    final_ema,
    w_in_err,
    w_back_err,
    tables_err,
    w_in_fac,
    w_back_fac,
    tables_fac,
):
    y, core, z = where_am_i()
    replica = lax.axis_index("xx")
    section = lax.axis_index("yl") * 2 + core
    vocab_part = section * 8 + lax.axis_index("yh") * 4 + z
    shard = core * 4 + z
    seq_rep = tokens.shape[0]
    row_total = seq_rep * LENGTH
    vocab_shard = tables.shape[1]
    own_cols = tables.shape[2]
    cosine, sine = rotary_tables()

    seq_index = jnp.arange(groups.shape[0], dtype=jnp.int32)
    live = seq_index % seq_rep < counts[seq_index // seq_rep]
    domain_hit = groups[:, None] == jnp.arange(domain.shape[0], dtype=jnp.int32)[None, :]
    seq_weight = jnp.where(live, jnp.sum(jnp.where(domain_hit, domain[None, :], 0.0), 1), 0.0)
    weight_total = jnp.sum(seq_weight)
    own_weight = lax.dynamic_slice_in_dim(seq_weight, replica * seq_rep, seq_rep, 0)
    token_ids = tokens[:, :LENGTH].reshape(-1)
    target_ids = tokens[:, 1:].reshape(-1)

    pad_ids = -vocab_shard % 128
    tall = vocab_shard + pad_ids
    short = jnp.pad(
        jnp.transpose(tables.astype(BF), (0, 2, 1)), ((0, 0), (0, 0), (0, pad_ids))
    )
    small = jnp.concatenate(
        [
            jnp.pad(vecs[0], ((0, 2), (0, 0))),
            jnp.pad(b_in, ((0, 7), (0, D - b_in.shape[1]))),
        ]
    )
    sources = (jnp.concatenate([w_in[0].T.astype(BF), w_back[0].astype(BF)]), small)
    err = jnp.transpose(
        tables_err.reshape(2, vocab_shard, D // 128, 128), (1, 2, 0, 3)
    ).reshape(-1, 128)
    embed_t, *packs_0, err = all_features(short[0], 0, sources, err, vocab_shard, tall)
    packs = {0: packs_0}
    head_t = lax.all_gather(short[1], "xx", axis=0, tiled=True)

    def own_ids(ids):
        local = ids - vocab_part * vocab_shard
        inside = (local >= 0) & (local < vocab_shard)
        return jnp.where(inside, local, -1).reshape(16, 1, 2 * BLOCK)

    own_tokens, own_targets = own_ids(token_ids), own_ids(target_ids)
    x, hat = embedded(embed_t.reshape(D, tall), own_tokens)
    head = jnp.transpose(head_t)

    gains = jnp.pad(final_norm, ((0, 6), (0, 0)))
    weights, kept, before = [], [], []
    for index in range(LAYERS):
        w_all, rest = packs[index]
        weights.append((w_all, rest[8, : b_in.shape[1]], rest))
        shift = jnp.broadcast_to((rest[4] + rest[5])[None], (8, D))
        before.append(x)
        branch, keep = block_forward(hat.reshape(LENGTH, D), weights[index], cosine, sine)
        kept.append(keep)
        branch = branch.reshape(8, BLOCK, D)
        if index + 1 < LAYERS:
            hat, x, *packs[index + 1] = next_hat(branch, x, shift, index + 1, sources)

    x, normed, probs, stats, joined = last_and_lse(
        vocab_shard, branch, x, shift, gains, head, own_targets
    )
    losses = joined[:, :, 1, :].reshape(seq_rep, LENGTH)
    loss_part = jnp.sum(own_weight * jnp.mean(losses, 1))
    coefs = jnp.broadcast_to(
        jnp.repeat(own_weight / (weight_total * LENGTH), 4)[:, None, None], (16, 1, 2 * BLOCK)
    )
    steep, grad_all, grad, grad_gains = loss_back(
        probs, stats, joined, own_targets, coefs, head_t, x, gains
    )
    grad_gains = grad_gains[:2]
    vector_rows = [None] * LAYERS
    grad_table = None
    returned = [None] * LAYERS
    for index in reversed(range(LAYERS)):
        outbias = jnp.sum(grad, 0)[None]
        grad_hat, (w_grad, bias_row, norm_rows) = block_backward(
            grad_all.reshape(LENGTH, D), kept[index], weights[index], cosine, sine
        )
        vector_rows[index] = jnp.concatenate([norm_rows, outbias, outbias], 0)
        given = (w_grad, jnp.pad(bias_row[None], ((0, 7), (0, D - bias_row.shape[0]))))
        grad_hat = grad_hat.reshape(8, BLOCK, D)
        if index >= LAYERS - 2:
            parts = (0, 1) if index == LAYERS - 1 else (2, 3)
            grad_all, grad, *returned[index], grad_table = next_grad(
                index, grad_hat, before[index], grad, given, parts, steep, normed, grad_table
            )
        elif index:
            grad_all, grad, *returned[index] = next_grad(
                index, grad_hat, before[index], grad, given
            )
        else:
            grad_embed, *returned[index] = lowest_grad(
                index, grad_hat, before[index], grad, own_tokens, given, tall
            )

    def of_own_layer(n):
        picked = returned[LAYERS - 1][n]
        for index in range(LAYERS - 1):
            picked = jnp.where(section == index, returned[index][n], picked)
        return picked

    loss_row = jnp.zeros((1, D), F32).at[0, 0].set(jnp.where(shard + y * 8 == 0, loss_part, 0.0))
    vectors = jnp.concatenate(vector_rows + [grad_gains, loss_row], 0)
    vectors = jnp.pad(vectors, ((0, 32 - vectors.shape[0]), (0, 0))).reshape(32, D // 128, 128)
    vectors = jnp.pad(vectors, ((0, 0), (0, 8 - D // 128), (0, 0)))
    full = of_own_layer(0)
    n_in = b_in.shape[1]
    full_in = full[:n_in] + w_in_err[0, 0].T
    full_back = full[n_in:] + w_back_err[0, 0]
    facs = (
        w_in_fac[0].T,
        w_back_fac[0].T,
        jnp.pad(tables_fac[0].T, ((0, 0), (0, pad_ids))),
        jnp.pad(tables_fac[1].T, ((0, 0), (0, pad_ids))),
    )
    m_embed, m_head, basis, own, sums, bias_sum, vector_sums = compressed(
        vocab_shard, grad_embed, grad_table, err, full_in, full_back, facs, of_own_layer(1), vectors
    )
    bias_sum = bias_sum[:1, : b_in.shape[1]]
    vector_sums = vector_sums[:, : D // 128, :].reshape(32, D)
    vec_sum = lax.dynamic_slice_in_dim(vector_sums, section * 6, 6, 0)
    final_sum = vector_sums[6 * LAYERS : 6 * LAYERS + 2]
    loss_sum = vector_sums[6 * LAYERS + 2, 0]

    def of_tables(arrays):
        return [jnp.transpose(a, (1, 0, 2)).reshape(-1, 128) for a in arrays]

    token_count = lax.axis_size("xx") * seq_rep * LENGTH
    rate_layer = 2.0 * math.sqrt(token_count)
    rate_vector = 6.0 * math.sqrt(token_count)
    rate_tables = [rate * math.sqrt(token_count * VOCAB) for rate in (50.0, 0.5)]
    params = (
        [w_in[0].T, w_in_mom[0].T, w_in_ema[0].T, w_back[0], w_back_mom[0], w_back_ema[0]]
        + of_tables((tables, tables_mom, tables_ema))
    )
    err_tab, err_in, err_back, *new = updated(
        vocab_shard, (rate_layer, rate_tables), (m_embed, m_head), full_in, full_back,
        basis, own, sums, params, (vocab_shard * 8, 128),
    )
    err_tab = jnp.transpose(
        err_tab.reshape(vocab_shard, D // 128, 2, 128), (2, 0, 1, 3)
    ).reshape(tables_err.shape)
    in_w, in_m, in_e = [a.T[None] for a in new[:3]]
    back_w, back_m, back_e = [a[None] for a in new[3:6]]
    tab_w, tab_m, tab_e = [
        jnp.transpose(a.reshape(vocab_shard, 2, own_cols), (1, 0, 2)) for a in new[6:]
    ]
    _, places = factor_places(full_in.shape[0], full_back.shape[0], vocab_shard)
    fac_in, fac_back, fac_embed, fac_head = [
        sums[half, :, at : at + width].T for half, at, width in places
    ]
    bias_w, bias_m, bias_e = stepped(rate_layer, b_in, b_in_mom, b_in_ema, bias_sum)
    vec_w, vec_m, vec_e = stepped(rate_vector, vecs, vecs_mom, vecs_ema, vec_sum[None])
    fin_w, fin_m, fin_e = stepped(rate_layer, final_norm, final_mom, final_ema, final_sum)
    return (
        loss_sum,
        weight_total,
        in_w,
        back_w,
        tab_w,
        bias_w,
        vec_w,
        fin_w,
        in_m,
        back_m,
        tab_m,
        bias_m,
        vec_m,
        fin_m,
        in_e,
        back_e,
        tab_e,
        bias_e,
        vec_e,
        fin_e,
        err_in.T[None, None],
        err_back[None, None],
        err_tab,
        fac_in[None],
        fac_back[None],
        fac_embed,
        fac_head,
    )


def solution(mesh):
    fine = Mesh(
        np.asarray(mesh.devices).reshape(2, 2, 2, 4, 4), ("yl", "co", "yh", "zz", "xx")
    )
    names = {"section": ("yl", "co"), "tensor": ("yh", "zz"), "dp": ("xx",)}

    def spec(*axes):
        return P(*[None if a is None else sum((names[n] for n in a.split()), ()) for a in axes])

    layer_in, layer_back = spec("section", None, "tensor"), spec("section", "tensor", None)
    table, bias = spec(None, "section tensor", "dp"), spec("section", "tensor")
    vector = spec("section", None, None)
    params = (layer_in, layer_back, table, bias, vector, P())
    errors = (
        spec("dp", "section", None, "tensor"),
        spec("dp", "section", "tensor", None),
        spec("dp", None, "section tensor", None),
    )
    in_specs = (
        (spec("dp", None), P(), P(), P())
        + params * 3
        + errors
        + (layer_back, layer_back, spec(None, "section tensor", None))
    )
    out_specs = (
        (P(), P())
        + params * 3
        + errors
        + (layer_back, layer_back, spec("section tensor", None), spec("section tensor", None))
    )
    return jax.shard_map(
        on_device, mesh=fine, in_specs=in_specs, out_specs=out_specs, check_vma=False
    )
```

time: 733 us -> 631 us (0.86)
  matrix products: 140 us -> 76 us
  other arithmetic: 53.5 us -> 36.8 us
  local copies, waits for them, and re-layouts: 47.6 us -> 31.3 us
    dot_general x34 -> x32, matrix products: 47.6 us -> 15.2 us  [dot_rows(): lax.dot_general(left, right, (((0,), (0,)), ((), ())), preferred_element_...]
    dot_general x34 -> x32, matrix products: 51.4 us -> 25.6 us  [dot_plain(): return jnp.dot(left, right, preferred_element_type=F32)]
    unnamed x499 -> x364, local copies, waits for them, and re-layouts: 30.1 us -> 13.6 us
    reduce_sum x4 -> x0, other arithmetic: 12.9 us -> none  [the longest x1 11.9 us: on_device(): total_local = jnp.sum(jnp.exp(logits - top_local[:, None]), 1)]
    dot_general x33 -> x32, matrix products: 40.9 us -> 35.2 us  [dot_cols(): lax.dot_general(left, right, (((1,), (1,)), ((), ())), preferred_element_...]
    pallas_call x18 -> x13, Pallas kernels: 464 us -> 459 us  [kernel_call(): pl.pallas_call(body, out_shape=out_shape, in_specs=in_specs or [VMEM_SPEC...]
  transfers between devices with their start and end apart: 1 -> 1, of which waited for: 0 -> 0; matrix products, arithmetic and copies ran while one was open for 10% -> 8% of each run, Pallas kernels for 29% -> 24%
where the time goes in v3:
time: 631 us; the launch traced here: 622 us
  Pallas kernels  459 us (73%)
  matrix products  76 us (12%)
  other arithmetic  36.8 us (6%)
  local copies, waits for them, and re-layouts  31.3 us (5%)
  between operations  19.1 us (3%)
    pallas_call x13, Pallas kernels, kernel_call(): pl.pallas_call(body, out_shape=out_shape, in_specs=in_specs or [VMEM_SPEC...  459 us
    dot_general x32, matrix products, dot_cols(): lax.dot_general(left, right, (((1,), (1,)), ((), ())), preferred_element_...  35.2 us
    dot_general x32, matrix products, dot_plain(): return jnp.dot(left, right, preferred_element_type=F32)  25.6 us
    dot_general x32, matrix products, dot_rows(): lax.dot_general(left, right, (((0,), (0,)), ((), ())), preferred_element_...  15.2 us
    unnamed x364, local copies, waits for them, and re-layouts  13.6 us
  transfers between devices with their start and end apart: 1, of which 0 were waited for; matrix products, arithmetic and copies ran while one was open for 8% of the time, Pallas kernels for 24%

profile of v3, /device:TPU:0, one launch (start us, length us, event | category | flops | bytes accessed | tf_op | source)
XLA Modules:
  0.0 622.3 jit_solution(12095867603651931877)
XLA Ops:
  7.3 1.7 convert_element_type.313
  11.6 37.5 %shard_map.475 = (bf16[4,128,1664]{2,1,0:T(8,128)(2,1)S(1)}, bf16[768,512]{1,0:T(8,128)(2,1)S(1)}, f32[16,512]{1,0:T(8,128)S(1)}, f32[2,1664,512]{2,1,0:T(8,128)}) custom-call(bf16[128,1664]{1,0:T(8,128)(2,1)S(1)} %get-tuple-element.221.block, f32[12576,128]{1,0:T(8,128)} %bitcast.302, bf16[768,512]{1,0:T(8,128)(2,1)S(1)} %pad_maximum_fusion.refs_0_, ...), custom_call_target="tpu_custom_call" | custom-call | tf_op jit(solution)/shard_map/pallas_call | solution.py:76
  50.8 46.9 %shard_map.476 = (f32[128,512]{1,0:T(8,128)S(1)}, bf16[8,128,512]{2,1,0:T(8,128)(2,1)S(1)}) custom-call(bf16[512,1664]{1,0:T(8,128)(2,1)S(1)} %bitcast.296, s32[16,1,256]{2,1,0:T(1,128)S(1)} %and_select_fusion.1.ids), custom_call_target="tpu_custom_call" | custom-call | tf_op jit(solution)/shard_map/pallas_call | solution.py:76
  103.4 3.7 multiply_convert_fusion.11
  107.9 20.7 %shard_map.477 = (bf16[8,128,512]{2,1,0:T(8,128)(2,1)S(1)}, f32[128,512]{1,0:T(8,128)S(1)}, bf16[768,512]{1,0:T(8,128)(2,1)S(1)}, f32[16,512]{1,0:T(8,128)S(1)}) custom-call(bf16[8,128,512]{2,1,0:T(8,128)(2,1)S(1)} %bitcast.294, f32[128,512]{1,0:T(8,128)S(1)} %get-tuple-element.106.x, f32[8,512]{1,0:T(8,128)S(1)} %broadcast_in_dim.188.shift, ...), custom_call_target="tpu_custom_call" | custom-call | tf_op jit(solution)/shard_map/pallas_call | solution.py:76
  134.8 3.7 multiply_convert_fusion.10
  139.3 24.5 %shard_map.478 = (bf16[8,128,512]{2,1,0:T(8,128)(2,1)S(1)}, f32[128,512]{1,0:T(8,128)S(1)}, bf16[768,512]{1,0:T(8,128)(2,1)S(1)}, f32[16,512]{1,0:T(8,128)S(1)}) custom-call(bf16[8,128,512]{2,1,0:T(8,128)(2,1)S(1)} %bitcast.295, f32[128,512]{1,0:T(8,128)S(1)} %get-tuple-element.110.x, f32[8,512]{1,0:T(8,128)S(1)} %broadcast_in_dim.190.shift, ...), custom_call_target="tpu_custom_call" | custom-call | tf_op jit(solution)/shard_map/pallas_call | solution.py:76
  170.0 3.6 multiply_convert_fusion.9
  174.4 20.9 %shard_map.479 = (bf16[8,128,512]{2,1,0:T(8,128)(2,1)S(1)}, f32[128,512]{1,0:T(8,128)S(1)}, bf16[768,512]{1,0:T(8,128)(2,1)S(1)}, f32[16,512]{1,0:T(8,128)S(1)}) custom-call(bf16[8,128,512]{2,1,0:T(8,128)(2,1)S(1)} %bitcast.293, f32[128,512]{1,0:T(8,128)S(1)} %get-tuple-element.114.x, f32[8,512]{1,0:T(8,128)S(1)} %broadcast_in_dim.192.shift, ...), custom_call_target="tpu_custom_call" | custom-call | tf_op jit(solution)/shard_map/pallas_call | solution.py:76
  212.1 1.8 convolution_convert_fusion.20
  215.2 3.7 multiply_convert_fusion.8
  221.0 3.6 copy.69.head
  225.3 68.9 %shard_map.480 = (f32[128,512]{1,0:T(8,128)}, bf16[16,256,512]{2,1,0:T(8,128)(2,1)}, bf16[16,1664,256]{2,1,0:T(8,128)(2,1)}, f32[16,2,8,128]{3,2,1,0:T(8,128)}, f32[16,2,8,128]{3,2,1,0:T(8,128)}) custom-call(bf16[8,128,512]{2,1,0:T(8,128)(2,1)} %bitcast.308, f32[128,512]{1,0:T(8,128)} %copy-done.6, f32[8,512]{1,0:T(8,128)} %broadcast_in_dim.194.shift, ...), custom_call_target="tpu_custom_call" | custom-call | tf_op jit(solution)/shard_map/pallas_call | solution.py:76
  297.0 52.7 %shard_map.481 = (bf16[4,1664,1024]{2,1,0:T(8,128)(2,1)}, bf16[8,128,512]{2,1,0:T(8,128)(2,1)}, f32[128,512]{1,0:T(8,128)}, f32[8,512]{1,0:T(8,128)}) custom-call(bf16[16,1664,256]{2,1,0:T(8,128)(2,1)} %get-tuple-element.119.probs, f32[16,2,8,128]{3,2,1,0:T(8,128)} %get-tuple-element.120.stats, f32[16,2,8,128]{3,2,1,0:T(8,128)} %get-tuple-element.121.joined, ...), custom_call_target="tpu_custom_call" | custom-call | tf_op jit(solution)/shard_map/pallas_call | solution.py:76
  364.1 23.2 %shard_map.482 = (bf16[8,128,512]{2,1,0:T(8,128)(2,1)S(1)}, f32[128,512]{1,0:T(8,128)S(1)}, f32[768,512]{1,0:T(8,128)S(1)}, f32[8,512]{1,0:T(8,128)S(1)}, f32[1664,512]{1,0:T(8,128)}) custom-call(bf16[8,128,512]{2,1,0:T(8,128)(2,1)S(1)} %bitcast.298, f32[128,512]{1,0:T(8,128)S(1)} %copy-done.7, f32[128,512]{1,0:T(8,128)S(1)} %copy-done.8, ...), custom_call_target="tpu_custom_call" | custom-call | tf_op jit(solution)/shard_map/pallas_call | solution.py:76
  400.1 25.3 %shard_map.483 = (bf16[8,128,512]{2,1,0:T(8,128)(2,1)S(1)}, f32[128,512]{1,0:T(8,128)S(1)}, f32[768,512]{1,0:T(8,128)S(1)}, f32[8,512]{1,0:T(8,128)S(1)}, f32[1664,512]{1,0:T(8,128)}) custom-call(bf16[8,128,512]{2,1,0:T(8,128)(2,1)S(1)} %bitcast.297, f32[128,512]{1,0:T(8,128)S(1)} %get-tuple-element.114.x, f32[128,512]{1,0:T(8,128)S(1)} %get-tuple-element.128.grad, ...), custom_call_target="tpu_custom_call" | custom-call | tf_op jit(solution)/shard_map/pallas_call | solution.py:76
  438.6 22.7 %shard_map.484 = (bf16[8,128,512]{2,1,0:T(8,128)(2,1)S(1)}, f32[128,512]{1,0:T(8,128)S(1)}, f32[768,512]{1,0:T(8,128)S(1)}, f32[8,512]{1,0:T(8,128)S(1)}) custom-call(bf16[8,128,512]{2,1,0:T(8,128)(2,1)S(1)} %bitcast.299, f32[128,512]{1,0:T(8,128)S(1)} %copy-done.21, f32[128,512]{1,0:T(8,128)S(1)} %get-tuple-element.131.grad, ...), custom_call_target="tpu_custom_call" | custom-call | tf_op jit(solution)/shard_map/pallas_call | solution.py:76
  470.6 2.8 fusion.146
  474.9 2.5 convert_reduce_fusion
  477.9 2.9 fusion.283
  482.5 63.6 %shard_map.485 = (f32[1664,512]{1,0:T(8,128)}, f32[768,512]{1,0:T(8,128)}, f32[8,512]{1,0:T(8,128)}) custom-call(bf16[8,128,512]{2,1,0:T(8,128)(2,1)} %bitcast.314, f32[128,512]{1,0:T(8,128)} %copy-done.19, f32[128,512]{1,0:T(8,128)} %copy-done.17, s32[16,1,256]{2,1,0:T(1,128)} %copy-done.28, bf16[768,512]{1,0:T(8,128)(2,1)} %pad_maximum_fusion.4.refs_0_, ...), custom_call_target="tpu_custom_call" | custom-call | tf_op jit(solution)/shard_map/pallas_call | solution.py:76
  546.1 2.3 select_select_fusion
  554.3 35.2 %shard_map.486 = (f32[1664,512]{1,0:T(8,128)}, f32[1664,512]{1,0:T(8,128)}, f32[4,8,512]{2,1,0:T(8,128)}, f32[2,8,2176]{2,1,0:T(8,128)}, f32[2,8,2176]{2,1,0:T(8...) custom-call(f32[1664,512]{1,0:T(8,128)} %get-tuple-element.134.g_embed, f32[1664,512]{1,0:T(8,128)} %get-tuple-element.135.g_head, ...), custom_call_target="tpu_custom_call" | custom-call | tf_op jit(solution)/shard_map/pallas_call | solution.py:76
  598.4 16.8 %shard_map.487 = (f32[12576,128]{1,0:T(8,128)}, f32[448,512]{1,0:T(8,128)}, f32[320,512]{1,0:T(8,128)}, f32[448,512]{1,0:T(8,128)}, f32[448,512]{1,0:T(8,128)}, ...) custom-call(f32[1664,512]{1,0:T(8,128)} %get-tuple-element.147.m_emb, ...), custom_call_target="tpu_custom_call" | custom-call | tf_op jit(solution)/shard_map/pallas_call | solution.py:76
  (600 shorter events, 111.9 us)
Async XLA Ops:
  7.2 196.0 %copy-start = (s32[4]{0:T(128)S(1)}, s32[4]{0:T(128)}, u32[]{:S(2)}) copy-start(s32[4]{0:T(128)} %param.32) | copy-start | bytes 52
  7.2 213.8 %all-gather.3.cloned.1.call-start = ((), (), s32[]{:S(2)}) async-start(), calls=%async_computation | async-start | bytes 2129920 | tf_op jit(solution)/shard_map/all_gather | solution.py:1268
  11.6 38.5 %copy-start.122 = (s32[4,1025]{1,0:T(4,128)S(1)}, s32[4,1025]{1,0:T(4,128)}, u32[]{:S(2)}) copy-start(s32[4,1025]{1,0:T(4,128)} %param.30) | copy-start | bytes 49204
  50.0 48.3 %copy-start.137 = (f32[1,512]{1,0:T(1,128)}, f32[1,512]{1,0:T(1,128)S(1)}, u32[]{:S(2)}) copy-start(f32[1,512]{1,0:T(1,128)S(1)} %get-tuple-element.267) | copy-start | bytes 6148
  50.0 48.3 %copy-start.139 = (f32[1,512]{1,0:T(1,128)}, f32[1,512]{1,0:T(1,128)S(1)}, u32[]{:S(2)}) copy-start(f32[1,512]{1,0:T(1,128)S(1)} %get-tuple-element.269) | copy-start | bytes 6148
  50.8 47.5 %copy-start.28 = (s32[16,1,256]{2,1,0:T(1,128)}, s32[16,1,256]{2,1,0:T(1,128)S(1)}, u32[]{:S(2)}) copy-start(s32[16,1,256]{2,1,0:T(1,128)S(1)} %and_select_fusion.1.ids) | copy-start | bytes 49156
  50.8 47.5 %copy-start.23 = (bf16[768,512]{1,0:T(8,128)(2,1)S(1)}, bf16[768,512]{1,0:T(8,128)(2,1)}, u32[]{:S(2)}) copy-start(bf16[768,512]{1,0:T(8,128)(2,1)} %copy-done.22) | copy-start | bytes 2359300
  129.8 296.8 %copy-start.76 = (bf16[1024,48]{0,1:T(8,128)(2,1)}, bf16[1024,48]{0,1:T(8,128)(2,1)S(1)}, u32[]{:S(2)}) copy-start(bf16[1024,48]{0,1:T(8,128)(2,1)S(1)} %get-tuple-element.242) | copy-start | bytes 294916
  209.5 142.2 %copy-start.131 = (f32[512]{0:T(512)}, f32[512]{0:T(512)S(1)}, u32[]{:S(2)}) copy-start(f32[512]{0:T(512)S(1)} %log_add_fusion.4) | copy-start | bytes 6148
  297.0 54.4 %copy-start.52 = (f32[512,512]{0,1:T(8,128)S(1)}, f32[512,512]{0,1:T(8,128)}, u32[]{:S(2)}) copy-start(f32[512,512]{0,1:T(8,128)} %get-tuple-element.301) | copy-start | bytes 3145732
  297.0 54.4 %copy-start.64 = (bf16[1024,192]{0,1:T(8,128)(2,1)S(1)}, bf16[1024,192]{0,1:T(8,128)(2,1)}, u32[]{:S(2)}) copy-start(bf16[1024,192]{0,1:T(8,128)(2,1)} %copy-done.63) | copy-start | bytes 1179652
  400.1 25.8 %copy-start.45 = (f32[512,512]{0,1:T(8,128)S(1)}, f32[512,512]{0,1:T(8,128)}, u32[]{:S(2)}) copy-start(f32[512,512]{0,1:T(8,128)} %copy-done.44) | copy-start | bytes 3145732
  400.1 25.8 %copy-start.60 = (bf16[1024,192]{0,1:T(8,128)(2,1)S(1)}, bf16[1024,192]{0,1:T(8,128)(2,1)}, u32[]{:S(2)}) copy-start(bf16[1024,192]{0,1:T(8,128)(2,1)} %copy-done.59) | copy-start | bytes 1179652
  481.5 64.6 %copy-start.3 = (f32[768,512]{1,0:T(8,128)S(1)}, f32[768,512]{1,0:T(8,128)}, u32[]{:S(2)}) copy-start(f32[768,512]{1,0:T(8,128)} %copy-done.2) | copy-start | bytes 4718596
  481.5 64.6 %copy-start.5 = (f32[768,512]{1,0:T(8,128)S(1)}, f32[768,512]{1,0:T(8,128)}, u32[]{:S(2)}) copy-start(f32[768,512]{1,0:T(8,128)} %copy-done.4) | copy-start | bytes 4718596
  554.2 41.5 %copy-start.154 = (f32[1,448]{1,0:T(1,128)S(1)}, f32[1,448]{1,0:T(1,128)}, u32[]{:S(2)}) copy-start(f32[1,448]{1,0:T(1,128)} %param.37) | copy-start | bytes 5380
  554.2 41.5 %copy-start.169 = (f32[1,448]{1,0:T(1,128)S(1)}, f32[1,448]{1,0:T(1,128)}, u32[]{:S(2)}) copy-start(f32[1,448]{1,0:T(1,128)} %param.49) | copy-start | bytes 5380
  554.2 41.6 %copy-start.170 = (f32[1,448]{1,0:T(1,128)S(1)}, f32[1,448]{1,0:T(1,128)}, u32[]{:S(2)}) copy-start(f32[1,448]{1,0:T(1,128)} %param.43) | copy-start | bytes 5380
  554.2 42.9 %copy-start.124 = (f32[1,6,512]{2,0,1:T(1,128)S(1)}, f32[1,6,512]{2,0,1:T(1,128)}, u32[]{:S(2)}) copy-start(f32[1,6,512]{2,0,1:T(1,128)} %param.38) | copy-start | bytes 36868
  554.2 42.9 %copy-start.135 = (f32[1,6,512]{2,0,1:T(1,128)S(1)}, f32[1,6,512]{2,0,1:T(1,128)}, u32[]{:S(2)}) copy-start(f32[1,6,512]{2,0,1:T(1,128)} %param.50) | copy-start | bytes 36868
  554.2 42.9 %copy-start.136 = (f32[1,6,512]{2,0,1:T(1,128)S(1)}, f32[1,6,512]{2,0,1:T(1,128)}, u32[]{:S(2)}) copy-start(f32[1,6,512]{2,0,1:T(1,128)} %param.44) | copy-start | bytes 36868
  554.3 43.5 %copy-start.133 = (f32[2,512]{1,0:T(2,128)S(1)}, f32[2,512]{1,0:T(2,128)}, u32[]{:S(2)}) copy-start(f32[2,512]{1,0:T(2,128)} %param.39) | copy-start | bytes 12292
  554.3 43.5 %copy-start.155 = (f32[2,512]{1,0:T(2,128)S(1)}, f32[2,512]{1,0:T(2,128)}, u32[]{:S(2)}) copy-start(f32[2,512]{1,0:T(2,128)} %param.51) | copy-start | bytes 12292
  554.3 43.5 %copy-start.156 = (f32[2,512]{1,0:T(2,128)S(1)}, f32[2,512]{1,0:T(2,128)}, u32[]{:S(2)}) copy-start(f32[2,512]{1,0:T(2,128)} %param.45) | copy-start | bytes 12292
  (156 other events, 584.3 us)
Sparse Core Ops, SparseCore 0:
  11.1 40.0 all-gather.2

commit v4 on v3

--- a/solution.py
+++ b/solution.py
@@ -20,6 +20,7 @@
 STEP = 5
 BLOCK = 128
 CHUNK = 128
+ROWS = 256
 TILES = D // 128
 
 EPS_NORM = 1e-05
@@ -117,7 +118,7 @@
     )
 
 
-def row_sum(part, r1, s, r2, sems1, sems2, meanwhile=None):
+def row_sum(part, r1, s, r2, sems1, sems2):
     y, core, z = where_am_i()
     first = []
     for i, k in enumerate(FAR + (0,)):
@@ -129,8 +130,6 @@
         first[i].wait_recv()
         s[i] = (part[zz * 2 + core].astype(F32) + r1[i].astype(F32)).astype(BF)
         second.append(send(s.at[i], r2.at[i], sems2, i, {"zz": zz}))
-    if meanwhile is not None:
-        meanwhile()
     first[3].wait_recv()
     total = part[z * 2 + core].astype(F32) + r1[3].astype(F32)
     for i in range(3):
@@ -141,15 +140,13 @@
     return total
 
 
-def row_gather(everyone, sems3, sems4, meanwhile=None):
+def row_gather(everyone, sems3, sems4):
     y, core, z = where_am_i()
     own = everyone.at[z * 2 + core]
     third = [
         send(own, own, sems3, i, {"zz": lax.rem(z + k, 4)}) for i, k in enumerate(FAR)
     ]
     fourth = [send(own, own, sems4, 3, {"co": 1 - core})]
-    if meanwhile is not None:
-        meanwhile()
     for i, k in enumerate(FAR):
         third[i].wait_recv()
         came = everyone.at[lax.rem(z + 4 - k, 4) * 2 + core]
@@ -160,6 +157,51 @@
         copy.wait()
 
 
+HALVES = [pl.ds(0, BLOCK // 2), pl.ds(BLOCK // 2, BLOCK // 2)]
+
+
+def row_exchange(part, everyone, middle, r1, s, r2, sems, hooks):
+    y, core, z = where_am_i()
+    own = z * 2 + core
+    first, second, third, fourth = [], [], [], []
+    for h, rows in enumerate(HALVES):
+        for i, k in enumerate(FAR + (0,)):
+            block = part.at[lax.rem(z + k, 4) * 2 + 1 - core, rows]
+            first.append(send(block, r1.at[i, rows], sems[0:2], 4 * h + i, {"co": 1 - core}))
+    for h, rows in enumerate(HALVES):
+        for i, k in enumerate(FAR):
+            zz = lax.rem(z + k, 4)
+            first[4 * h + i].wait_recv()
+            s[i, rows] = (part[zz * 2 + core, rows].astype(F32) + r1[i, rows].astype(F32)).astype(BF)
+            second.append(send(s.at[i, rows], r2.at[i, rows], sems[2:4], 3 * h + i, {"zz": zz}))
+    hooks[0]()
+    for h, rows in enumerate(HALVES):
+        first[4 * h + 3].wait_recv()
+        total = part[own, rows].astype(F32) + r1[3, rows].astype(F32)
+        for i in range(3):
+            second[3 * h + i].wait_recv()
+            total = total + r2[i, rows].astype(F32)
+        everyone[own, rows] = middle(rows, total).astype(BF)
+        mine = everyone.at[own, rows]
+        for i, k in enumerate(FAR):
+            third.append(send(mine, mine, sems[4:6], 3 * h + i, {"zz": lax.rem(z + k, 4)}))
+        fourth.append(send(mine, mine, sems[6:8], 6 + h, {"co": 1 - core}))
+    hooks[1]()
+    for h, rows in enumerate(HALVES):
+        for i, k in enumerate(FAR):
+            third[3 * h + i].wait_recv()
+            came = everyone.at[lax.rem(z + 4 - k, 4) * 2 + core, rows]
+            fourth.append(send(came, came, sems[6:8], 3 * h + i, {"co": 1 - core}))
+    for copy in first + second + third:
+        copy.wait_send()
+    for copy in fourth:
+        copy.wait()
+
+
+def nothing():
+    pass
+
+
 def row_peers():
     y, core, z = where_am_i()
     return [{"co": 1 - core}] + [{"zz": lax.rem(z + k, 4)} for k in FAR]
@@ -171,6 +213,7 @@
     pltpu.VMEM((3, BLOCK, D), BF),
 ] + sem_pairs(4, 3)
 GATHER_SCRATCH = sem_pairs(3, 4)
+EXCHANGE_SCRATCH = SUM_SCRATCH[:3] + sem_pairs(8, 6, 6, 8)
 
 
 def pair_peer():
@@ -312,48 +355,65 @@
     ]
 
 
-def forward_body(layer, part, x, shift, *refs):
+def forward_body(layer, part, x, rest, *refs):
     sources, everyone, x_new, places, refs = refs[:2], refs[2], refs[3], refs[4:6], refs[6:]
-    r1, s, r2, e, f, g, h, a, b, c, d = refs[:11]
-    sems = refs[11:]
-    y, core, z = where_am_i()
+    r1, s, r2, sems, side = refs[0], refs[1], refs[2], refs[3:11], refs[11:]
     greet(row_peers() + column_peers())
-    take_start(layer, sources, places, sems)
-    after = x[...] + row_sum(part, r1, s, r2, (e, f), (g, h)) + shift[0:1]
-    x_new[...] = after
-    everyone[z * 2 + core] = normed_rows(after)[0].astype(BF)
-    row_gather(everyone, (a, b), (c, d))
-    take_finish(layer, sources, places, sems)
-
-
-def next_hat(part, x, shift, layer, sources):
+    take_start(layer, sources, places, side)
+
+    def middle(rows, total):
+        after = x[rows] + total + (rest[4:5] + rest[5:6])
+        x_new[rows] = after
+        return normed_rows(after)[0]
+
+    row_exchange(part, everyone, middle, r1, s, r2, sems, (nothing, nothing))
+    take_finish(layer, sources, places, side)
+
+
+def next_hat(part, x, rest, layer, sources):
     return kernel_call(
         functools.partial(forward_body, layer),
         [jax.ShapeDtypeStruct((8, BLOCK, D), BF), jax.ShapeDtypeStruct((BLOCK, D), F32)]
         + [jax.ShapeDtypeStruct(a.shape, a.dtype) for a in sources],
-        (part, x, shift, *sources),
-        SUM_SCRATCH + GATHER_SCRATCH + take_scratch(len(sources)),
+        (part, x, rest, *sources),
+        EXCHANGE_SCRATCH + take_scratch(len(sources)),
         10 + layer,
     )
 
 
-def backward_body(layer, table_parts, part, x, grad, *refs):
+def backward_body(layer, table_parts, finish, part, x, grad, *refs):
     sources, refs = refs[:2], refs[2:]
     begun, steep, tokens = (), None, None
     if table_parts:
         steep, tokens, refs = refs[0], refs[1], refs[2:]
         if table_parts[0]:
             begun, refs = refs[:1], refs[1:]
+    if finish:
+        begun, err, factor, refs = refs[0], refs[1], refs[2], refs[3:]
     everyone, g_new, sums, refs = refs[0], refs[1], refs[2:4], refs[4:]
     if table_parts:
         table_grad, refs = refs[0], refs[1:]
+    if finish:
+        matrix, left, refs = refs[0], refs[1], refs[2:]
     landed, give_sems, refs = refs[:2], refs[2:6], refs[6:]
-    r1, s, r2, e, f, g, h, a, b, c, d = refs[:11]
-    y, core, z = where_am_i()
+    r1, s, r2, sems, refs = refs[0], refs[1], refs[2], refs[3:11], refs[11:]
     greet(row_peers() + column_peers())
-    hooks = [None, None]
+    hooks = [nothing, nothing]
+    if finish:
+        errors, err_sem = refs
+        load = pltpu.make_async_copy(err.at[1], errors, err_sem)
+        load.start()
+
+        def whole_matrix():
+            load.wait()
+            matrix[...] = begun[...] + errors[...]
+
+        def left_factor():
+            left[...] = short_dot(factor[...], matrix[...], ((1,), (0,)))
+
+        hooks = [whole_matrix, left_factor]
     if table_parts:
-        slopes, rows, sem_slopes, sem_rows = refs[11:]
+        slopes, rows, sem_slopes, sem_rows = refs
         loads = []
         for n, q in enumerate(table_parts):
             loads.append(
@@ -378,17 +438,23 @@
 
         hooks = [lambda: table_step(0), lambda: table_step(1)]
     give_start(layer, sources, landed, give_sems)
-    after = grad[...] + norm_back(x[...], row_sum(part, r1, s, r2, (e, f), (g, h), hooks[0]))
-    g_new[...] = after
-    everyone[z * 2 + core] = after.astype(BF)
-    row_gather(everyone, (a, b), (c, d), hooks[1])
+
+    def middle(rows, total):
+        after = grad[rows] + norm_back(x[rows], total)
+        g_new[rows] = after
+        return after
+
+    row_exchange(part, everyone, middle, r1, s, r2, sems, hooks)
     give_finish(layer, sources, landed, sums, give_sems)
 
 
-def next_grad(layer, part, x, grad, sources, table_parts=(), steep=None, tokens=None, begun=None):
-    args, outs, scratch = [], [], []
+def next_grad(layer, part, x, grad, sources, table_parts=(), steep=None, tokens=None, begun=None,
+              finish=None):
+    some = pl.BlockSpec(memory_space=pl.ANY)
+    args, specs, outs, scratch = [], [], [], []
     if table_parts:
         args = [steep, tokens] + ([] if begun is None else [begun])
+        specs = [some, some] + ([] if begun is None else [VMEM_SPEC])
         outs = [jax.ShapeDtypeStruct((steep.shape[1], D), F32)]
         scratch = [
             pltpu.VMEM((2, *steep.shape[1:]), BF),
@@ -396,16 +462,19 @@
             pltpu.SemaphoreType.DMA((2,)),
             pltpu.SemaphoreType.DMA((2,)),
         ]
-    specs = [VMEM_SPEC] * (3 + len(sources)) + [pl.BlockSpec(memory_space=pl.ANY)] * 2 + [VMEM_SPEC]
+    if finish:
+        args, specs = [begun, *finish], [VMEM_SPEC, some, VMEM_SPEC]
+        outs = [jax.ShapeDtypeStruct(begun.shape, F32), jax.ShapeDtypeStruct((RANK, D), F32)]
+        scratch = [pltpu.VMEM(begun.shape, F32), pltpu.SemaphoreType.DMA]
     return kernel_call(
-        functools.partial(backward_body, layer, table_parts),
+        functools.partial(backward_body, layer, table_parts, finish is not None),
         [jax.ShapeDtypeStruct((8, BLOCK, D), BF), jax.ShapeDtypeStruct((BLOCK, D), F32)]
         + [jax.ShapeDtypeStruct(a.shape, F32) for a in sources]
         + outs,
         (part, x, grad, *sources, *args),
-        give_scratch(sources) + SUM_SCRATCH + GATHER_SCRATCH + scratch,
+        give_scratch(sources) + EXCHANGE_SCRATCH + scratch,
         20 + layer,
-        in_specs=specs[: 3 + len(sources) + len(args)],
+        in_specs=[VMEM_SPEC] * (3 + len(sources)) + specs,
     )
 
 
@@ -444,6 +513,9 @@
     return pl.ds(pl.multiple_of(core * BLOCK, BLOCK), BLOCK)
 
 
+AHEAD = 10
+
+
 def plane_collect(everyone, sems, on_chip):
     y, core, z = where_am_i()
     a, b, c, d = sems
@@ -457,26 +529,33 @@
         came = everyone.at[yy * 4 + zz, core_rows(core)]
         return remote(came, came, c.at[i], d.at[i], {"co": 1 - core})
 
-    across(0).start()
-
-    @pl.loop(1, 16)
-    def _(i):
-        direct(i).start()
-
     def use(i):
         across(i).wait_recv()
         yy, zz = chip(i, -1)
         on_chip(i, yy * 4 + zz)
 
+    across(0).start()
+    for i in range(1, 1 + AHEAD):
+        direct(i).start()
+    use(0)
+    direct(1 + AHEAD).start()
     direct(1).wait_recv()
     across(1).start()
-    use(0)
-
-    @pl.loop(2, 16)
-    def _(i):
+
+    def step(i, more):
+        if more:
+            direct(i + AHEAD).start()
         direct(i).wait_recv()
         across(i).start()
         use(i - 1)
+
+    @pl.loop(2, 16 - AHEAD)
+    def _(i):
+        step(i, True)
+
+    @pl.loop(16 - AHEAD, 16)
+    def _(i):
+        step(i, False)
 
     use(15)
 
@@ -503,7 +582,7 @@
 
     def make(i):
         yy, zz = chip(i, 1)
-        part = group(yy * 4 + zz)
+        part = group(i, yy * 4 + zz)
         low, high = part[:, :BLOCK], part[:, BLOCK:]
         keep[i] = jnp.where(core == 0, low, high).astype(BF)
         other[i] = jnp.where(core == 0, high, low).astype(BF)
@@ -562,7 +641,7 @@
     y, core, z = where_am_i()
     greet(plane_peers(False))
 
-    def group(c):
+    def group(i, c):
         onehot_into(hot, ids[c])
         return jnp.dot(table[...], hot[...], preferred_element_type=F32)
 
@@ -584,14 +663,16 @@
 
 
 def lse_body(
-    vocab, part, x, shift, gains, head, targets,
-    x_new, everyone, probs, stats, joined, logits, came, r1, s, r2, *sems,
+    vocab, part, x, rest, gains, head, targets,
+    x_new, tokens_out, probs_out, stats, joined,
+    everyone, probs, out_sems, logits, came, r1, s, r2, *sems,
 ):
     y, core, z = where_am_i()
     greet(plane_peers(True))
     here = y * 4 + z
     a, b, c, d = sems[8:]
-    after = x[...] + row_sum(part, r1, s, r2, sems[0:2], sems[2:4]) + shift[0:1]
+    shift = rest[4:5] + rest[5:6]
+    after = x[...] + row_sum(part, r1, s, r2, sems[0:2], sems[2:4]) + shift
     x_new[...] = after
     everyone[here, core_rows(core)] = (
         normed_rows(after)[0] * gains[0:1] + gains[1:2]
@@ -605,14 +686,26 @@
             stats.at[where, to], came.at[2 * i + flip], a.at[2 * i + flip], b.at[2 * i + flip], device
         )
 
+    tokens_write = pltpu.make_async_copy(everyone, tokens_out, out_sems.at[16])
+
+    def probs_write(i):
+        yy, zz = chip(i, -1)
+        return pltpu.make_async_copy(
+            probs.at[yy * 4 + zz], probs_out.at[yy * 4 + zz], out_sems.at[i]
+        )
+
     def on_chip(i, where):
         logits[...] = dot_cols(head[...], everyone[where])
         wanted = targets[where]
 
+        whole = vocab // 128
+        edge = pl.ds(whole * 128, tall - whole * 128)
+        logits[edge, :] = jnp.where(
+            vocab_rows(whole, tall - whole * 128) < vocab, logits[edge, :], NEG_BIG
+        )
+
         def highest(v, top):
-            rows = pl.ds(pl.multiple_of(v * 128, 128), 128)
-            value = jnp.where(vocab_rows(v, 128) < vocab, logits[rows, :], NEG_BIG)
-            logits[rows, :] = value
+            value = logits[pl.ds(pl.multiple_of(v * 128, 128), 128), :]
             return jnp.maximum(top, jnp.max(value.reshape(16, 8, 2 * BLOCK), 0))
 
         top = lax.fori_loop(0, tall // 128, highest, jnp.full((8, 2 * BLOCK), NEG_BIG, F32))
@@ -642,6 +735,7 @@
         )
         stats[where, 0] = found[:, :BLOCK]
         stats[where, 1] = found[:, BLOCK:]
+        probs_write(i).start()
         if isinstance(i, int) and i == 0:
             came[0] = stats[where, core]
         else:
@@ -649,6 +743,7 @@
         stat_copy(i, 1, where).start()
 
     plane_collect(everyone, sems[4:8], on_chip)
+    tokens_write.start()
 
     @pl.loop(1, 16)
     def _(i):
@@ -680,9 +775,14 @@
         lse_copy(i, 1).wait()
 
     lse_copy(0, 1).wait()
-
-
-def last_and_lse(vocab, part, x, shift, gains, head, targets):
+    tokens_write.wait()
+
+    @pl.loop(0, 16)
+    def _(i):
+        probs_write(i).wait()
+
+
+def last_and_lse(vocab, part, x, rest, gains, head, targets):
     tall = head.shape[0]
     return kernel_call(
         functools.partial(lse_body, vocab),
@@ -693,26 +793,47 @@
             jax.ShapeDtypeStruct((16, 2, 8, BLOCK), F32),
             jax.ShapeDtypeStruct((16, 2, 8, BLOCK), F32),
         ],
-        (part, x, shift, gains, head, targets),
-        [pltpu.VMEM((tall, 2 * BLOCK), F32), pltpu.VMEM((32, 8, BLOCK), F32)]
+        (part, x, rest, gains, head, targets),
+        [
+            pltpu.VMEM((16, 2 * BLOCK, D), BF),
+            pltpu.VMEM((16, tall, 2 * BLOCK), BF),
+            pltpu.SemaphoreType.DMA((17,)),
+            pltpu.VMEM((tall, 2 * BLOCK), F32),
+            pltpu.VMEM((32, 8, BLOCK), F32),
+        ]
         + SUM_SCRATCH
         + COLLECT_SEMS
         + sem_pairs(32, 32),
         8,
         56,
+        out_specs=[VMEM_SPEC] + [pl.BlockSpec(memory_space=pl.ANY)] * 2 + [VMEM_SPEC] * 2,
     )
 
 
 def loss_back_body(
-    probs, stats, joined, targets, coefs, head_t, x, gains,
-    steep, row_all, grad, grad_gains, slopes, keep, other, r1, s, r2, *sems,
+    probs_in, stats, joined, targets, coefs, head_t, x, gains,
+    steep, row_all, grad, grad_gains, slopes, probs, in_sems, keep, other, r1, s, r2, *sems,
 ):
     y, core, z = where_am_i()
+
+    def read(i):
+        yy, zz = chip(i, 1)
+        return pltpu.make_async_copy(
+            probs_in.at[yy * 4 + zz], probs.at[yy * 4 + zz], in_sems.at[i]
+        )
+
+    @pl.loop(1, 16)
+    def _(i):
+        read(i).start()
+
+    read(0).start()
     greet(plane_peers(False))
     tall = head_t.shape[1]
     written = pltpu.make_async_copy(slopes, steep, sems[8])
 
-    def group(c):
+    def group(i, c):
+        read(i).wait()
+
         def row(ref):
             return jnp.concatenate([ref[c, 0, 0:1, :], ref[c, 1, 0:1, :]], 1)
 
@@ -761,12 +882,17 @@
             jax.ShapeDtypeStruct((8, D), F32),
         ],
         (probs, stats, joined, targets, coefs, head_t, x, gains),
-        [pltpu.VMEM((4, tall, 8 * BLOCK), BF)]
+        [
+            pltpu.VMEM((4, tall, 8 * BLOCK), BF),
+            pltpu.VMEM((16, tall, 2 * BLOCK), BF),
+            pltpu.SemaphoreType.DMA((16,)),
+        ]
         + TOTAL_SCRATCH
         + GATHER_SCRATCH
         + [pltpu.SemaphoreType.DMA],
         9,
         56,
+        in_specs=[pl.BlockSpec(memory_space=pl.ANY)] + [VMEM_SPEC] * 7,
         out_specs=[pl.BlockSpec(memory_space=pl.ANY)] + [VMEM_SPEC] * 3,
     )
 
@@ -893,14 +1019,16 @@
     def up(n):
         return -(-n // 128) * 128
 
-    half = max(up(cols) + up(vocab), up(rows) + up(vocab))
+    half = up(cols) + -(-vocab // ROWS) * ROWS
     return half, ((0, 0, cols), (1, 0, rows), (0, up(cols), vocab), (1, up(rows), vocab))
 
 
 def compress_body(
-    vocab, g_embed, g_head, err, m_in, m_back, q_in, q_back, q_embed, q_head, bias, vectors,
-    m_embed, m_head, basis, own, sums, bias_sum, vector_sum,
-    left, left_came, bias_came, joint, joint_came, work, vec_came, vec_mine, vec_sums, vec_all,
+    vocab, g_embed_in, m_head_in, left_head, err, err_in, err_back, q_in, q_back, q_embed,
+    ret0, ret1, ret2, ret3, bias0, bias1, bias2, bias3, out_rows, vectors,
+    m_embed, m_layer, basis, own, sums, bias_sum, vector_sum,
+    g_embed, m_head, errors, came, landed, out_sum, load_sems, give_send, give_recv,
+    bias, left, left_came, bias_came, joint, joint_came, work, vec_came, vec_mine, vec_sums, vec_all,
     *sems,
 ):
     y, core, z = where_am_i()
@@ -910,6 +1038,27 @@
     for k in range(1, 32):
         p = lax.rem(me + k, 32)
         peers.append((p, {**at_chip(p // 8, lax.rem(p, 4)), "co": lax.rem(p // 4, 2)}))
+    own_layer = home_and_layer()[1]
+    rets = (ret0, ret1, ret2, ret3)
+
+    def load(index):
+        size = rets[index].shape[0]
+        return pltpu.make_async_copy(rets[index], came.at[pl.ds(0, size)], load_sems.at[0])
+
+    def load_own(act):
+        for index in range(LAYERS):
+
+            @pl.when(own_layer == index)
+            def _():
+                act(load(index))
+
+    load_err = pltpu.make_async_copy(err.at[0], errors, load_sems.at[1])
+    load_embed = pltpu.make_async_copy(g_embed_in, g_embed, load_sems.at[2])
+    load_head = pltpu.make_async_copy(m_head_in, m_head, load_sems.at[3])
+    load_embed.start()
+    load_err.start()
+    load_own(lambda copy: copy.start())
+    load_head.start()
     greet([device for _, device in peers] + [device for _, device in replicas_peers()])
     pairs = [(sems[2 * n], sems[2 * n + 1]) for n in range(len(sems) // 2)]
     vec_first = [
@@ -918,12 +1067,38 @@
     ]
     vec_came[me] = vectors[me]
 
-    half, places = factor_places(m_in.shape[0], m_back.shape[0], vocab)
-    m_embed[...] = g_embed[...] + err[0]
-    m_head[...] = g_head[...] + err[1]
-    blocks = (m_in, m_back, m_embed, m_head)
-    for b, (factor, block) in enumerate(zip((q_in, q_back, q_embed, q_head), blocks)):
-        left[b] = short_dot(factor[...], block[...], ((1,), (0,)))
+    cols, rows = err_in.shape[0], err_back.shape[0]
+    half, places = factor_places(cols, rows, vocab)
+    of_in, of_back = pl.ds(0, cols), pl.ds(cols, rows)
+    give = (0, (out_rows,), (landed,))
+    give_start(*give, (give_send, give_recv))
+    for index, bias_part in enumerate((bias0, bias1, bias2, bias3)):
+
+        @pl.when(own_layer == index)
+        def _():
+            bias[...] = bias_part[...]
+
+    load_embed.wait()
+    load_err.wait()
+    m_embed[...] = g_embed[...] + errors[...]
+    left[2] = short_dot(q_embed[...], m_embed[...], ((1,), (0,)))
+    load_own(lambda copy: copy.wait())
+    m_layer[of_in, :] = came[of_in, :] + err_in[...]
+    left[0] = short_dot(q_in[...], m_layer[of_in, :], ((1,), (0,)))
+    give_finish(*give, (out_sum,), (give_send, give_recv))
+
+    @pl.when(own_layer == 0)
+    def _():
+        m_layer[of_back, :] = out_sum[...] + err_back[...]
+
+    @pl.when(own_layer != 0)
+    def _():
+        m_layer[of_back, :] = came[of_back, :] + err_back[...]
+
+    left[1] = short_dot(q_back[...], m_layer[of_back, :], ((1,), (0,)))
+    load_head.wait()
+    blocks = (m_layer.at[of_in], m_layer.at[of_back], m_embed, m_head)
+    left[3] = left_head[...]
 
     for copy in vec_first:
         copy.wait_recv()
@@ -971,17 +1146,35 @@
     vector_sum[...] = vec_all[...]
 
 
-def compressed(vocab, g_embed, g_head, err, m_in, m_back, facs, bias, vectors):
-    half, _ = factor_places(m_in.shape[0], m_back.shape[0], vocab)
+def compressed(vocab, g_embed, m_head, left_head, err, errs, facs, returned, out_rows, vectors):
+    half, _ = factor_places(errs[0].shape[0], errs[1].shape[0], vocab)
     tall = g_embed.shape
+    layers = [r[0] for r in returned]
+    rows = (errs[0].shape[0] + errs[1].shape[0], D)
+    some = pl.BlockSpec(memory_space=pl.ANY)
+    biases = [r[1] for r in returned]
+    bias = biases[0]
     return kernel_call(
         functools.partial(compress_body, vocab),
         [
             jax.ShapeDtypeStruct(s, F32)
-            for s in (tall, tall, (4, 8, D), (2, 8, half), (2, 8, half), bias.shape, vectors.shape)
+            for s in (
+                tall, rows, (4, 8, D), (2, 8, half), (2, 8, half), bias.shape,
+                vectors.shape,
+            )
         ],
-        (g_embed, g_head, err, m_in, m_back, *facs, bias, vectors),
+        (g_embed, m_head, left_head, err, *errs, *facs, *layers, *biases, out_rows, vectors),
         [
+            pltpu.VMEM(tall, F32),
+            pltpu.VMEM(tall, F32),
+            pltpu.VMEM(tall, F32),
+            pltpu.VMEM(rows, F32),
+            pltpu.VMEM((4, *out_rows.shape), BF),
+            pltpu.VMEM(out_rows.shape, F32),
+            pltpu.SemaphoreType.DMA((4,)),
+            pltpu.SemaphoreType.DMA((1,)),
+            pltpu.SemaphoreType.DMA((4,)),
+            pltpu.VMEM(bias.shape, F32),
             pltpu.VMEM((4, 8, D), F32),
             pltpu.VMEM((4, 4, 8, D), F32),
             pltpu.VMEM((4, *bias.shape), F32),
@@ -996,6 +1189,7 @@
         + sem_pairs(31, 3, 3, 3, 31, 3),
         30,
         56,
+        in_specs=[some, some, VMEM_SPEC, some] + [VMEM_SPEC] * 5 + [some] * 4 + [VMEM_SPEC] * 6,
     )
 
 
@@ -1011,70 +1205,83 @@
 
 
 def update_body(
-    vocab, rate_layer, rate_tables, m_embed, m_head, m_in, m_back, basis, own, sums,
-    in_w, in_m, in_e, back_w, back_m, back_e, tab_w, tab_m, tab_e,
-    err_tab, err_in, err_back, o_in_w, o_in_m, o_in_e, o_back_w, o_back_m, o_back_e,
-    o_tab_w, o_tab_m, o_tab_e,
+    vocab, rates, m_embed, m_head, m_layer, basis, own, sums, bias_sum, vector_sum, *refs
 ):
+    rate_layer, rate_vector, rate_tables = rates
+    olds, new = refs[:18], refs[18:36]
+    (err_tab, err_in, err_back, *factors) = refs[36:]
     x = lax.axis_index("xx")
-    half, places = factor_places(m_in.shape[0], m_back.shape[0], vocab)
-    whole = vocab // CHUNK
+    cols, rows = err_in.shape[0], err_back.shape[0]
+    half, places = factor_places(cols, rows, vocab)
     own_cols = pl.ds(pl.multiple_of(x * 128, 128), 128)
-
-    def part(ref, b, start, count):
-        return ref[places[b][0], :, pl.ds(pl.multiple_of(places[b][1] + start, 128), count)]
-
-    def table_rows(start, count):
-        for b, matrix in ((2, m_embed), (3, m_head)):
-            span = CHUNK
-            product = outer_dot(part(own, b, start, span), basis[b])
-            for tile in range(TILES):
-                far = pl.ds(start * (2 * TILES) + 2 * tile + b - 2, count, stride=2 * TILES)
-                err_tab[far, :] = (
-                    matrix[pl.ds(start, count), pl.ds(tile * 128, 128)]
-                    - product[:count, tile * 128 : (tile + 1) * 128]
+    step = pl.program_id(0)
+    start = pl.multiple_of(step * ROWS, ROWS)
+
+    def change(rate, group, at, reduced):
+        values = stepped(rate, *[old[at] for old in olds[group : group + 3]], reduced)
+        for out, value in zip(new[group : group + 3], values):
+            out[at] = value
+
+    for b, matrix in ((2, m_embed), (3, m_head)):
+        lanes = pl.ds(pl.multiple_of(places[b][1] + start, 128), ROWS)
+        product = outer_dot(own[places[b][0], :, lanes], basis[b])
+        for tile in range(TILES):
+            far = pl.ds(2 * tile + b - 2, ROWS, stride=2 * TILES)
+            lane = slice(tile * 128, (tile + 1) * 128)
+            err_tab[far, :] = matrix[:, lane] - product[:, lane]
+        reduced = outer_dot(sums[places[b][0], :, lanes], basis[b, :, own_cols])
+        change(rate_tables[b - 2], 6, (pl.ds(b - 2, ROWS, stride=2), slice(None)), reduced)
+
+    @pl.when(step == 0)
+    def _():
+        for b, (first, count, err) in enumerate(((0, cols, err_in), (cols, rows, err_back))):
+            for begin in range(0, count, CHUNK):
+                size = min(CHUNK, count - begin)
+                at = (pl.ds(begin, size), slice(None))
+                lanes = pl.ds(places[b][1] + begin, size)
+                err[at] = m_layer[pl.ds(first + begin, size), :] - outer_dot(
+                    own[places[b][0], :, lanes], basis[b]
                 )
-            reduced = outer_dot(part(sums, b, start, span), basis[b, :, own_cols])
-            near = pl.ds(start * 2 + b - 2, count, stride=2)
-            new = stepped(
-                rate_tables[b - 2], tab_w[near, :], tab_m[near, :], tab_e[near, :], reduced[:count]
-            )
-            for out, value in zip((o_tab_w, o_tab_m, o_tab_e), new):
-                out[near, :] = value
-
-    @pl.loop(0, whole)
-    def _(c):
-        table_rows(pl.multiple_of(c * CHUNK, CHUNK), CHUNK)
-
-    if vocab > whole * CHUNK:
-        table_rows(whole * CHUNK, vocab - whole * CHUNK)
-
-    layer_parts = (
-        (m_in, err_in, (in_w, in_m, in_e), (o_in_w, o_in_m, o_in_e)),
-        (m_back, err_back, (back_w, back_m, back_e), (o_back_w, o_back_m, o_back_e)),
-    )
-    for b, (matrix, err, olds, outs) in enumerate(layer_parts):
-        for start in range(0, matrix.shape[0], CHUNK):
-            count = min(CHUNK, matrix.shape[0] - start)
-            at = pl.ds(start, count)
-            lanes = pl.ds(places[b][1] + start, count)
-            err[at, :] = matrix[at, :] - outer_dot(own[places[b][0], :, lanes], basis[b])
-            reduced = outer_dot(sums[places[b][0], :, lanes], basis[b])
-            new = stepped(rate_layer, *[old[at, :] for old in olds], reduced)
-            for out, value in zip(outs, new):
-                out[at, :] = value
-
-
-def updated(vocab, rates, m_tables, m_in, m_back, basis, own, sums, params, err_shape):
-    outs = [err_shape, m_in.shape, m_back.shape] + [a.shape for a in params]
-    return kernel_call(
-        functools.partial(update_body, vocab, rates[0], rates[1]),
-        [jax.ShapeDtypeStruct(a, F32) for a in outs],
-        (*m_tables, m_in, m_back, basis, own, sums, *params),
-        [],
-        None,
-        56,
-    )
+                reduced = outer_dot(sums[places[b][0], :, lanes], basis[b])
+                change(rate_layer, 3 * b, at, reduced)
+        for factor, (group, at, width) in zip(factors, places):
+            factor[...] = sums[group, :, pl.ds(at, width)]
+        change(rate_layer, 9, (slice(None), slice(None)), bias_sum[0:1, :cols])
+        section = home_and_layer()[1]
+        for tile in range(TILES):
+            lanes = (slice(None), pl.ds(tile * 128, 128))
+            change(rate_vector, 12, lanes, vector_sum[pl.ds(section * 6, 6), tile, :])
+            final = vector_sum[6 * LAYERS : 6 * LAYERS + 2, tile, :]
+            change(rate_layer, 15, lanes, final)
+
+
+def updated(vocab, rates, m_tables, m_layer, basis, own, sums, bias_sum, vector_sum, params):
+    cols, rows = params[0].shape[0], params[3].shape[0]
+
+    def whole(shape):
+        return pl.BlockSpec(shape, lambda step: (0,) * len(shape))
+
+    def spec(index, array):
+        if 6 <= index < 9:
+            return pl.BlockSpec((2 * ROWS, 128), lambda step: (step, 0))
+        return whole(array.shape)
+
+    before = (*m_tables, m_layer, basis, own, sums, bias_sum, vector_sum)
+    factors = [(RANK, cols), (RANK, rows), (RANK, vocab), (RANK, vocab)]
+    outs = [a.shape for a in params] + [(vocab * 8, 128), (cols, D), (rows, D)] + factors
+    param_specs = [spec(n, a) for n, a in enumerate(params)]
+    return pl.pallas_call(
+        functools.partial(update_body, vocab, rates),
+        grid=(-(-vocab // ROWS),),
+        out_shape=[jax.ShapeDtypeStruct(a, F32) for a in outs],
+        in_specs=[pl.BlockSpec((ROWS, D), lambda step: (step, 0))] * 2
+        + [whole(a.shape) for a in before[2:]]
+        + param_specs,
+        out_specs=param_specs
+        + [pl.BlockSpec((8 * ROWS, 128), lambda step: (step, 0))]
+        + [whole(a) for a in outs[19:]],
+        compiler_params=pltpu.CompilerParams(vmem_limit_bytes=56 * 2**20),
+    )(*before, *params)
 
 
 def rotary_tables():
@@ -1172,13 +1379,11 @@
     grad_query = rotate(grad_query, cosine, -sine)
     grad_key = rotate(grad_key, cosine, -sine)
     grad_qkv = jnp.concatenate([grad_query, grad_key, grad_value], 1).astype(BF)
-    grad_weights = jnp.concatenate(
-        [
-            dot_rows(grad_qkv, first_in).astype(BF),
-            dot_rows(grad_up, second_in).astype(BF),
-            dot_rows(attended, grad_low).astype(BF),
-            dot_rows(hidden, grad_low).astype(BF),
-        ]
+    grad_weights = (
+        dot_rows(grad_qkv, first_in).astype(BF),
+        dot_rows(grad_up, second_in).astype(BF),
+        dot_rows(attended, grad_low).astype(BF),
+        dot_rows(hidden, grad_low).astype(BF),
     )
     grad_bias = jnp.concatenate(
         [jnp.sum(grad_qkv.astype(F32), 0), jnp.sum(grad_up.astype(F32), 0)]
@@ -1276,21 +1481,19 @@
     x, hat = embedded(embed_t.reshape(D, tall), own_tokens)
     head = jnp.transpose(head_t)
 
-    gains = jnp.pad(final_norm, ((0, 6), (0, 0)))
     weights, kept, before = [], [], []
     for index in range(LAYERS):
         w_all, rest = packs[index]
         weights.append((w_all, rest[8, : b_in.shape[1]], rest))
-        shift = jnp.broadcast_to((rest[4] + rest[5])[None], (8, D))
         before.append(x)
         branch, keep = block_forward(hat.reshape(LENGTH, D), weights[index], cosine, sine)
         kept.append(keep)
         branch = branch.reshape(8, BLOCK, D)
         if index + 1 < LAYERS:
-            hat, x, *packs[index + 1] = next_hat(branch, x, shift, index + 1, sources)
+            hat, x, *packs[index + 1] = next_hat(branch, x, rest, index + 1, sources)
 
     x, normed, probs, stats, joined = last_and_lse(
-        vocab_shard, branch, x, shift, gains, head, own_targets
+        vocab_shard, branch, x, rest, final_norm, head, own_targets
     )
     losses = joined[:, :, 1, :].reshape(seq_rep, LENGTH)
     loss_part = jnp.sum(own_weight * jnp.mean(losses, 1))
@@ -1298,7 +1501,7 @@
         jnp.repeat(own_weight / (weight_total * LENGTH), 4)[:, None, None], (16, 1, 2 * BLOCK)
     )
     steep, grad_all, grad, grad_gains = loss_back(
-        probs, stats, joined, own_targets, coefs, head_t, x, gains
+        probs, stats, joined, own_targets, coefs, head_t, x, final_norm
     )
     grad_gains = grad_gains[:2]
     vector_rows = [None] * LAYERS
@@ -1310,6 +1513,8 @@
             grad_all.reshape(LENGTH, D), kept[index], weights[index], cosine, sine
         )
         vector_rows[index] = jnp.concatenate([norm_rows, outbias, outbias], 0)
+        w_grad_in, w_grad_out = w_grad[:2], w_grad[2:]
+        w_grad = jnp.concatenate(w_grad if index else w_grad_in)
         given = (w_grad, jnp.pad(bias_row[None], ((0, 7), (0, D - bias_row.shape[0]))))
         grad_hat = grad_hat.reshape(8, BLOCK, D)
         if index >= LAYERS - 2:
@@ -1318,42 +1523,31 @@
                 index, grad_hat, before[index], grad, given, parts, steep, normed, grad_table
             )
         elif index:
-            grad_all, grad, *returned[index] = next_grad(
-                index, grad_hat, before[index], grad, given
+            *most, m_head, left_head = next_grad(
+                index, grad_hat, before[index], grad, given, begun=grad_table,
+                finish=(err, jnp.pad(tables_fac[1].T, ((0, 0), (0, pad_ids)))),
             )
+            grad_all, grad, *returned[index] = most
         else:
             grad_embed, *returned[index] = lowest_grad(
                 index, grad_hat, before[index], grad, own_tokens, given, tall
             )
 
-    def of_own_layer(n):
-        picked = returned[LAYERS - 1][n]
-        for index in range(LAYERS - 1):
-            picked = jnp.where(section == index, returned[index][n], picked)
-        return picked
-
     loss_row = jnp.zeros((1, D), F32).at[0, 0].set(jnp.where(shard + y * 8 == 0, loss_part, 0.0))
     vectors = jnp.concatenate(vector_rows + [grad_gains, loss_row], 0)
     vectors = jnp.pad(vectors, ((0, 32 - vectors.shape[0]), (0, 0))).reshape(32, D // 128, 128)
     vectors = jnp.pad(vectors, ((0, 0), (0, 8 - D // 128), (0, 0)))
-    full = of_own_layer(0)
-    n_in = b_in.shape[1]
-    full_in = full[:n_in] + w_in_err[0, 0].T
-    full_back = full[n_in:] + w_back_err[0, 0]
     facs = (
         w_in_fac[0].T,
         w_back_fac[0].T,
         jnp.pad(tables_fac[0].T, ((0, 0), (0, pad_ids))),
-        jnp.pad(tables_fac[1].T, ((0, 0), (0, pad_ids))),
-    )
-    m_embed, m_head, basis, own, sums, bias_sum, vector_sums = compressed(
-        vocab_shard, grad_embed, grad_table, err, full_in, full_back, facs, of_own_layer(1), vectors
-    )
-    bias_sum = bias_sum[:1, : b_in.shape[1]]
-    vector_sums = vector_sums[:, : D // 128, :].reshape(32, D)
-    vec_sum = lax.dynamic_slice_in_dim(vector_sums, section * 6, 6, 0)
-    final_sum = vector_sums[6 * LAYERS : 6 * LAYERS + 2]
-    loss_sum = vector_sums[6 * LAYERS + 2, 0]
+    )
+    errs = (w_in_err[0, 0].T, w_back_err[0, 0])
+    m_embed, m_layer, basis, own, sums, bias_sum, vector_sums = compressed(
+        vocab_shard, grad_embed, m_head, left_head, err, errs, facs, returned,
+        jnp.concatenate(w_grad_out), vectors,
+    )
+    loss_sum = vector_sums[6 * LAYERS + 2, 0, 0]
 
     def of_tables(arrays):
         return [jnp.transpose(a, (1, 0, 2)).reshape(-1, 128) for a in arrays]
@@ -1365,26 +1559,25 @@
     params = (
         [w_in[0].T, w_in_mom[0].T, w_in_ema[0].T, w_back[0], w_back_mom[0], w_back_ema[0]]
         + of_tables((tables, tables_mom, tables_ema))
-    )
-    err_tab, err_in, err_back, *new = updated(
-        vocab_shard, (rate_layer, rate_tables), (m_embed, m_head), full_in, full_back,
-        basis, own, sums, params, (vocab_shard * 8, 128),
-    )
+        + [b_in, b_in_mom, b_in_ema, vecs[0], vecs_mom[0], vecs_ema[0]]
+        + [final_norm, final_mom, final_ema]
+    )
+    new = updated(
+        vocab_shard, (rate_layer, rate_vector, rate_tables), (m_embed, m_head), m_layer,
+        basis, own, sums, bias_sum, vector_sums, params,
+    )
+    err_tab, err_in, err_back, fac_in, fac_back, fac_embed, fac_head = new[18:]
     err_tab = jnp.transpose(
         err_tab.reshape(vocab_shard, D // 128, 2, 128), (2, 0, 1, 3)
     ).reshape(tables_err.shape)
     in_w, in_m, in_e = [a.T[None] for a in new[:3]]
     back_w, back_m, back_e = [a[None] for a in new[3:6]]
     tab_w, tab_m, tab_e = [
-        jnp.transpose(a.reshape(vocab_shard, 2, own_cols), (1, 0, 2)) for a in new[6:]
+        jnp.transpose(a.reshape(vocab_shard, 2, own_cols), (1, 0, 2)) for a in new[6:9]
     ]
-    _, places = factor_places(full_in.shape[0], full_back.shape[0], vocab_shard)
-    fac_in, fac_back, fac_embed, fac_head = [
-        sums[half, :, at : at + width].T for half, at, width in places
-    ]
-    bias_w, bias_m, bias_e = stepped(rate_layer, b_in, b_in_mom, b_in_ema, bias_sum)
-    vec_w, vec_m, vec_e = stepped(rate_vector, vecs, vecs_mom, vecs_ema, vec_sum[None])
-    fin_w, fin_m, fin_e = stepped(rate_layer, final_norm, final_mom, final_ema, final_sum)
+    bias_w, bias_m, bias_e = new[9:12]
+    vec_w, vec_m, vec_e = [a[None] for a in new[12:15]]
+    fin_w, fin_m, fin_e = new[15:18]
     return (
         loss_sum,
         weight_total,
@@ -1409,10 +1602,10 @@
         err_in.T[None, None],
         err_back[None, None],
         err_tab,
-        fac_in[None],
-        fac_back[None],
-        fac_embed,
-        fac_head,
+        fac_in.T[None],
+        fac_back.T[None],
+        fac_embed.T,
+        fac_head.T,
     )
 
 

time: 631 us -> 604 us (0.957)
  Pallas kernels: 459 us -> 444 us
  other arithmetic: 36.8 us -> 26 us
    pallas_call x13 -> x12, Pallas kernels: 459 us -> 427 us  [kernel_call(): pl.pallas_call(body, out_shape=out_shape, in_specs=in_specs or [VMEM_SPEC...]
    pallas_call x0 -> x1, Pallas kernels: none -> 16.6 us  [updated(): pl.pallas_call(functools.partial(update_body, vocab, rates), grid=(-(-voc...]
    unnamed x364 -> x379, local copies, waits for them, and re-layouts: 13.6 us -> 18.5 us
  transfers between devices with their start and end apart: 1 -> 1, of which waited for: 0 -> 0; matrix products, arithmetic and copies ran while one was open for 8% -> 8% of each run, Pallas kernels for 24% -> 25%
where the time goes in v4:
time: 604 us; the launch traced here: 595 us
  Pallas kernels  444 us (74%)
  matrix products  74.7 us (12%)
  local copies, waits for them, and re-layouts  31.2 us (5%)
  other arithmetic  26 us (4%)
  between operations  19.5 us (3%)
    pallas_call x12, Pallas kernels, kernel_call(): pl.pallas_call(body, out_shape=out_shape, in_specs=in_specs or [VMEM_SPEC...  427 us
    dot_general x32, matrix products, dot_cols(): lax.dot_general(left, right, (((1,), (1,)), ((), ())), preferred_element_...  33.8 us
    dot_general x32, matrix products, dot_plain(): return jnp.dot(left, right, preferred_element_type=F32)  25.6 us
    unnamed x379, local copies, waits for them, and re-layouts  18.5 us
    pallas_call x1, Pallas kernels, updated(): pl.pallas_call(functools.partial(update_body, vocab, rates), grid=(-(-voc...  16.6 us
    dot_general x32, matrix products, dot_rows(): lax.dot_general(left, right, (((0,), (0,)), ((), ())), preferred_element_...  15.3 us
  transfers between devices with their start and end apart: 1, of which 0 were waited for; matrix products, arithmetic and copies ran while one was open for 8% of the time, Pallas kernels for 25%

profile of v4, /device:TPU:0, one launch (start us, length us, event | category | flops | bytes accessed | tf_op | source)
XLA Modules:
  0.0 595.3 jit_solution(18422765938389314265)
XLA Ops:
  7.3 1.7 convert_element_type.311
  12.1 37.4 %shard_map.475 = (bf16[4,128,1664]{2,1,0:T(8,128)(2,1)S(1)}, bf16[768,512]{1,0:T(8,128)(2,1)S(1)}, f32[16,512]{1,0:T(8,128)S(1)}, f32[2,1664,512]{2,1,0:T(8,128)}) custom-call(bf16[128,1664]{1,0:T(8,128)(2,1)S(1)} %get-tuple-element.350.block, f32[12576,128]{1,0:T(8,128)} %bitcast.282, bf16[768,512]{1,0:T(8,128)(2,1)S(1)} %pad_maximum_fusion.refs_0_, ...), custom_call_target="tpu_custom_call" | custom-call | tf_op jit(solution)/shard_map/pallas_call | solution.py:77
  52.3 47.1 %shard_map.476 = (f32[128,512]{1,0:T(8,128)S(1)}, bf16[8,128,512]{2,1,0:T(8,128)(2,1)S(1)}) custom-call(bf16[512,1664]{1,0:T(8,128)(2,1)S(1)} %bitcast.276, s32[16,1,256]{2,1,0:T(1,128)S(1)} %and_select_fusion.1.ids), custom_call_target="tpu_custom_call" | custom-call | tf_op jit(solution)/shard_map/pallas_call | solution.py:77
  105.7 3.7 multiply_convert_fusion.11
  110.1 20.1 %shard_map.477 = (bf16[8,128,512]{2,1,0:T(8,128)(2,1)S(1)}, f32[128,512]{1,0:T(8,128)S(1)}, bf16[768,512]{1,0:T(8,128)(2,1)S(1)}, f32[16,512]{1,0:T(8,128)S(1)}) custom-call(bf16[8,128,512]{2,1,0:T(8,128)(2,1)S(1)} %bitcast.274, f32[128,512]{1,0:T(8,128)S(1)} %get-tuple-element.121.x, f32[16,512]{1,0:T(8,128)S(1)} %copy-done.29, ...), custom_call_target="tpu_custom_call" | custom-call | tf_op jit(solution)/shard_map/pallas_call | solution.py:77
  136.6 3.7 multiply_convert_fusion.10
  141.1 25.5 %shard_map.478 = (bf16[8,128,512]{2,1,0:T(8,128)(2,1)S(1)}, f32[128,512]{1,0:T(8,128)S(1)}, bf16[768,512]{1,0:T(8,128)(2,1)S(1)}, f32[16,512]{1,0:T(8,128)S(1)}) custom-call(bf16[8,128,512]{2,1,0:T(8,128)(2,1)S(1)} %bitcast.275, f32[128,512]{1,0:T(8,128)S(1)} %get-tuple-element.125.x, f32[16,512]{1,0:T(8,128)S(1)} %get-tuple-element.123.rest, ...), custom_call_target="tpu_custom_call" | custom-call | tf_op jit(solution)/shard_map/pallas_call | solution.py:77
  172.7 3.6 multiply_convert_fusion.9
  176.8 21.4 %shard_map.479 = (bf16[8,128,512]{2,1,0:T(8,128)(2,1)S(1)}, f32[128,512]{1,0:T(8,128)S(1)}, bf16[768,512]{1,0:T(8,128)(2,1)S(1)}, f32[16,512]{1,0:T(8,128)S(1)}) custom-call(bf16[8,128,512]{2,1,0:T(8,128)(2,1)S(1)} %bitcast.273, f32[128,512]{1,0:T(8,128)S(1)} %get-tuple-element.129.x, f32[16,512]{1,0:T(8,128)S(1)} %get-tuple-element.127.rest, ...), custom_call_target="tpu_custom_call" | custom-call | tf_op jit(solution)/shard_map/pallas_call | solution.py:77
  209.8 1.8 convolution_convert_fusion.20
  212.9 3.6 multiply_convert_fusion.8
  218.7 3.6 copy.78.head
  222.4 60.7 %shard_map.480 = (f32[128,512]{1,0:T(8,128)}, bf16[16,256,512]{2,1,0:T(8,128)(2,1)}, bf16[16,1664,256]{2,1,0:T(8,128)(2,1)}, f32[16,2,8,128]{3,2,1,0:T(8,128)}, f32[16,2,8,128]{3,2,1,0:T(8,128)}) custom-call(bf16[8,128,512]{2,1,0:T(8,128)(2,1)} %bitcast.288, f32[128,512]{1,0:T(8,128)} %copy-done.5, f32[16,512]{1,0:T(8,128)} %copy-done.27, ...), custom_call_target="tpu_custom_call" | custom-call | tf_op jit(solution)/shard_map/pallas_call | solution.py:77
  285.9 49.6 %shard_map.481 = (bf16[4,1664,1024]{2,1,0:T(8,128)(2,1)}, bf16[8,128,512]{2,1,0:T(8,128)(2,1)}, f32[128,512]{1,0:T(8,128)}, f32[8,512]{1,0:T(8,128)}) custom-call(bf16[16,1664,256]{2,1,0:T(8,128)(2,1)} %get-tuple-element.134.probs_in, f32[16,2,8,128]{3,2,1,0:T(8,128)} %get-tuple-element.135.stats, f32[16,2,8,128]{3,2,1,0:T(8,128)} %get-tuple-element.136.joined, ...), custom_call_target="tpu_custom_call" | custom-call | tf_op jit(solution)/shard_map/pallas_call | solution.py:77
  335.5 1.7 convolution_convert_fusion.15
  350.1 21.9 %shard_map.482 = (bf16[8,128,512]{2,1,0:T(8,128)(2,1)S(1)}, f32[128,512]{1,0:T(8,128)S(1)}, f32[768,512]{1,0:T(8,128)S(1)}, f32[8,512]{1,0:T(8,128)S(1)}, f32[1664,512]{1,0:T(8,128)}) custom-call(bf16[8,128,512]{2,1,0:T(8,128)(2,1)S(1)} %bitcast.279, f32[128,512]{1,0:T(8,128)S(1)} %copy-done.6, f32[128,512]{1,0:T(8,128)S(1)} %copy-done.7, ...), custom_call_target="tpu_custom_call" | custom-call | tf_op jit(solution)/shard_map/pallas_call | solution.py:77
  385.1 25.7 %shard_map.483 = (bf16[8,128,512]{2,1,0:T(8,128)(2,1)S(1)}, f32[128,512]{1,0:T(8,128)S(1)}, f32[768,512]{1,0:T(8,128)S(1)}, f32[8,512]{1,0:T(8,128)S(1)}, f32[1664,512]{1,0:T(8,128)}) custom-call(bf16[8,128,512]{2,1,0:T(8,128)(2,1)S(1)} %bitcast.278, f32[128,512]{1,0:T(8,128)S(1)} %get-tuple-element.129.x, f32[128,512]{1,0:T(8,128)S(1)} %get-tuple-element.143.grad, ...), custom_call_target="tpu_custom_call" | custom-call | tf_op jit(solution)/shard_map/pallas_call | solution.py:77
  423.7 26.7 %shard_map.484 = (bf16[8,128,512]{2,1,0:T(8,128)(2,1)S(1)}, f32[128,512]{1,0:T(8,128)S(1)}, f32[768,512]{1,0:T(8,128)S(1)}, f32[8,512]{1,0:T(8,128)S(1)}, f32[1664,512]{1,0:T(8,128)}, /*index=5*/f32[8,512]{1,0:T(8,128)S(1)}) custom-call(bf16[8,128,512]{2,1,0:T(8,128)(2,1)S(1)} %bitcast.277, f32[128,512]{1,0:T(8,128)S(1)} %copy-done.13, ...), custom_call_target="tpu_custom_call" | custom-call | tf_op jit(solution)/shard_map/pallas_call | solution.py:77
  458.3 2.8 fusion.146
  464.0 2.5 convert_reduce_fusion
  467.1 2.9 fusion.283
  475.3 50.9 %shard_map.485 = (f32[1664,512]{1,0:T(8,128)}, f32[448,512]{1,0:T(8,128)}, f32[8,512]{1,0:T(8,128)}) custom-call(bf16[8,128,512]{2,1,0:T(8,128)(2,1)} %bitcast.294, f32[128,512]{1,0:T(8,128)} %copy-done.14, f32[128,512]{1,0:T(8,128)} %copy-done.15, s32[16,1,256]{2,1,0:T(1,128)} %copy-done.26, bf16[448,512]{1,0:T(8,128)(2,1)} %pad_maximum_fusion.4.refs_0_, ...), custom_call_target="tpu_custom_call" | custom-call | tf_op jit(solution)/shard_map/pallas_call | solution.py:77
  526.2 40.1 %shard_map.486 = (f32[1664,512]{1,0:T(8,128)}, f32[768,512]{1,0:T(8,128)}, f32[4,8,512]{2,1,0:T(8,128)}, f32[2,8,2304]{2,1,0:T(8,128)}, f32[2,8,2304]{2,1,0:T(8,...) custom-call(f32[1664,512]{1,0:T(8,128)} %get-tuple-element.151.g_embed_in, ...), custom_call_target="tpu_custom_call" | custom-call | tf_op jit(solution)/shard_map/pallas_call | solution.py:77
  567.5 16.6 %shard_map.487 = (f32[448,512]{1,0:T(8,128)}, f32[448,512]{1,0:T(8,128)}, f32[448,512]{1,0:T(8,128)}, f32[320,512]{1,0:T(8,128)}, f32[320,512]{1,0:T(8,128)}, /*...) custom-call(f32[1664,512]{1,0:T(8,128)} %get-tuple-element.164.m_emb, ...), custom_call_target="tpu_custom_call" | custom-call | tf_op jit(solution)/shard_map/pallas_call | solution.py:1273
  (598 shorter events, 100.5 us)
Async XLA Ops:
  7.2 195.9 %copy-start = (s32[4]{0:T(128)S(1)}, s32[4]{0:T(128)}, u32[]{:S(2)}) copy-start(s32[4]{0:T(128)} %param.32) | copy-start | bytes 52
  7.2 211.5 %all-gather.3.cloned.1.call-start = ((), (), s32[]{:S(2)}) async-start(), calls=%async_computation | async-start | bytes 2129920 | tf_op jit(solution)/shard_map/all_gather | solution.py:1473
  11.6 37.8 %copy-start.16 = (f32[16,512]{1,0:T(8,128)}, f32[16,512]{1,0:T(8,128)S(1)}, u32[]{:S(2)}) copy-start(f32[16,512]{1,0:T(8,128)S(1)} %select_maximum_fusion.refs_1_) | copy-start | bytes 98308
  12.1 39.4 %copy-start.138 = (s32[4,1025]{1,0:T(4,128)S(1)}, s32[4,1025]{1,0:T(4,128)}, u32[]{:S(2)}) copy-start(s32[4,1025]{1,0:T(4,128)} %param.30) | copy-start | bytes 49204
  50.9 49.8 %copy-start.149 = (f32[1,512]{1,0:T(1,128)}, f32[1,512]{1,0:T(1,128)S(1)}, u32[]{:S(2)}) copy-start(f32[1,512]{1,0:T(1,128)S(1)} %get-tuple-element.389) | copy-start | bytes 6148
  52.2 48.5 %copy-start.26 = (s32[16,1,256]{2,1,0:T(1,128)}, s32[16,1,256]{2,1,0:T(1,128)S(1)}, u32[]{:S(2)}) copy-start(s32[16,1,256]{2,1,0:T(1,128)S(1)} %and_select_fusion.1.ids) | copy-start | bytes 49156
  52.3 48.5 %copy-start.19 = (bf16[768,512]{1,0:T(8,128)(2,1)S(1)}, bf16[768,512]{1,0:T(8,128)(2,1)}, u32[]{:S(2)}) copy-start(bf16[768,512]{1,0:T(8,128)(2,1)} %copy-done.18) | copy-start | bytes 2359300
  52.3 48.5 %copy-start.164 = (f32[1,192]{1,0:T(1,128)S(1)}, f32[1,192]{1,0:T(1,128)}, u32[]{:S(2)}) copy-start(f32[1,192]{1,0:T(1,128)} %slice.564) | copy-start | bytes 2308
  109.4 20.9 %copy-start.88 = (bf16[1024,256]{1,0:T(8,128)(2,1)}, bf16[1024,256]{1,0:T(8,128)(2,1)S(1)}, u32[]{:S(2)}) copy-start(bf16[1024,256]{1,0:T(8,128)(2,1)S(1)} %get-tuple-element.327) | copy-start | bytes 1572868
  176.4 21.8 %copy-start.92 = (bf16[1024,256]{1,0:T(8,128)(2,1)}, bf16[1024,256]{1,0:T(8,128)(2,1)S(1)}, u32[]{:S(2)}) copy-start(bf16[1024,256]{1,0:T(8,128)(2,1)S(1)} %get-tuple-element.323) | copy-start | bytes 1572868
  200.4 137.5 %copy-start.85 = (bf16[1024,48]{0,1:T(8,128)(2,1)}, bf16[1024,48]{0,1:T(8,128)(2,1)S(1)}, u32[]{:S(2)}) copy-start(bf16[1024,48]{0,1:T(8,128)(2,1)S(1)} %get-tuple-element.367) | copy-start | bytes 294916
  201.8 171.1 %copy-start.141 = (f32[512]{0:T(512)}, f32[512]{0:T(512)S(1)}, u32[]{:S(2)}) copy-start(f32[512]{0:T(512)S(1)} %log_add_fusion.5) | copy-start | bytes 6148
  202.9 134.7 %copy-start.142 = (f32[512]{0:T(512)}, f32[512]{0:T(512)S(1)}, u32[]{:S(2)}) copy-start(f32[512]{0:T(512)S(1)} %log_add_fusion.4) | copy-start | bytes 6148
  285.9 51.3 %copy-start.58 = (f32[512,512]{0,1:T(8,128)S(1)}, f32[512,512]{0,1:T(8,128)}, u32[]{:S(2)}) copy-start(f32[512,512]{0,1:T(8,128)} %copy-done.57) | copy-start | bytes 3145732
  285.9 51.3 %copy-start.70 = (bf16[1024,192]{0,1:T(8,128)(2,1)S(1)}, bf16[1024,192]{0,1:T(8,128)(2,1)}, u32[]{:S(2)}) copy-start(bf16[1024,192]{0,1:T(8,128)(2,1)} %copy-done.69) | copy-start | bytes 1179652
  350.0 22.0 %copy-start.23 = (bf16[768,512]{1,0:T(8,128)(2,1)S(1)}, bf16[768,512]{1,0:T(8,128)(2,1)}, u32[]{:S(2)}) copy-start(bf16[768,512]{1,0:T(8,128)(2,1)} %copy-done.22) | copy-start | bytes 2359300
  350.0 22.4 %copy-start.54 = (f32[512,512]{0,1:T(8,128)S(1)}, f32[512,512]{0,1:T(8,128)}, u32[]{:S(2)}) copy-start(f32[512,512]{0,1:T(8,128)} %copy-done.53) | copy-start | bytes 3145732
  350.1 22.4 %copy-start.68 = (bf16[1024,192]{0,1:T(8,128)(2,1)S(1)}, bf16[1024,192]{0,1:T(8,128)(2,1)}, u32[]{:S(2)}) copy-start(bf16[1024,192]{0,1:T(8,128)(2,1)} %copy-done.67) | copy-start | bytes 1179652
  385.1 25.8 %copy-start.21 = (bf16[768,512]{1,0:T(8,128)(2,1)S(1)}, bf16[768,512]{1,0:T(8,128)(2,1)}, u32[]{:S(2)}) copy-start(bf16[768,512]{1,0:T(8,128)(2,1)} %copy-done.20) | copy-start | bytes 2359300
  385.1 26.2 %copy-start.50 = (f32[512,512]{0,1:T(8,128)S(1)}, f32[512,512]{0,1:T(8,128)}, u32[]{:S(2)}) copy-start(f32[512,512]{0,1:T(8,128)} %copy-done.49) | copy-start | bytes 3145732
  385.1 26.2 %copy-start.66 = (bf16[1024,192]{0,1:T(8,128)(2,1)S(1)}, bf16[1024,192]{0,1:T(8,128)(2,1)}, u32[]{:S(2)}) copy-start(bf16[1024,192]{0,1:T(8,128)(2,1)} %copy-done.65) | copy-start | bytes 1179652
  423.7 28.2 %copy-start.46 = (f32[512,512]{0,1:T(8,128)S(1)}, f32[512,512]{0,1:T(8,128)}, u32[]{:S(2)}) copy-start(f32[512,512]{0,1:T(8,128)} %copy-done.45) | copy-start | bytes 3145732
  423.7 28.2 %copy-start.64 = (bf16[1024,192]{0,1:T(8,128)(2,1)S(1)}, bf16[1024,192]{0,1:T(8,128)(2,1)}, u32[]{:S(2)}) copy-start(bf16[1024,192]{0,1:T(8,128)(2,1)} %copy-done.63) | copy-start | bytes 1179652
  567.5 20.6 %copy-start.1 = (s32[4]{0:T(128)S(1)}, s32[4]{0:T(128)}, u32[]{:S(2)}) copy-start(s32[4]{0:T(128)} %param.32) | copy-start | bytes 52
  (162 other events, 423.7 us)
Sparse Core Ops, SparseCore 0:
  11.1 40.2 all-gather.2

commit v5 on v4

--- a/solution.py
+++ b/solution.py
@@ -837,7 +837,7 @@
         def row(ref):
             return jnp.concatenate([ref[c, 0, 0:1, :], ref[c, 1, 0:1, :]], 1)
 
-        coef, wanted = coefs[c], targets[c]
+        coef, wanted = coefs[lax.div(c, 4)], targets[c]
         scale = jnp.exp(row(stats) - row(joined)) * coef
         lanes = pl.ds(pl.multiple_of(lax.rem(c, 4) * (2 * BLOCK), 2 * BLOCK), 2 * BLOCK)
 
@@ -1026,8 +1026,8 @@
 def compress_body(
     vocab, g_embed_in, m_head_in, left_head, err, err_in, err_back, q_in, q_back, q_embed,
     ret0, ret1, ret2, ret3, bias0, bias1, bias2, bias3, out_rows, vectors,
-    m_embed, m_layer, basis, own, sums, bias_sum, vector_sum,
-    g_embed, m_head, errors, came, landed, out_sum, load_sems, give_send, give_recv,
+    m_embed_out, m_layer_out, basis, own, sums, bias_sum, vector_sum,
+    m_embed, m_layer, g_embed, m_head, errors, came, landed, out_sum, load_sems, give_send, give_recv,
     bias, left, left_came, bias_came, joint, joint_came, work, vec_came, vec_mine, vec_sums, vec_all,
     *sems,
 ):
@@ -1057,9 +1057,13 @@
     load_head = pltpu.make_async_copy(m_head_in, m_head, load_sems.at[3])
     load_embed.start()
     load_err.start()
+    m_embed_write = pltpu.make_async_copy(m_embed, m_embed_out, load_sems.at[4])
+    m_layer_write = pltpu.make_async_copy(m_layer, m_layer_out, load_sems.at[5])
     load_own(lambda copy: copy.start())
     load_head.start()
     greet([device for _, device in peers] + [device for _, device in replicas_peers()])
+    give = (0, (out_rows,), (landed,))
+    give_start(*give, (give_send, give_recv))
     pairs = [(sems[2 * n], sems[2 * n + 1]) for n in range(len(sems) // 2)]
     vec_first = [
         send(vectors.at[p], vec_came.at[me], pairs[0], k, device)
@@ -1070,8 +1074,6 @@
     cols, rows = err_in.shape[0], err_back.shape[0]
     half, places = factor_places(cols, rows, vocab)
     of_in, of_back = pl.ds(0, cols), pl.ds(cols, rows)
-    give = (0, (out_rows,), (landed,))
-    give_start(*give, (give_send, give_recv))
     for index, bias_part in enumerate((bias0, bias1, bias2, bias3)):
 
         @pl.when(own_layer == index)
@@ -1100,23 +1102,20 @@
     blocks = (m_layer.at[of_in], m_layer.at[of_back], m_embed, m_head)
     left[3] = left_head[...]
 
+    second = replicas_exchange(left, left_came, *pairs[1])
+    second += replicas_exchange(bias, bias_came, *pairs[2])
+    left_came[x] = left[...]
+    bias_came[x] = bias[...]
+    m_embed_write.start()
+    m_layer_write.start()
     for copy in vec_first:
         copy.wait_recv()
     vec_mine[...] = jnp.sum(vec_came[...], 0)
-    second = []
-    for n, (src, dst) in enumerate(
-        ((left, left_came), (bias, bias_came), (vec_mine, vec_sums))
-    ):
-        second += replicas_exchange(src, dst, *pairs[1 + n])
-    left_came[x] = left[...]
-    bias_came[x] = bias[...]
+    vec_second = replicas_exchange(vec_mine, vec_sums, *pairs[3])
     vec_sums[x] = vec_mine[...]
     for copy in second:
         copy.wait()
     bias_sum[...] = jnp.sum(bias_came[...], 0)
-    vec_all[me] = jnp.sum(vec_sums[...], 0)
-    mine = vec_all.at[me]
-    third = [send(mine, mine, pairs[4], k, device) for k, (_, device) in enumerate(peers)]
     work[...] = jnp.sum(left_came[...], 0)
     order = lax.broadcasted_iota(jnp.int32, (1, RANK, 1), 1)
     for index in range(RANK):
@@ -1135,6 +1134,11 @@
     joint[...] = own[...].reshape(joint.shape).astype(BF)
     fourth = replicas_exchange(joint, joint_came, *pairs[5])
     joint_came[x] = joint[...]
+    for copy in vec_second:
+        copy.wait()
+    vec_all[me] = jnp.sum(vec_sums[...], 0)
+    mine = vec_all.at[me]
+    third = [send(mine, mine, pairs[4], k, device) for k, (_, device) in enumerate(peers)]
     for copy in fourth:
         copy.wait()
     total = jnp.sum(joint_came[...].astype(F32), 0)
@@ -1144,6 +1148,8 @@
     for copy in third:
         copy.wait()
     vector_sum[...] = vec_all[...]
+    m_embed_write.wait()
+    m_layer_write.wait()
 
 
 def compressed(vocab, g_embed, m_head, left_head, err, errs, facs, returned, out_rows, vectors):
@@ -1166,12 +1172,14 @@
         (g_embed, m_head, left_head, err, *errs, *facs, *layers, *biases, out_rows, vectors),
         [
             pltpu.VMEM(tall, F32),
+            pltpu.VMEM(rows, F32),
+            pltpu.VMEM(tall, F32),
             pltpu.VMEM(tall, F32),
             pltpu.VMEM(tall, F32),
             pltpu.VMEM(rows, F32),
             pltpu.VMEM((4, *out_rows.shape), BF),
             pltpu.VMEM(out_rows.shape, F32),
-            pltpu.SemaphoreType.DMA((4,)),
+            pltpu.SemaphoreType.DMA((6,)),
             pltpu.SemaphoreType.DMA((1,)),
             pltpu.SemaphoreType.DMA((4,)),
             pltpu.VMEM(bias.shape, F32),
@@ -1190,6 +1198,7 @@
         30,
         56,
         in_specs=[some, some, VMEM_SPEC, some] + [VMEM_SPEC] * 5 + [some] * 4 + [VMEM_SPEC] * 6,
+        out_specs=[some, some] + [VMEM_SPEC] * 5,
     )
 
 
@@ -1498,7 +1507,7 @@
     losses = joined[:, :, 1, :].reshape(seq_rep, LENGTH)
     loss_part = jnp.sum(own_weight * jnp.mean(losses, 1))
     coefs = jnp.broadcast_to(
-        jnp.repeat(own_weight / (weight_total * LENGTH), 4)[:, None, None], (16, 1, 2 * BLOCK)
+        (own_weight / (weight_total * LENGTH))[:, None, None], (seq_rep, 1, 2 * BLOCK)
     )
     steep, grad_all, grad, grad_gains = loss_back(
         probs, stats, joined, own_targets, coefs, head_t, x, final_norm

time: 604 us -> 600 us (level)
  transfers between devices with their start and end apart: 1 -> 1, of which waited for: 0 -> 0; matrix products, arithmetic and copies ran while one was open for 8% -> 8% of each run, Pallas kernels for 25% -> 26%
where the time goes in v5:
time: 600 us; the launch traced here: 592 us
  Pallas kernels  441 us (74%)
  matrix products  74.7 us (12%)
  local copies, waits for them, and re-layouts  31.1 us (5%)
  other arithmetic  26 us (4%)
  between operations  19.5 us (3%)
    pallas_call x12, Pallas kernels, kernel_call(): pl.pallas_call(body, out_shape=out_shape, in_specs=in_specs or [VMEM_SPEC...  424 us
    dot_general x32, matrix products, dot_cols(): lax.dot_general(left, right, (((1,), (1,)), ((), ())), preferred_element_...  33.8 us
    dot_general x32, matrix products, dot_plain(): return jnp.dot(left, right, preferred_element_type=F32)  25.6 us
    unnamed x379, local copies, waits for them, and re-layouts  18.5 us
    pallas_call x1, Pallas kernels, updated(): pl.pallas_call(functools.partial(update_body, vocab, rates), grid=(-(-voc...  16.5 us
    dot_general x32, matrix products, dot_rows(): lax.dot_general(left, right, (((0,), (0,)), ((), ())), preferred_element_...  15.3 us
  transfers between devices with their start and end apart: 1, of which 0 were waited for; matrix products, arithmetic and copies ran while one was open for 8% of the time, Pallas kernels for 26%

profile of v5, /device:TPU:0, one launch (start us, length us, event | category | flops | bytes accessed | tf_op | source)
XLA Modules:
  0.0 591.9 jit_solution(17533145634481583)
XLA Ops:
  7.3 1.7 convert_element_type.311
  12.1 37.4 %shard_map.475 = (bf16[4,128,1664]{2,1,0:T(8,128)(2,1)S(1)}, bf16[768,512]{1,0:T(8,128)(2,1)S(1)}, f32[16,512]{1,0:T(8,128)S(1)}, f32[2,1664,512]{2,1,0:T(8,128)}) custom-call(bf16[128,1664]{1,0:T(8,128)(2,1)S(1)} %get-tuple-element.350.block, f32[12576,128]{1,0:T(8,128)} %bitcast.282, bf16[768,512]{1,0:T(8,128)(2,1)S(1)} %pad_maximum_fusion.refs_0_, ...), custom_call_target="tpu_custom_call" | custom-call | tf_op jit(solution)/shard_map/pallas_call | solution.py:77
  52.3 47.1 %shard_map.476 = (f32[128,512]{1,0:T(8,128)S(1)}, bf16[8,128,512]{2,1,0:T(8,128)(2,1)S(1)}) custom-call(bf16[512,1664]{1,0:T(8,128)(2,1)S(1)} %bitcast.276, s32[16,1,256]{2,1,0:T(1,128)S(1)} %and_select_fusion.1.ids), custom_call_target="tpu_custom_call" | custom-call | tf_op jit(solution)/shard_map/pallas_call | solution.py:77
  105.7 3.7 multiply_convert_fusion.11
  110.1 20.1 %shard_map.477 = (bf16[8,128,512]{2,1,0:T(8,128)(2,1)S(1)}, f32[128,512]{1,0:T(8,128)S(1)}, bf16[768,512]{1,0:T(8,128)(2,1)S(1)}, f32[16,512]{1,0:T(8,128)S(1)}) custom-call(bf16[8,128,512]{2,1,0:T(8,128)(2,1)S(1)} %bitcast.274, f32[128,512]{1,0:T(8,128)S(1)} %get-tuple-element.121.x, f32[16,512]{1,0:T(8,128)S(1)} %copy-done.29, ...), custom_call_target="tpu_custom_call" | custom-call | tf_op jit(solution)/shard_map/pallas_call | solution.py:77
  136.6 3.7 multiply_convert_fusion.10
  141.1 25.5 %shard_map.478 = (bf16[8,128,512]{2,1,0:T(8,128)(2,1)S(1)}, f32[128,512]{1,0:T(8,128)S(1)}, bf16[768,512]{1,0:T(8,128)(2,1)S(1)}, f32[16,512]{1,0:T(8,128)S(1)}) custom-call(bf16[8,128,512]{2,1,0:T(8,128)(2,1)S(1)} %bitcast.275, f32[128,512]{1,0:T(8,128)S(1)} %get-tuple-element.125.x, f32[16,512]{1,0:T(8,128)S(1)} %get-tuple-element.123.rest, ...), custom_call_target="tpu_custom_call" | custom-call | tf_op jit(solution)/shard_map/pallas_call | solution.py:77
  172.7 3.6 multiply_convert_fusion.9
  176.8 21.4 %shard_map.479 = (bf16[8,128,512]{2,1,0:T(8,128)(2,1)S(1)}, f32[128,512]{1,0:T(8,128)S(1)}, bf16[768,512]{1,0:T(8,128)(2,1)S(1)}, f32[16,512]{1,0:T(8,128)S(1)}) custom-call(bf16[8,128,512]{2,1,0:T(8,128)(2,1)S(1)} %bitcast.273, f32[128,512]{1,0:T(8,128)S(1)} %get-tuple-element.129.x, f32[16,512]{1,0:T(8,128)S(1)} %get-tuple-element.127.rest, ...), custom_call_target="tpu_custom_call" | custom-call | tf_op jit(solution)/shard_map/pallas_call | solution.py:77
  209.8 1.8 convolution_convert_fusion.20
  212.9 3.6 multiply_convert_fusion.8
  218.7 3.6 copy.78.head
  222.4 60.7 %shard_map.480 = (f32[128,512]{1,0:T(8,128)}, bf16[16,256,512]{2,1,0:T(8,128)(2,1)}, bf16[16,1664,256]{2,1,0:T(8,128)(2,1)}, f32[16,2,8,128]{3,2,1,0:T(8,128)}, f32[16,2,8,128]{3,2,1,0:T(8,128)}) custom-call(bf16[8,128,512]{2,1,0:T(8,128)(2,1)} %bitcast.288, f32[128,512]{1,0:T(8,128)} %copy-done.5, f32[16,512]{1,0:T(8,128)} %copy-done.27, ...), custom_call_target="tpu_custom_call" | custom-call | tf_op jit(solution)/shard_map/pallas_call | solution.py:77
  285.7 49.6 %shard_map.481 = (bf16[4,1664,1024]{2,1,0:T(8,128)(2,1)}, bf16[8,128,512]{2,1,0:T(8,128)(2,1)}, f32[128,512]{1,0:T(8,128)}, f32[8,512]{1,0:T(8,128)}) custom-call(bf16[16,1664,256]{2,1,0:T(8,128)(2,1)} %get-tuple-element.134.probs_in, f32[16,2,8,128]{3,2,1,0:T(8,128)} %get-tuple-element.135.stats, f32[16,2,8,128]{3,2,1,0:T(8,128)} %get-tuple-element.136.joined, ...), custom_call_target="tpu_custom_call" | custom-call | tf_op jit(solution)/shard_map/pallas_call | solution.py:77
  335.4 1.7 convolution_convert_fusion.15
  349.9 21.9 %shard_map.482 = (bf16[8,128,512]{2,1,0:T(8,128)(2,1)S(1)}, f32[128,512]{1,0:T(8,128)S(1)}, f32[768,512]{1,0:T(8,128)S(1)}, f32[8,512]{1,0:T(8,128)S(1)}, f32[1664,512]{1,0:T(8,128)}) custom-call(bf16[8,128,512]{2,1,0:T(8,128)(2,1)S(1)} %bitcast.279, f32[128,512]{1,0:T(8,128)S(1)} %copy-done.6, f32[128,512]{1,0:T(8,128)S(1)} %copy-done.7, ...), custom_call_target="tpu_custom_call" | custom-call | tf_op jit(solution)/shard_map/pallas_call | solution.py:77
  385.0 25.7 %shard_map.483 = (bf16[8,128,512]{2,1,0:T(8,128)(2,1)S(1)}, f32[128,512]{1,0:T(8,128)S(1)}, f32[768,512]{1,0:T(8,128)S(1)}, f32[8,512]{1,0:T(8,128)S(1)}, f32[1664,512]{1,0:T(8,128)}) custom-call(bf16[8,128,512]{2,1,0:T(8,128)(2,1)S(1)} %bitcast.278, f32[128,512]{1,0:T(8,128)S(1)} %get-tuple-element.129.x, f32[128,512]{1,0:T(8,128)S(1)} %get-tuple-element.143.grad, ...), custom_call_target="tpu_custom_call" | custom-call | tf_op jit(solution)/shard_map/pallas_call | solution.py:77
  423.5 26.7 %shard_map.484 = (bf16[8,128,512]{2,1,0:T(8,128)(2,1)S(1)}, f32[128,512]{1,0:T(8,128)S(1)}, f32[768,512]{1,0:T(8,128)S(1)}, f32[8,512]{1,0:T(8,128)S(1)}, f32[1664,512]{1,0:T(8,128)}, /*index=5*/f32[8,512]{1,0:T(8,128)S(1)}) custom-call(bf16[8,128,512]{2,1,0:T(8,128)(2,1)S(1)} %bitcast.277, f32[128,512]{1,0:T(8,128)S(1)} %copy-done.13, ...), custom_call_target="tpu_custom_call" | custom-call | tf_op jit(solution)/shard_map/pallas_call | solution.py:77
  458.1 2.8 fusion.146
  463.8 2.5 convert_reduce_fusion
  466.9 2.9 fusion.283
  475.1 50.6 %shard_map.485 = (f32[1664,512]{1,0:T(8,128)}, f32[448,512]{1,0:T(8,128)}, f32[8,512]{1,0:T(8,128)}) custom-call(bf16[8,128,512]{2,1,0:T(8,128)(2,1)} %bitcast.294, f32[128,512]{1,0:T(8,128)} %copy-done.14, f32[128,512]{1,0:T(8,128)} %copy-done.15, s32[16,1,256]{2,1,0:T(1,128)} %copy-done.26, bf16[448,512]{1,0:T(8,128)(2,1)} %pad_maximum_fusion.4.refs_0_, ...), custom_call_target="tpu_custom_call" | custom-call | tf_op jit(solution)/shard_map/pallas_call | solution.py:77
  525.7 37.2 %shard_map.486 = (f32[1664,512]{1,0:T(8,128)}, f32[768,512]{1,0:T(8,128)}, f32[4,8,512]{2,1,0:T(8,128)}, f32[2,8,2304]{2,1,0:T(8,128)}, f32[2,8,2304]{2,1,0:T(8,...) custom-call(f32[1664,512]{1,0:T(8,128)} %get-tuple-element.151.g_embed_in, ...), custom_call_target="tpu_custom_call" | custom-call | tf_op jit(solution)/shard_map/pallas_call | solution.py:77
  564.1 16.5 %shard_map.487 = (f32[448,512]{1,0:T(8,128)}, f32[448,512]{1,0:T(8,128)}, f32[448,512]{1,0:T(8,128)}, f32[320,512]{1,0:T(8,128)}, f32[320,512]{1,0:T(8,128)}, /*...) custom-call(f32[1664,512]{1,0:T(8,128)} %get-tuple-element.164.m_emb, ...), custom_call_target="tpu_custom_call" | custom-call | tf_op jit(solution)/shard_map/pallas_call | solution.py:1282
  (596 shorter events, 100.3 us)
Async XLA Ops:
  7.2 195.9 %copy-start = (s32[4]{0:T(128)S(1)}, s32[4]{0:T(128)}, u32[]{:S(2)}) copy-start(s32[4]{0:T(128)} %param.32) | copy-start | bytes 52
  7.2 211.5 %all-gather.3.cloned.1.call-start = ((), (), s32[]{:S(2)}) async-start(), calls=%async_computation | async-start | bytes 2129920 | tf_op jit(solution)/shard_map/all_gather | solution.py:1482
  11.6 37.8 %copy-start.16 = (f32[16,512]{1,0:T(8,128)}, f32[16,512]{1,0:T(8,128)S(1)}, u32[]{:S(2)}) copy-start(f32[16,512]{1,0:T(8,128)S(1)} %select_maximum_fusion.refs_1_) | copy-start | bytes 98308
  12.1 39.4 %copy-start.138 = (s32[4,1025]{1,0:T(4,128)S(1)}, s32[4,1025]{1,0:T(4,128)}, u32[]{:S(2)}) copy-start(s32[4,1025]{1,0:T(4,128)} %param.30) | copy-start | bytes 49204
  50.9 49.8 %copy-start.149 = (f32[1,512]{1,0:T(1,128)}, f32[1,512]{1,0:T(1,128)S(1)}, u32[]{:S(2)}) copy-start(f32[1,512]{1,0:T(1,128)S(1)} %get-tuple-element.389) | copy-start | bytes 6148
  52.2 48.5 %copy-start.26 = (s32[16,1,256]{2,1,0:T(1,128)}, s32[16,1,256]{2,1,0:T(1,128)S(1)}, u32[]{:S(2)}) copy-start(s32[16,1,256]{2,1,0:T(1,128)S(1)} %and_select_fusion.1.ids) | copy-start | bytes 49156
  52.3 48.5 %copy-start.19 = (bf16[768,512]{1,0:T(8,128)(2,1)S(1)}, bf16[768,512]{1,0:T(8,128)(2,1)}, u32[]{:S(2)}) copy-start(bf16[768,512]{1,0:T(8,128)(2,1)} %copy-done.18) | copy-start | bytes 2359300
  52.3 48.5 %copy-start.164 = (f32[1,192]{1,0:T(1,128)S(1)}, f32[1,192]{1,0:T(1,128)}, u32[]{:S(2)}) copy-start(f32[1,192]{1,0:T(1,128)} %slice.564) | copy-start | bytes 2308
  109.4 20.9 %copy-start.88 = (bf16[1024,256]{1,0:T(8,128)(2,1)}, bf16[1024,256]{1,0:T(8,128)(2,1)S(1)}, u32[]{:S(2)}) copy-start(bf16[1024,256]{1,0:T(8,128)(2,1)S(1)} %get-tuple-element.327) | copy-start | bytes 1572868
  176.4 21.8 %copy-start.92 = (bf16[1024,256]{1,0:T(8,128)(2,1)}, bf16[1024,256]{1,0:T(8,128)(2,1)S(1)}, u32[]{:S(2)}) copy-start(bf16[1024,256]{1,0:T(8,128)(2,1)S(1)} %get-tuple-element.323) | copy-start | bytes 1572868
  200.4 137.3 %copy-start.85 = (bf16[1024,48]{0,1:T(8,128)(2,1)}, bf16[1024,48]{0,1:T(8,128)(2,1)S(1)}, u32[]{:S(2)}) copy-start(bf16[1024,48]{0,1:T(8,128)(2,1)S(1)} %get-tuple-element.367) | copy-start | bytes 294916
  201.8 170.9 %copy-start.141 = (f32[512]{0:T(512)}, f32[512]{0:T(512)S(1)}, u32[]{:S(2)}) copy-start(f32[512]{0:T(512)S(1)} %log_add_fusion.5) | copy-start | bytes 6148
  202.9 134.5 %copy-start.142 = (f32[512]{0:T(512)}, f32[512]{0:T(512)S(1)}, u32[]{:S(2)}) copy-start(f32[512]{0:T(512)S(1)} %log_add_fusion.4) | copy-start | bytes 6148
  285.7 51.3 %copy-start.58 = (f32[512,512]{0,1:T(8,128)S(1)}, f32[512,512]{0,1:T(8,128)}, u32[]{:S(2)}) copy-start(f32[512,512]{0,1:T(8,128)} %copy-done.57) | copy-start | bytes 3145732
  285.7 51.3 %copy-start.70 = (bf16[1024,192]{0,1:T(8,128)(2,1)S(1)}, bf16[1024,192]{0,1:T(8,128)(2,1)}, u32[]{:S(2)}) copy-start(bf16[1024,192]{0,1:T(8,128)(2,1)} %copy-done.69) | copy-start | bytes 1179652
  349.9 22.0 %copy-start.23 = (bf16[768,512]{1,0:T(8,128)(2,1)S(1)}, bf16[768,512]{1,0:T(8,128)(2,1)}, u32[]{:S(2)}) copy-start(bf16[768,512]{1,0:T(8,128)(2,1)} %copy-done.22) | copy-start | bytes 2359300
  349.9 22.4 %copy-start.54 = (f32[512,512]{0,1:T(8,128)S(1)}, f32[512,512]{0,1:T(8,128)}, u32[]{:S(2)}) copy-start(f32[512,512]{0,1:T(8,128)} %copy-done.53) | copy-start | bytes 3145732
  349.9 22.4 %copy-start.68 = (bf16[1024,192]{0,1:T(8,128)(2,1)S(1)}, bf16[1024,192]{0,1:T(8,128)(2,1)}, u32[]{:S(2)}) copy-start(bf16[1024,192]{0,1:T(8,128)(2,1)} %copy-done.67) | copy-start | bytes 1179652
  384.9 25.8 %copy-start.21 = (bf16[768,512]{1,0:T(8,128)(2,1)S(1)}, bf16[768,512]{1,0:T(8,128)(2,1)}, u32[]{:S(2)}) copy-start(bf16[768,512]{1,0:T(8,128)(2,1)} %copy-done.20) | copy-start | bytes 2359300
  384.9 26.2 %copy-start.50 = (f32[512,512]{0,1:T(8,128)S(1)}, f32[512,512]{0,1:T(8,128)}, u32[]{:S(2)}) copy-start(f32[512,512]{0,1:T(8,128)} %copy-done.49) | copy-start | bytes 3145732
  384.9 26.2 %copy-start.66 = (bf16[1024,192]{0,1:T(8,128)(2,1)S(1)}, bf16[1024,192]{0,1:T(8,128)(2,1)}, u32[]{:S(2)}) copy-start(bf16[1024,192]{0,1:T(8,128)(2,1)} %copy-done.65) | copy-start | bytes 1179652
  423.5 28.2 %copy-start.46 = (f32[512,512]{0,1:T(8,128)S(1)}, f32[512,512]{0,1:T(8,128)}, u32[]{:S(2)}) copy-start(f32[512,512]{0,1:T(8,128)} %copy-done.45) | copy-start | bytes 3145732
  423.5 28.1 %copy-start.64 = (bf16[1024,192]{0,1:T(8,128)(2,1)S(1)}, bf16[1024,192]{0,1:T(8,128)(2,1)}, u32[]{:S(2)}) copy-start(bf16[1024,192]{0,1:T(8,128)(2,1)} %copy-done.63) | copy-start | bytes 1179652
  564.1 20.5 %copy-start.1 = (s32[4]{0:T(128)S(1)}, s32[4]{0:T(128)}, u32[]{:S(2)}) copy-start(s32[4]{0:T(128)} %param.32) | copy-start | bytes 52
  (162 other events, 423.8 us)
Sparse Core Ops, SparseCore 0:
  11.1 40.2 all-gather.2
